TPU v7x, 128 devices: a whole 4x4x4 slice. The times are simulated.
128 devices in a mesh: seq: 32 (over y, x_lo, z), ch: 4 (over x_hi, core).
Axes of the slice: x: 4 (x_hi: 2, x_lo: 2; x = x_hi * 2 + x_lo), y: 4, z: 4, core: 2. Of those that a mesh axis runs over, the one named last changes fastest.
Arguments:
- coupled_first: bfloat16 [64, 524288], P('ch', 'seq'), may hold values from -6 to 6
- coupled_second: bfloat16 [64, 524288], P('ch', 'seq'), may hold values from -3 to 3
- spectra: bfloat16 [2, 2, 64, 524288], P(None, None, 'ch', 'seq'), may hold values from -4.1875 to 4.1875
- short_taps: float32 [2, 3, 64], P(None, None, 'ch'), may hold values from -1.6 to 1.6
- mixing: bfloat16 [64, 64], P('ch'), may hold values from -0.75 to 0.75
Outputs:
- input_second: float32 [64, 524288], P('ch', 'seq')
All inputs are finite; a program needn't handle non-finite values.
Results may differ from a plain program's by a relative error of at most 0.035.
Values may be sent and summed in bfloat16 or wider, within the bound.
No kernel may reach another device: no remote copies, remote signals or barrier semaphores. Data moves between devices by JAX's collectives and lax.ppermute only.
A program may use at most 128 MiB of HBM per device.

v0:
```python
import jax
import jax.numpy as jnp
from jax import lax
from jax.sharding import PartitionSpec as P

S = 1024


def from_behind(value, axis, steps):
    count = lax.axis_size(axis)
    pairs = [(source, (source + steps) % count) for source in range(count)]
    return lax.ppermute(value, axis, pairs)


def angle_table(row_count, row_start, col_count, col_start, modulus):
    left = (jnp.arange(row_count, dtype=jnp.int32) + row_start)[:, None]
    right = (jnp.arange(col_count, dtype=jnp.int32) + col_start)[None, :]
    angle = (left * right % modulus).astype(jnp.float32) * (2.0 * jnp.pi / modulus)
    return (jnp.cos(angle), jnp.sin(angle))


def dft_table(count):
    cosine_table, sine_table = angle_table(count, 0, count, 0, count)
    return (cosine_table.astype(jnp.bfloat16), sine_table.astype(jnp.bfloat16))


def along_last(values, table):
    return jnp.einsum("...n,nk->...k", values, table, preferred_element_type=jnp.float32)


def along_middle(values, table):
    return jnp.einsum("cnj,nk->ckj", values, table, preferred_element_type=jnp.float32)


def section_first(matrix, col_start, modulus):
    row_count = matrix.shape[1]
    cosine_table, sine_table = dft_table(row_count)
    real_part = along_middle(matrix, cosine_table)
    imag_part = -along_middle(matrix, sine_table)
    twist_cos, twist_sin = angle_table(row_count, 0, matrix.shape[2], col_start, modulus)
    out_real = real_part * twist_cos + imag_part * twist_sin
    out_imag = imag_part * twist_cos - real_part * twist_sin
    return jnp.stack([out_real, out_imag]).astype(jnp.bfloat16)


def section_second(paired):
    col_count = paired.shape[-1]
    cosine_table, sine_table = dft_table(col_count)
    out_real = along_last(paired[0], cosine_table) + along_last(paired[1], sine_table)
    out_imag = along_last(paired[1], cosine_table) - along_last(paired[0], sine_table)
    return jnp.stack([out_real, out_imag]).astype(jnp.bfloat16)


def section_third(paired, row_start, modulus):
    col_count = paired.shape[-1]
    cosine_table, sine_table = dft_table(col_count)
    scale = 1.0 / col_count
    real_part = (along_last(paired[0], cosine_table) - along_last(paired[1], sine_table)) * scale
    imag_part = (along_last(paired[1], cosine_table) + along_last(paired[0], sine_table)) * scale
    twist_cos, twist_sin = angle_table(paired.shape[2], row_start, col_count, 0, modulus)
    out_real = real_part * twist_cos - imag_part * twist_sin
    out_imag = imag_part * twist_cos + real_part * twist_sin
    return jnp.stack([out_real, out_imag]).astype(jnp.bfloat16)


def section_last(paired):
    row_count = paired.shape[2]
    cosine_table, sine_table = dft_table(row_count)
    result = along_middle(paired[0], cosine_table) - along_middle(paired[1], sine_table)
    return (result * (1.0 / row_count)).astype(jnp.bfloat16)


def complex_product(filters, spectrum):
    filter_real = filters[0].astype(jnp.float32)
    filter_imag = filters[1].astype(jnp.float32)
    spec_real = spectrum[0].astype(jnp.float32)
    spec_imag = spectrum[1].astype(jnp.float32)
    out_real = filter_real * spec_real - filter_imag * spec_imag
    out_imag = filter_real * spec_imag + filter_imag * spec_real
    return jnp.stack([out_real, out_imag]).astype(jnp.bfloat16)


def conv_sequence(signal, filters):
    channels, positions = signal.shape
    seq_count = lax.axis_size("seq")
    seq_place = lax.axis_index("seq")
    rows_local = positions // S
    whole_length = positions * seq_count
    spread = lax.all_to_all(
        signal.reshape(channels, rows_local, S), "seq", split_axis=2, concat_axis=1, tiled=True
    )
    first = section_first(spread, seq_place * (S // seq_count), whole_length)
    turned = lax.all_to_all(first, "seq", split_axis=2, concat_axis=3, tiled=True)
    spectrum = section_second(turned)
    natural = lax.all_to_all(spectrum, "seq", split_axis=3, concat_axis=2, tiled=True)
    product = lax.all_to_all(
        complex_product(filters, natural), "seq", split_axis=2, concat_axis=3, tiled=True
    )
    back = section_third(product, seq_place * rows_local, whole_length)
    gathered = lax.all_to_all(back, "seq", split_axis=3, concat_axis=2, tiled=True)
    result = section_last(gathered)
    return lax.all_to_all(result, "seq", split_axis=1, concat_axis=2, tiled=True).reshape(
        channels, positions
    )


def gate_pair(signal, tap_table, before):
    count = signal.shape[1]
    wide = jnp.concatenate([before, signal], axis=1).astype(jnp.float32)
    present = wide[:, 2:]
    first_lag = wide[:, 1 : count + 1]
    second_lag = wide[:, :count]
    gate_one = (
        tap_table[0, 0][:, None] * present
        + tap_table[0, 1][:, None] * first_lag
        + tap_table[0, 2][:, None] * second_lag
    )
    gate_two = (
        tap_table[1, 0][:, None] * present
        + tap_table[1, 1][:, None] * first_lag
        + tap_table[1, 2][:, None] * second_lag
    )
    return (gate_one, gate_two)


def operator_sequence(signal, filters, tap_table):
    positions = signal.shape[1]
    before = from_behind(signal[:, positions - 2 :], "seq", 1)
    gate_one, gate_two = gate_pair(signal, tap_table, before)
    middle = (gate_one * conv_sequence(signal, filters[0]).astype(jnp.float32)).astype(jnp.bfloat16)
    return (gate_two * conv_sequence(middle, filters[1]).astype(jnp.float32)).astype(jnp.bfloat16)


def project(values, weights):
    return lax.psum_scatter(
        lax.dot_general(
            weights, values, (((0,), (0,)), ((), ())), preferred_element_type=jnp.float32
        ).astype(jnp.bfloat16),
        "ch",
        scatter_dimension=0,
        tiled=True,
    ).astype(jnp.float32)


def on_device(coupled_first, coupled_second, spectra, short_taps, mixing):
    seq_count = lax.axis_size("seq")
    channels, positions = coupled_first.shape
    whole_length = positions * seq_count
    row_count = whole_length // S
    folded = spectra.reshape(2, 2, channels, positions // row_count, row_count).transpose(
        0, 1, 2, 4, 3
    )
    update = project(operator_sequence(coupled_first, folded, short_taps), mixing)
    return coupled_second.astype(jnp.float32) - update


def solution(mesh):
    return jax.shard_map(
        on_device,
        mesh=mesh,
        in_specs=(
            P("ch", "seq"),
            P("ch", "seq"),
            P(None, None, "ch", "seq"),
            P(None, None, "ch"),
            P("ch", None),
        ),
        out_specs=P("ch", "seq"),
        check_vma=False,
    )
```

profile of v0, /device:TPU:1, one launch (start us, length us, event | category | flops | bytes accessed | tf_op | source)
XLA Modules:
  0.0 984.0 jit_solution(16818133150200555021)
XLA Ops:
  12.6 7.1 reshape.376
  19.7 10.3 %all-to-all-start = ((bf16[32,2,4096]{2,1,0:T(2,128)(2,1)}), bf16[32,2,4096]{2,1,0:T(2,128)(2,1)S(1)}, u32[]{:S(2)}, u32[]{:S(2)}) async-start(bf16[32,2,4096]{2,1,0:T(2,128)(2,1)} %reshape.376), calls=%async_computation | async-start | bytes 1048576 | tf_op jit(solution)/shard_map/all_to_all | solution.py:89
  30.4 9.5 all-to-all-done
  72.6 18.9 %all_to_all.174 = bf16[32,2,8192]{2,1,0:T(2,128)(2,1)S(1)} all-to-all(bf16[32,2,8192]{2,1,0:T(2,128)(2,1)S(1)} %reshape.378), channel_id=1, replica_groups=mesh['seq'=32,'ch'=4] {'seq'}, dimensions={0} | all-to-all | bytes 2097152 | tf_op jit(solution)/shard_map/all_to_all | solution.py:93
  103.8 17.0 %fusion.23 = f32[16,16,1024]{2,1,0:T(8,128)} fusion(bf16[16,16,1024]{2,1,0:T(8,128)(2,1)S(1)} %squeeze.25), kind=kOutput, calls=%fused_computation.28 | convolution fusion | flops 552599552 | bytes 1572864 | tf_op jit(solution)/shard_map/...n,nk->...k/dot_general | solution.py:28
  123.6 16.5 %fusion.21 = f32[16,16,1024]{2,1,0:T(8,128)S(1)} fusion(bf16[16,16,1024]{2,1,0:T(8,128)(2,1)S(1)} %squeeze.24), kind=kOutput, calls=%fused_computation.27 | convolution fusion | flops 552599552 | bytes 1572864 | tf_op jit(solution)/shard_map/...n,nk->...k/dot_general | solution.py:28
  140.1 16.1 %fusion.77 = bf16[1,16,16,1024]{3,2,1,0:T(8,128)(2,1)S(1)} fusion(f32[16,16,1024]{2,1,0:T(8,128)S(1)} %copy-done.22, bf16[16,16,1024]{2,1,0:T(8,128)(2,1)S(1)} %squeeze.24), kind=kOutput, calls=%fused_computation.60 | convolution fusion | flops 553123840 | bytes 2097152 | tf_op jit(solution)/shard_map/...n,nk->...k/dot_general | solution.py:28
  156.3 16.4 %fusion.80 = bf16[1,16,16,1024]{3,2,1,0:T(8,128)(2,1)S(1)} fusion(f32[16,16,1024]{2,1,0:T(8,128)S(1)} %fusion.21, bf16[16,16,1024]{2,1,0:T(8,128)(2,1)S(1)} %squeeze.25), kind=kOutput, calls=%fused_computation.61 | convolution fusion | flops 553123840 | bytes 2097152 | tf_op jit(solution)/shard_map/...n,nk->...k/dot_general | solution.py:28
  172.8 12.0 %copy.140 = bf16[2,16,16,1024]{2,1,0,3:T(8,128)(2,1)} copy(bf16[2,16,16,1024]{3,2,1,0:T(8,128)(2,1)S(1)} %pad_maximum_fusion.1) | data formatting | bytes 2097152 | tf_op jit(solution)/shard_map/stack | solution.py:51
  184.8 11.2 %reshape.380 = bf16[32,2,8192]{2,1,0:T(2,128)(2,1)} reshape(bf16[1024,2,16,16]{3,2,1,0:T(8,128)(2,1)} %bitcast.298) | data formatting | bytes 2097152
  203.9 12.0 %all-to-all-done.2 = bf16[32,2,8192]{2,1,0:T(2,128)(2,1)S(1)} async-done(((bf16[32,2,8192]{2,1,0:T(2,128)(2,1)}), bf16[32,2,8192]{2,1,0:T(2,128)(2,1)S(1)}, u32[]{:S(2)}, u32[]{:S(2)}) %all-to-all-start.2) | async-done | bytes 1048608 | tf_op jit(solution)/shard_map/all_to_all | solution.py:95
  215.9 7.5 reshape.381
  223.5 9.8 %copy.141 = bf16[2,16,16,32,32]{4,2,3,1,0:T(8,128)(2,1)} copy(bf16[2,16,16,32,32]{2,1,0,4,3:T(8,128)(2,1)} %bitcast.299) | data formatting | bytes 2097152 | tf_op jit(solution)/shard_map/all_to_all | solution.py:95
  255.5 7.4 reshape.382
  268.5 14.0 %all-to-all-done.3 = bf16[32,2,8192]{2,1,0:T(2,128)(2,1)S(1)} async-done(((bf16[32,2,8192]{2,1,0:T(2,128)(2,1)}), bf16[32,2,8192]{2,1,0:T(2,128)(2,1)S(1)}, u32[]{:S(2)}, u32[]{:S(2)}) %all-to-all-start.3) | async-done | bytes 1048608 | tf_op jit(solution)/shard_map/all_to_all | solution.py:96
  294.8 17.0 %fusion.19 = f32[16,16,1024]{2,1,0:T(8,128)} fusion(bf16[16,16,1024]{2,1,0:T(8,128)(2,1)S(1)} %squeeze.27), kind=kOutput, calls=%fused_computation.26 | convolution fusion | flops 552599552 | bytes 1572864 | tf_op jit(solution)/shard_map/...n,nk->...k/dot_general | solution.py:28
  314.7 16.5 %fusion.17 = f32[16,16,1024]{2,1,0:T(8,128)S(1)} fusion(bf16[16,16,1024]{2,1,0:T(8,128)(2,1)S(1)} %squeeze.26), kind=kOutput, calls=%fused_computation.25 | convolution fusion | flops 552599552 | bytes 1572864 | tf_op jit(solution)/shard_map/...n,nk->...k/dot_general | solution.py:28
  331.2 16.2 %fusion.47 = f32[16,16,1024]{2,1,0:T(8,128)S(1)} fusion(f32[16,16,1024]{2,1,0:T(8,128)S(1)} %copy-done.20, bf16[16,16,1024]{2,1,0:T(8,128)(2,1)S(1)} %squeeze.26), kind=kOutput, calls=%fused_computation.42 | convolution fusion | flops 552861696 | bytes 2621440 | tf_op jit(solution)/shard_map/...n,nk->...k/dot_general | solution.py:28
  347.5 16.5 %fusion.105 = (bf16[1,16,16,1024]{3,2,1,0:T(8,128)(2,1)S(1)}, bf16[1,16,16,1024]{3,2,1,0:T(8,128)(2,1)S(1)}) fusion(f32[16,16,1024]{2,1,0:T(8,128)S(1)} %fusion.47, f32[16,1024]{1,0:T(8,128)S(1)} %get-tuple-element.40, f32[16,1024]{1,0:T(8,128)S(1)} %get-tuple-element.39, f32[16,16,1024]{2,1,0:T(8,128)S(1)} %fusion.17, bf16[16,16,1024]{2,1,0:T(8,128)(2,1)S(1)} %squeeze.27), kind=kOutput, calls=%fused_computation.104 | convolution fusion | flops 554958848 | bytes 3801088 | tf_op jit(solution)/shard_map/...n,nk->...k/dot_general | solution.py:28
  364.0 12.0 %copy.150 = bf16[2,16,16,1024]{2,1,0,3:T(8,128)(2,1)} copy(bf16[2,16,16,1024]{3,2,1,0:T(8,128)(2,1)S(1)} %pad_maximum_fusion.3) | data formatting | bytes 2097152 | tf_op jit(solution)/shard_map/stack | solution.py:63
  376.1 11.3 %reshape.384 = bf16[32,2,8192]{2,1,0:T(2,128)(2,1)} reshape(bf16[1024,2,16,16]{3,2,1,0:T(8,128)(2,1)} %bitcast.300) | data formatting | bytes 2097152
  394.2 12.6 %all-to-all-done.4 = bf16[32,2,8192]{2,1,0:T(2,128)(2,1)S(1)} async-done(((bf16[32,2,8192]{2,1,0:T(2,128)(2,1)}), bf16[32,2,8192]{2,1,0:T(2,128)(2,1)S(1)}, u32[]{:S(2)}, u32[]{:S(2)}) %all-to-all-start.4) | async-done | bytes 1048608 | tf_op jit(solution)/shard_map/all_to_all | solution.py:100
  406.8 8.0 reshape.385
  414.8 9.8 %copy.151 = bf16[2,16,16,32,32]{4,2,3,1,0:T(8,128)(2,1)} copy(bf16[2,16,16,32,32]{2,1,0,4,3:T(8,128)(2,1)} %bitcast.301) | data formatting | bytes 2097152 | tf_op jit(solution)/shard_map/all_to_all | solution.py:100
  452.6 8.8 all-to-all-done.5
  484.3 13.0 %all_to_all.175 = bf16[32,2,4096]{2,1,0:T(2,128)(2,1)S(1)} all-to-all(bf16[32,2,4096]{2,1,0:T(2,128)(2,1)S(1)} %reshape.388), channel_id=1, replica_groups=mesh['seq'=32,'ch'=4] {'seq'}, dimensions={0} | all-to-all | bytes 1048576 | tf_op jit(solution)/shard_map/all_to_all | solution.py:89
  531.4 15.1 %all_to_all.176 = bf16[32,2,8192]{2,1,0:T(2,128)(2,1)S(1)} all-to-all(bf16[32,2,8192]{2,1,0:T(2,128)(2,1)S(1)} %reshape.390), channel_id=1, replica_groups=mesh['seq'=32,'ch'=4] {'seq'}, dimensions={0} | all-to-all | bytes 2097152 | tf_op jit(solution)/shard_map/all_to_all | solution.py:93
  559.4 18.2 %fusion.15 = f32[16,16,1024]{2,1,0:T(8,128)} fusion(bf16[16,16,1024]{2,1,0:T(8,128)(2,1)} %squeeze.61), kind=kOutput, calls=%fused_computation.24 | convolution fusion | flops 552599552 | bytes 1572864 | tf_op jit(solution)/shard_map/...n,nk->...k/dot_general | solution.py:28
  581.4 17.1 %fusion.13 = f32[16,16,1024]{2,1,0:T(8,128)S(1)} fusion(bf16[16,16,1024]{2,1,0:T(8,128)(2,1)} %squeeze.60), kind=kOutput, calls=%fused_computation.23 | convolution fusion | flops 552599552 | bytes 1572864 | tf_op jit(solution)/shard_map/...n,nk->...k/dot_general | solution.py:28
  598.5 16.1 %fusion.83 = bf16[1,16,16,1024]{3,2,1,0:T(8,128)(2,1)S(1)} fusion(f32[16,16,1024]{2,1,0:T(8,128)S(1)} %copy-done.23, bf16[16,16,1024]{2,1,0:T(8,128)(2,1)S(1)} %copy-done.12), kind=kOutput, calls=%fused_computation.62 | convolution fusion | flops 553123840 | bytes 2097152 | tf_op jit(solution)/shard_map/...n,nk->...k/dot_general | solution.py:28
  614.6 16.4 %fusion.86 = bf16[1,16,16,1024]{3,2,1,0:T(8,128)(2,1)S(1)} fusion(f32[16,16,1024]{2,1,0:T(8,128)S(1)} %fusion.13, bf16[16,16,1024]{2,1,0:T(8,128)(2,1)S(1)} %copy-done.11), kind=kOutput, calls=%fused_computation.63 | convolution fusion | flops 553123840 | bytes 2097152 | tf_op jit(solution)/shard_map/...n,nk->...k/dot_general | solution.py:28
  631.1 12.0 %copy.166 = bf16[2,16,16,1024]{2,1,0,3:T(8,128)(2,1)} copy(bf16[2,16,16,1024]{3,2,1,0:T(8,128)(2,1)S(1)} %pad_maximum_fusion.5) | data formatting | bytes 2097152 | tf_op jit(solution)/shard_map/stack | solution.py:51
  643.2 10.4 %reshape.392 = bf16[32,2,8192]{2,1,0:T(2,128)(2,1)S(1)} reshape(bf16[1024,2,16,16]{3,2,1,0:T(8,128)(2,1)} %bitcast.302) | data formatting | bytes 2097152
  653.5 16.2 %all_to_all.177 = bf16[32,2,8192]{2,1,0:T(2,128)(2,1)S(1)} all-to-all(bf16[32,2,8192]{2,1,0:T(2,128)(2,1)S(1)} %reshape.392), channel_id=1, replica_groups=mesh['seq'=32,'ch'=4] {'seq'}, dimensions={0} | all-to-all | bytes 2097152 | tf_op jit(solution)/shard_map/all_to_all | solution.py:95
  669.7 7.5 reshape.393
  677.3 9.8 %copy.167 = bf16[2,16,16,32,32]{4,2,3,1,0:T(8,128)(2,1)} copy(bf16[2,16,16,32,32]{2,1,0,4,3:T(8,128)(2,1)} %bitcast.303) | data formatting | bytes 2097152 | tf_op jit(solution)/shard_map/all_to_all | solution.py:95
  717.7 15.6 %all_to_all.178 = bf16[32,2,8192]{2,1,0:T(2,128)(2,1)S(1)} all-to-all(bf16[32,2,8192]{2,1,0:T(2,128)(2,1)S(1)} %reshape.394), channel_id=1, replica_groups=mesh['seq'=32,'ch'=4] {'seq'}, dimensions={0} | all-to-all | bytes 2097152 | tf_op jit(solution)/shard_map/all_to_all | solution.py:96
  746.3 18.2 %fusion.11 = f32[16,16,1024]{2,1,0:T(8,128)} fusion(bf16[16,16,1024]{2,1,0:T(8,128)(2,1)} %squeeze.63), kind=kOutput, calls=%fused_computation.22 | convolution fusion | flops 552599552 | bytes 1572864 | tf_op jit(solution)/shard_map/...n,nk->...k/dot_general | solution.py:28
  768.4 17.0 %fusion.9 = f32[16,16,1024]{2,1,0:T(8,128)S(1)} fusion(bf16[16,16,1024]{2,1,0:T(8,128)(2,1)} %squeeze.62), kind=kOutput, calls=%fused_computation.21 | convolution fusion | flops 552599552 | bytes 1572864 | tf_op jit(solution)/shard_map/...n,nk->...k/dot_general | solution.py:28
  785.5 16.2 %fusion.59 = f32[16,16,1024]{2,1,0:T(8,128)S(1)} fusion(f32[16,16,1024]{2,1,0:T(8,128)S(1)} %copy-done.21, bf16[16,16,1024]{2,1,0:T(8,128)(2,1)S(1)} %copy-done.13), kind=kOutput, calls=%fused_computation.46 | convolution fusion | flops 552861696 | bytes 2621440 | tf_op jit(solution)/shard_map/...n,nk->...k/dot_general | solution.py:28
  801.8 16.2 %fusion.110 = (bf16[1,16,16,1024]{3,2,1,0:T(8,128)(2,1)S(1)}, bf16[1,16,16,1024]{3,2,1,0:T(8,128)(2,1)S(1)}) fusion(f32[16,16,1024]{2,1,0:T(8,128)S(1)} %fusion.59, f32[16,1024]{1,0:T(8,128)S(1)} %get-tuple-element.40, f32[16,1024]{1,0:T(8,128)S(1)} %get-tuple-element.39, f32[16,16,1024]{2,1,0:T(8,128)S(1)} %fusion.9, bf16[16,16,1024]{2,1,0:T(8,128)(2,1)S(1)} %copy-done.10), kind=kOutput, calls=%fused_computation.109 | convolution fusion | flops 554958848 | bytes 3801088 | tf_op jit(solution)/shard_map/...n,nk->...k/dot_general | solution.py:28
  818.1 12.0 %copy.176 = bf16[2,16,16,1024]{2,1,0,3:T(8,128)(2,1)} copy(bf16[2,16,16,1024]{3,2,1,0:T(8,128)(2,1)S(1)} %pad_maximum_fusion.7) | data formatting | bytes 2097152 | tf_op jit(solution)/shard_map/stack | solution.py:63
  830.1 10.4 %reshape.396 = bf16[32,2,8192]{2,1,0:T(2,128)(2,1)S(1)} reshape(bf16[1024,2,16,16]{3,2,1,0:T(8,128)(2,1)} %bitcast.304) | data formatting | bytes 2097152
  840.5 15.7 %all_to_all.179 = bf16[32,2,8192]{2,1,0:T(2,128)(2,1)S(1)} all-to-all(bf16[32,2,8192]{2,1,0:T(2,128)(2,1)S(1)} %reshape.396), channel_id=1, replica_groups=mesh['seq'=32,'ch'=4] {'seq'}, dimensions={0} | all-to-all | bytes 2097152 | tf_op jit(solution)/shard_map/all_to_all | solution.py:100
  856.2 7.5 reshape.397
  863.7 9.8 %copy.177 = bf16[2,16,16,32,32]{4,2,3,1,0:T(8,128)(2,1)} copy(bf16[2,16,16,32,32]{2,1,0,4,3:T(8,128)(2,1)} %bitcast.305) | data formatting | bytes 2097152 | tf_op jit(solution)/shard_map/all_to_all | solution.py:100
  900.2 13.8 %all_to_all.180 = bf16[32,2,4096]{2,1,0:T(2,128)(2,1)} all-to-all(bf16[32,2,4096]{2,1,0:T(2,128)(2,1)} %reshape.398), channel_id=1, replica_groups=mesh['seq'=32,'ch'=4] {'seq'}, dimensions={0} | all-to-all | bytes 1048576 | tf_op jit(solution)/shard_map/all_to_all | solution.py:102
  927.0 47.6 %reduce-scatter.2.cloned.1.call-done = bf16[16,16384]{1,0:T(8,128)(2,1)} async-done(((bf16[64,16384]{1,0:T(8,128)(2,1)}), bf16[16,16384]{1,0:T(8,128)(2,1)}) %reduce-scatter.2.cloned.1.call-update) | async-done | bytes 524304 | tf_op jit(solution)/shard_map/reduce_scatter | solution.py:135
  (164 shorter events, 302.9 us)
Async XLA Ops:
  6.5 918.3 %copy-start = (bf16[16,64]{1,0:T(8,128)(2,1)S(1)}, bf16[16,64]{1,0:T(8,128)(2,1)}, u32[]{:S(2)}) copy-start(bf16[16,64]{1,0:T(8,128)(2,1)} %param.9) | copy-start | bytes 6148
  19.7 20.2 %all-to-all-start = ((bf16[32,2,4096]{2,1,0:T(2,128)(2,1)}), bf16[32,2,4096]{2,1,0:T(2,128)(2,1)S(1)}, u32[]{:S(2)}, u32[]{:S(2)}) async-start(bf16[32,2,4096]{2,1,0:T(2,128)(2,1)} %reshape.376), calls=%async_computation | async-start | bytes 1048576 | tf_op jit(solution)/shard_map/all_to_all | solution.py:89
  103.8 17.0 %copy-start.3 = (bf16[1,16,16,32,32]{4,2,3,1,0:T(8,128)(2,1)S(1)}, bf16[1,16,16,32,32]{4,2,3,1,0:T(8,128)(2,1)}, u32[]{:S(2)}) copy-start(bf16[1,16,16,32,32]{4,2,3,1,0:T(8,128)(2,1)} %get-tuple-element.24) | copy-start | bytes 1572868
  123.6 16.5 %copy-start.22 = (f32[16,16,1024]{2,1,0:T(8,128)S(1)}, f32[16,16,1024]{2,1,0:T(8,128)}, u32[]{:S(2)}) copy-start(f32[16,16,1024]{2,1,0:T(8,128)} %fusion.23) | copy-start | bytes 3145732
  196.0 19.9 %all-to-all-start.2 = ((bf16[32,2,8192]{2,1,0:T(2,128)(2,1)}), bf16[32,2,8192]{2,1,0:T(2,128)(2,1)S(1)}, u32[]{:S(2)}, u32[]{:S(2)}) async-start(bf16[32,2,8192]{2,1,0:T(2,128)(2,1)} %reshape.380), calls=%async_computation.2 | async-start | bytes 2097152 | tf_op jit(solution)/shard_map/all_to_all | solution.py:95
  203.9 43.3 %copy-start.1 = (bf16[8,8,32,512]{3,2,1,0:T(8,128)(2,1)}, bf16[8,8,32,512]{3,2,1,0:T(8,128)(2,1)S(1)}, u32[]{:S(2)}) copy-start(bf16[8,8,32,512]{3,2,1,0:T(8,128)(2,1)S(1)} %copy.187) | copy-start | bytes 6291460
  262.9 19.6 %all-to-all-start.3 = ((bf16[32,2,8192]{2,1,0:T(2,128)(2,1)}), bf16[32,2,8192]{2,1,0:T(2,128)(2,1)S(1)}, u32[]{:S(2)}, u32[]{:S(2)}) async-start(bf16[32,2,8192]{2,1,0:T(2,128)(2,1)} %reshape.382), calls=%async_computation.3 | async-start | bytes 2097152 | tf_op jit(solution)/shard_map/all_to_all | solution.py:96
  294.8 17.0 %copy-start.4 = (bf16[1,16,16,32,32]{4,2,3,1,0:T(8,128)(2,1)S(1)}, bf16[1,16,16,32,32]{4,2,3,1,0:T(8,128)(2,1)}, u32[]{:S(2)}) copy-start(bf16[1,16,16,32,32]{4,2,3,1,0:T(8,128)(2,1)} %get-tuple-element.17) | copy-start | bytes 1572868
  314.7 16.5 %copy-start.20 = (f32[16,16,1024]{2,1,0:T(8,128)S(1)}, f32[16,16,1024]{2,1,0:T(8,128)}, u32[]{:S(2)}) copy-start(f32[16,16,1024]{2,1,0:T(8,128)} %fusion.19) | copy-start | bytes 3145732
  376.1 16.3 %copy-start.7 = (bf16[16,16384]{1,0:T(8,128)(2,1)S(1)}, bf16[16,16384]{1,0:T(8,128)(2,1)}, u32[]{:S(2)}) copy-start(bf16[16,16384]{1,0:T(8,128)(2,1)} %param.5) | copy-start | bytes 1572868
  376.1 17.6 %copy-start.16 = (f32[2,3,16]{2,0,1:T(2,128)S(1)}, f32[2,3,16]{2,0,1:T(2,128)}, u32[]{:S(2)}) copy-start(f32[2,3,16]{2,0,1:T(2,128)} %param.8) | copy-start | bytes 1156
  387.3 19.5 %all-to-all-start.4 = ((bf16[32,2,8192]{2,1,0:T(2,128)(2,1)}), bf16[32,2,8192]{2,1,0:T(2,128)(2,1)S(1)}, u32[]{:S(2)}, u32[]{:S(2)}) async-start(bf16[32,2,8192]{2,1,0:T(2,128)(2,1)} %reshape.384), calls=%async_computation.4 | async-start | bytes 2097152 | tf_op jit(solution)/shard_map/all_to_all | solution.py:100
  392.5 59.9 %collective-permute-start = (bf16[16,2]{1,0:T(8,128)(2,1)S(1)}, bf16[16,2]{1,0:T(8,128)(2,1)S(1)}, u32[]{:S(2)}, u32[]{:S(2)}) collective-permute-start(bf16[16,2]{1,0:T(8,128)(2,1)S(1)} %slice.125), channel_id=1, source_target_pairs={{0,4},{4,8},{8,12},{12,16},{16,20},{20,24},{24,28},{28,32},{32,36}... | collective-permute-start | bytes 200 | tf_op jit(solution)/shard_map/ppermute | solution.py:12
  437.5 4.9 copy-start.8
  447.4 14.0 %all-to-all-start.5 = ((bf16[32,2,4096]{2,1,0:T(2,128)(2,1)}), bf16[32,2,4096]{2,1,0:T(2,128)(2,1)}, u32[]{:S(2)}, u32[]{:S(2)}) async-start(bf16[32,2,4096]{2,1,0:T(2,128)(2,1)} %reshape.386), calls=%async_computation.5 | async-start | bytes 1048576 | tf_op jit(solution)/shard_map/all_to_all | solution.py:102
  452.3 522.3 %reduce-scatter.2.cloned.1.call-start = ((), (), s32[]{:S(2)}) async-start(), calls=%async_computation.13 | async-start | bytes 2621440 | tf_op jit(solution)/shard_map/reduce_scatter | solution.py:135
  507.6 5.3 copy-start.14
  559.4 18.2 %copy-start.5 = (bf16[1,16,16,32,32]{4,2,3,1,0:T(8,128)(2,1)S(1)}, bf16[1,16,16,32,32]{4,2,3,1,0:T(8,128)(2,1)}, u32[]{:S(2)}) copy-start(bf16[1,16,16,32,32]{4,2,3,1,0:T(8,128)(2,1)} %get-tuple-element.14) | copy-start | bytes 1572868
  581.3 17.1 %copy-start.12 = (bf16[16,16,1024]{2,1,0:T(8,128)(2,1)S(1)}, bf16[16,16,1024]{2,1,0:T(8,128)(2,1)}, u32[]{:S(2)}) copy-start(bf16[16,16,1024]{2,1,0:T(8,128)(2,1)} %squeeze.60) | copy-start | bytes 1572868
  581.3 17.1 %copy-start.23 = (f32[16,16,1024]{2,1,0:T(8,128)S(1)}, f32[16,16,1024]{2,1,0:T(8,128)}, u32[]{:S(2)}) copy-start(f32[16,16,1024]{2,1,0:T(8,128)} %fusion.15) | copy-start | bytes 3145732
  598.5 16.2 %copy-start.11 = (bf16[16,16,1024]{2,1,0:T(8,128)(2,1)S(1)}, bf16[16,16,1024]{2,1,0:T(8,128)(2,1)}, u32[]{:S(2)}) copy-start(bf16[16,16,1024]{2,1,0:T(8,128)(2,1)} %squeeze.61) | copy-start | bytes 1572868
  698.7 3.8 copy-start.2
  746.3 18.2 %copy-start.6 = (bf16[1,16,16,32,32]{4,2,3,1,0:T(8,128)(2,1)S(1)}, bf16[1,16,16,32,32]{4,2,3,1,0:T(8,128)(2,1)}, u32[]{:S(2)}) copy-start(bf16[1,16,16,32,32]{4,2,3,1,0:T(8,128)(2,1)} %get-tuple-element.7) | copy-start | bytes 1572868
  768.4 17.1 %copy-start.13 = (bf16[16,16,1024]{2,1,0:T(8,128)(2,1)S(1)}, bf16[16,16,1024]{2,1,0:T(8,128)(2,1)}, u32[]{:S(2)}) copy-start(bf16[16,16,1024]{2,1,0:T(8,128)(2,1)} %squeeze.62) | copy-start | bytes 1572868
  768.4 17.1 %copy-start.21 = (f32[16,16,1024]{2,1,0:T(8,128)S(1)}, f32[16,16,1024]{2,1,0:T(8,128)}, u32[]{:S(2)}) copy-start(f32[16,16,1024]{2,1,0:T(8,128)} %fusion.11) | copy-start | bytes 3145732
  785.5 16.3 %copy-start.10 = (bf16[16,16,1024]{2,1,0:T(8,128)(2,1)S(1)}, bf16[16,16,1024]{2,1,0:T(8,128)(2,1)}, u32[]{:S(2)}) copy-start(bf16[16,16,1024]{2,1,0:T(8,128)(2,1)} %squeeze.63) | copy-start | bytes 1572868
  888.2 5.3 copy-start.9
  921.2 3.5 copy-start.17
  921.2 3.6 copy-start.18
  921.3 3.6 copy-start.19
  924.8 49.8 %copy-start.15 = (bf16[16,16384]{1,0:T(8,128)(2,1)S(1)}, bf16[16,16384]{1,0:T(8,128)(2,1)}, u32[]{:S(2)}) copy-start(bf16[16,16384]{1,0:T(8,128)(2,1)} %param.6) | copy-start | bytes 1572868
Sparse Core Ops, SparseCore 0:
  927.1 47.3 reduce-scatter.1
where the time goes:
time: 991 us; the launch traced here: 984 us
  local copies, waits for them, and re-layouts  392 us (40%)
  matrix products  312 us (31%)
  blocking collectives  108 us (11%)
  waiting for transfers between devices  104 us (10%)
  starting transfers between devices  32.3 us (3%)
  other arithmetic  20.7 us (2%)
  between operations  14.7 us (1%)
    dot_general x16, matrix products, along_last(): jnp.einsum('...n,nk->...k', values, table, preferred_element_type=jnp.flo...  268 us
    unnamed x75, local copies, waits for them, and re-layouts  153 us
    reduce_scatter x1, waiting for transfers between devices, project(): lax.psum_scatter(lax.dot_general(weights, values, (((0,), (0,)), ((), ())...  47.6 us
    unnamed x8, matrix products  41.9 us
    all_to_all x2, blocking collectives, conv_sequence(): lax.all_to_all(first, 'seq', split_axis=2, concat_axis=3, tiled=True)  34 us
    another operation x2, local copies, waits for them, and re-layouts, section_third(): return jnp.stack([out_real, out_imag]).astype(jnp.bfloat16)  24.1 us
    another operation x2, local copies, waits for them, and re-layouts, section_second(): return jnp.stack([out_real, out_imag]).astype(jnp.bfloat16)  24.1 us
  transfers between devices with their start and end apart: 7, of which 6 were waited for; matrix products, arithmetic and copies ran while one was open for 5% of the time, Pallas kernels for 0%

commit v1 on v0

v1 whole, which is shorter than its diff:
```python
import jax
import jax.numpy as jnp
import numpy as np
from jax import lax
from jax.experimental import pallas as pl
from jax.experimental.pallas import tpu as pltpu
from jax.sharding import PartitionSpec as P

BF = jnp.bfloat16
F32 = jnp.float32
LANES = 128
N2 = 512
N1 = 1024
HALF = N1 // 4
EXTRA = 16
ROWS = HALF + EXTRA
TILE = 16
BLOCKS = 32
ANY = pl.BlockSpec(memory_space=pl.ANY)
SMEM = pl.BlockSpec(memory_space=pltpu.SMEM)
MIB = 1 << 20


def tables():
    order = np.arange(N1).reshape(BLOCKS, 2, TILE).transpose(1, 0, 2).reshape(-1)
    freq = np.arange(HALF)[None, :] + HALF * np.arange(2)[:, None]
    angle = (freq[:, :, None] * order[None, None, :] % N1) * (2.0 * np.pi / N1)
    forward = np.concatenate([np.cos(angle), -np.sin(angle)], axis=1)
    forward[0, HALF] = 1.0 - 2.0 * (order % 2)
    backward = forward.transpose(0, 2, 1).reshape(2, 2, N1 // 2, 2 * HALF) / (N1 * N2)
    inner = np.arange(N2)
    angle = (inner[:, None] * inner[None, :] % N2) * (2.0 * np.pi / N2)
    cosine, sine = np.cos(angle), np.sin(angle)
    wide = np.block([[cosine, -sine], [sine, cosine]])
    angle = freq[:, :, None] * inner[None, None, :] * (2.0 * np.pi / (N1 * N2))
    twist = np.stack([np.cos(angle), np.sin(angle)], axis=1)
    special = np.zeros((2, 2, EXTRA, N2))
    special[0, 0, 0] = np.cos(inner * (2.0 * np.pi / N1))
    special[0, 1, 0] = np.sin(inner * (2.0 * np.pi / N1))
    twist = np.concatenate([twist, special], axis=2)
    place = np.arange(HALF)
    straight = (place[:, None] == place[None, :]).astype(np.float32)
    turned = (place[None, :] == (HALF - place[:, None]) % HALF).astype(np.float32)
    mirror = (place[:, None] == HALF - 1 - place[None, :]).astype(np.float32)
    shuffles = np.stack([straight, turned, mirror])
    bf = lambda a: np.asarray(a, dtype=np.float32).astype(jnp.bfloat16)
    return (
        bf(forward), bf(backward), bf(np.stack([wide, wide.T])),
        np.asarray(twist, dtype=np.float32), bf(shuffles),
    )


def swap(value):
    return lax.ppermute(value, "ch", [(i, i ^ 1) for i in range(lax.axis_size("ch"))])


def split_kernel(half_ref, signal_ref, filter_ref, out_ref, wide_ref):
    plane = pl.program_id(0)
    half = half_ref[0]

    @pl.when(plane == 0)
    def _():
        for row in range(TILE):
            start = pl.multiple_of(half * (TILE * N2) + row * N2, N2)
            piece = signal_ref[:, pl.ds(start, N2)].astype(F32)
            for part in range(N2 // LANES):
                wide_ref[part, row * TILE:(row + 1) * TILE, :] = piece[:, part * LANES:(part + 1) * LANES]

    @pl.when(plane > 0)
    def _():
        lane = lax.broadcasted_iota(jnp.int32, (TILE, LANES), 1)
        for row in range(TILE):
            low = pl.multiple_of(row * N1 + half * HALF, HALF)
            high = pl.multiple_of(row * N1 + (3 - half) * HALF, HALF)
            across = pl.multiple_of(row * N1 + (2 + half) * HALF, HALF)
            low_piece = filter_ref[0, 0, :, pl.ds(low, HALF)].astype(F32)
            high_piece = filter_ref[0, 0, :, pl.ds(high, HALF)].astype(F32)
            across_piece = filter_ref[0, 0, :, pl.ds(across, LANES)].astype(F32)
            rows = slice(row * TILE, (row + 1) * TILE)
            wide_ref[0, rows, :] = low_piece[:, :LANES]
            wide_ref[1, rows, :] = low_piece[:, LANES:]
            wide_ref[2, rows, :] = jnp.where(lane == 0, across_piece, high_piece[:, :LANES])
            wide_ref[3, rows, :] = high_piece[:, LANES:]

    for channel in range(TILE):
        for part in range(N2 // LANES):
            out_ref[channel, 0, :, part * LANES:(part + 1) * LANES] = wide_ref[
                part, pl.ds(channel, TILE, stride=TILE), :
            ].astype(BF)


def split_channels(half, target, count, signal, spectra):
    channels, positions = signal.shape
    return pl.pallas_call(
        split_kernel,
        grid_spec=pltpu.PrefetchScalarGridSpec(
            num_scalar_prefetch=1,
            grid=(5,),
            in_specs=[
                pl.BlockSpec((channels, positions), lambda p, s: (0, 0)),
                pl.BlockSpec(
                    (1, 1, channels, positions),
                    lambda p, s: (jnp.maximum(p - 1, 0) // 2, jnp.maximum(p - 1, 0) % 2, 0, 0),
                ),
            ],
            out_specs=pl.BlockSpec((channels, 1, TILE, N2), lambda p, s: (s[1], p, 0, 0)),
            scratch_shapes=[pltpu.VMEM((N2 // LANES, TILE * TILE, LANES), F32)],
        ),
        out_shape=jax.ShapeDtypeStruct((count, 5, TILE, N2), BF),
        compiler_params=pltpu.CompilerParams(vmem_limit_bytes=16 * MIB),
        cost_estimate=pl.CostEstimate(flops=0, bytes_accessed=8 * MIB, transcendentals=0),
    )(jnp.stack([half, target]).astype(jnp.int32), signal, spectra)


def place_kernel(core_ref, piece_ref, whole_ref, out_ref):
    del core_ref, whole_ref
    out_ref[...] = piece_ref[...]


def place(core, piece, whole):
    block = (TILE, 1, TILE, N2)
    return pl.pallas_call(
        place_kernel,
        grid_spec=pltpu.PrefetchScalarGridSpec(
            num_scalar_prefetch=1,
            grid=(5,),
            in_specs=[pl.BlockSpec(block, lambda p, s: (0, p, 0, 0)), ANY],
            out_specs=pl.BlockSpec(block, lambda p, s: (1 - s[0], p, 0, 0)),
        ),
        out_shape=jax.ShapeDtypeStruct(whole.shape, whole.dtype),
        input_output_aliases={2: 0},
        compiler_params=pltpu.CompilerParams(vmem_limit_bytes=8 * MIB),
    )(core, piece, whole)


def fetch(source, target, sems, index):
    copy = pltpu.make_async_copy(source, target, sems.at[index])
    copy.start()
    return copy


def fold_filter(core, low_high, shuffle_ref, gain_ref, part):
    dims = (((1,), (1,)), ((), ()))
    low = low_high[:, :HALF]
    high = low_high[:, HALF:]
    straight = lax.dot_general(shuffle_ref[0], low, dims, preferred_element_type=F32)
    turned = lax.dot_general(shuffle_ref[1], high, dims, preferred_element_type=F32)
    turned_bf = turned.astype(BF)
    row = lax.broadcasted_iota(jnp.int32, (HALF, 1), 0)
    keep = jnp.where((row == 0) & (core == 0), 0.0, 1.0 if part == 0 else -1.0)
    for side in range(2):
        rev = jnp.dot(
            turned_bf[:, (1 - side) * HALF:(2 - side) * HALF], shuffle_ref[2], preferred_element_type=F32
        )
        here = slice(side * HALF, (side + 1) * HALF)
        gain_ref[part, :HALF, here] = straight[:, here] + keep * rev
    gain_ref[part, HALF:, :] = turned[:EXTRA]


def spectral(core, field, forward_ref, wide_ref, twist_ref, gain_ref, raw_ref, mid_ref, sum_ref, back_ref, waits):
    waits[0]()
    raw_ref[...] = jnp.dot(forward_ref[...], field, preferred_element_type=F32)
    waits[1]()
    step = TILE
    top = (lax.broadcasted_iota(jnp.int32, (step, 1), 0) == 0) & (core == 0)
    for start in range(0, HALF, step):
        rows = slice(start, start + step)
        real, imag = raw_ref[rows], raw_ref[HALF + start:HALF + start + step]
        cosine, sine = twist_ref[0, rows], twist_ref[1, rows]
        out_imag = imag * cosine - real * sine
        if start == 0:
            out_imag = jnp.where(top, 0.0, out_imag)
            mid_ref[HALF:, :N2] = (imag * twist_ref[0, HALF:]).astype(BF)
            mid_ref[HALF:, N2:] = (-imag * twist_ref[1, HALF:]).astype(BF)
        mid_ref[rows, :N2] = (real * cosine + imag * sine).astype(BF)
        mid_ref[rows, N2:] = out_imag.astype(BF)
    waits[2]()
    sum_ref[...] = jnp.dot(mid_ref[...], wide_ref[0], preferred_element_type=F32)
    waits[3]()
    for start in range(0, ROWS, step):
        rows = slice(start, start + step)
        real, imag = sum_ref[rows, :N2], sum_ref[rows, N2:]
        gain_real, gain_imag = gain_ref[0, rows], gain_ref[1, rows]
        mid_ref[rows, :N2] = (gain_real * real - gain_imag * imag).astype(BF)
        mid_ref[rows, N2:] = (gain_real * imag + gain_imag * real).astype(BF)
    sum_ref[...] = jnp.dot(mid_ref[...], wide_ref[1], preferred_element_type=F32)
    for start in range(0, HALF, step):
        rows = slice(start, start + step)
        real, imag = sum_ref[rows, :N2], sum_ref[rows, N2:]
        cosine, sine = twist_ref[0, rows], twist_ref[1, rows]
        out_imag = imag * cosine + real * sine
        if start == 0:
            extra = sum_ref[HALF:, :N2] * twist_ref[0, HALF:] - sum_ref[HALF:, N2:] * twist_ref[1, HALF:]
            out_imag = jnp.where(top, extra, out_imag)
        back_ref[rows] = (real * cosine - imag * sine).astype(BF)
        back_ref[HALF + start:HALF + start + step] = out_imag.astype(BF)


CONV_SCRATCH = [
    pltpu.VMEM((2, BLOCKS, TILE, N2), BF),
    pltpu.VMEM((2, BLOCKS, TILE, N2), BF),
    pltpu.VMEM((2 * HALF, N1), BF),
    pltpu.VMEM((2, N1 // 2, 2 * HALF), BF),
    pltpu.VMEM((2, 2 * N2, 2 * N2), BF),
    pltpu.VMEM((2, ROWS, N2), F32),
    pltpu.VMEM((3, HALF, HALF), BF),
    pltpu.VMEM((2, ROWS, N2), F32),
    pltpu.VMEM((2 * HALF, N2), F32),
    pltpu.VMEM((ROWS, 2 * N2), BF),
    pltpu.VMEM((ROWS, 2 * N2), F32),
    pltpu.VMEM((2 * HALF, N2), BF),
]


def start_tables(core, refs, scratch, sems):
    forward_hbm, backward_hbm, wide_hbm, twist_hbm, shuffle_hbm = refs
    _, _, forward, backward, wide, twist, shuffle = scratch[:7]
    return [
        fetch(forward_hbm.at[core], forward, sems, 0),
        fetch(twist_hbm.at[core], twist, sems, 1),
        fetch(wide_hbm, wide, sems, 2),
        fetch(shuffle_hbm, shuffle, sems, 3),
        fetch(backward_hbm.at[core], backward, sems, 4),
    ]


def first_conv_kernel(core_ref, got_ref, other_ref, *rest):
    table_refs, out_ref, scratch, sems = rest[:5], rest[5], rest[6:18], rest[18]
    field, parts, forward, backward, wide, twist, shuffle, gain, raw, mid, total, back = scratch
    core = core_ref[0]
    own = fetch(got_ref.at[:, 0], field.at[core], sems, 5)
    other = fetch(other_ref, field.at[1 - core], sems, 6)
    loads = start_tables(core, table_refs, scratch, sems)
    real = fetch(got_ref.at[:, 1], parts.at[0], sems, 7)
    imag = fetch(got_ref.at[:, 2], parts.at[1], sems, 8)

    def ready():
        own.wait()
        other.wait()
        loads[0].wait()

    def filters():
        real.wait()
        imag.wait()
        loads[3].wait()
        for part in range(2):
            fold_filter(core, parts[part].reshape(N2, N2), shuffle, gain, part)

    ready()
    spectral(
        core, field[...].reshape(N1, N2), forward, wide, twist, gain, raw, mid, total, back,
        (lambda: None, loads[1].wait, loads[2].wait, filters),
    )
    loads[4].wait()
    for half in range(2):
        out_ref[half] = jnp.dot(backward[half], back[...], preferred_element_type=F32).astype(BF).reshape(
            BLOCKS, TILE, N2
        )


def first_conv(core, got, other, consts):
    return pl.pallas_call(
        first_conv_kernel,
        in_specs=[SMEM] + [ANY] * 7,
        out_specs=pl.BlockSpec(memory_space=pltpu.VMEM),
        out_shape=jax.ShapeDtypeStruct((2, BLOCKS, TILE, N2), BF),
        scratch_shapes=CONV_SCRATCH + [pltpu.SemaphoreType.DMA((9,))],
        compiler_params=pltpu.CompilerParams(vmem_limit_bytes=40 * MIB),
        cost_estimate=pl.CostEstimate(flops=int(2.5e9), bytes_accessed=8 * MIB, transcendentals=0),
    )(core, got, other, *consts)


def gate_tile(field, half, block, taps):
    here = field[half, block].astype(F32)
    before_block = jnp.where(half == 0, (block + BLOCKS - 1) % BLOCKS, block)
    before = field[1 - half, before_block, :, N2 - LANES:].astype(F32)
    row = lax.broadcasted_iota(jnp.int32, (TILE, LANES), 0)
    lane = lax.broadcasted_iota(jnp.int32, (TILE, LANES), 1)
    above = jnp.where(row == 0, pltpu.roll(before, 1, 0), pltpu.roll(here[:, N2 - LANES:], 1, 0))
    out = taps[0] * here
    for lag in (1, 2):
        moved = pltpu.roll(here, lag, 1)
        edge = jnp.where(lane < lag, pltpu.roll(above, lag, 1), moved[:, :LANES])
        out = out + taps[lag] * jnp.concatenate([edge, moved[:, LANES:]], axis=1)
    return out


def second_conv_kernel(core_ref, taps_ref, got_ref, other_ref, mine_ref, theirs_ref, *rest):
    table_refs, keep_ref, send_ref, scratch, middle, sems = rest[:5], rest[5], rest[6], rest[7:19], rest[19], rest[20]
    field, parts, forward, backward, wide, twist, shuffle, gain, raw, mid, total, back = scratch
    core = core_ref[0]
    own = fetch(got_ref.at[:, 0], field.at[core], sems, 5)
    other = fetch(other_ref, field.at[1 - core], sems, 6)
    loads = start_tables(core, table_refs, scratch, sems)
    real = fetch(got_ref.at[:, 3], parts.at[0], sems, 7)
    imag = fetch(got_ref.at[:, 4], parts.at[1], sems, 8)
    own.wait()
    other.wait()
    taps = [taps_ref[0, lag] for lag in range(3)]

    @pl.loop(0, BLOCKS)
    def _(block):
        for half in range(2):
            summed = (mine_ref[half, block].astype(F32) + theirs_ref[half, block].astype(F32)).astype(BF)
            middle[half, block] = (gate_tile(field, half, block, taps) * summed.astype(F32)).astype(BF)

    loads[0].wait()

    def filters():
        real.wait()
        imag.wait()
        loads[3].wait()
        for part in range(2):
            fold_filter(core, parts[part].reshape(N2, N2), shuffle, gain, part)

    spectral(
        core, middle[...].reshape(N1, N2), forward, wide, twist, gain, raw, mid, total, back,
        (lambda: None, loads[1].wait, loads[2].wait, filters),
    )
    loads[4].wait()
    send_ref[...] = jnp.dot(backward[1 - core], back[...], preferred_element_type=F32).astype(BF).reshape(
        BLOCKS, TILE, N2
    )
    keep_ref[...] = jnp.dot(backward[core], back[...], preferred_element_type=F32).reshape(BLOCKS, TILE, N2)


def second_conv(core, taps, got, other, mine, theirs, consts):
    vmem = pl.BlockSpec(memory_space=pltpu.VMEM)
    return pl.pallas_call(
        second_conv_kernel,
        in_specs=[SMEM, SMEM, ANY, ANY, vmem, vmem] + [ANY] * 5,
        out_specs=(vmem, vmem),
        out_shape=(
            jax.ShapeDtypeStruct((BLOCKS, TILE, N2), F32),
            jax.ShapeDtypeStruct((BLOCKS, TILE, N2), BF),
        ),
        scratch_shapes=CONV_SCRATCH
        + [pltpu.VMEM((2, BLOCKS, TILE, N2), BF), pltpu.SemaphoreType.DMA((9,))],
        compiler_params=pltpu.CompilerParams(vmem_limit_bytes=40 * MIB),
        cost_estimate=pl.CostEstimate(flops=int(2.5e9), bytes_accessed=10 * MIB, transcendentals=0),
    )(core, taps, got, other, mine, theirs, *consts)


def last_kernel(core_ref, taps_ref, got_ref, other_ref, keep_ref, theirs_ref, out_ref, field, sems):
    core = core_ref[0]
    own = fetch(got_ref.at[:, 0], field.at[core], sems, 0)
    other = fetch(other_ref, field.at[1 - core], sems, 1)
    own.wait()
    other.wait()
    taps = [taps_ref[1, lag] for lag in range(3)]

    @pl.loop(0, BLOCKS)
    def _(block):
        summed = (keep_ref[block] + theirs_ref[block].astype(F32)).astype(BF)
        last = (gate_tile(field, core, block, taps) * summed.astype(F32)).astype(BF)
        for high in range(2):
            for side in range(2):
                out_ref[block, 2 * high + side] = last[:, side * HALF:(side + 1) * HALF]


def last_gate(core, taps, got, other, keep, theirs):
    vmem = pl.BlockSpec(memory_space=pltpu.VMEM)
    return pl.pallas_call(
        last_kernel,
        in_specs=[SMEM, SMEM, ANY, ANY, vmem, vmem],
        out_specs=vmem,
        out_shape=jax.ShapeDtypeStruct((BLOCKS, 4, TILE, HALF), BF),
        scratch_shapes=[pltpu.VMEM((2, BLOCKS, TILE, N2), BF), pltpu.SemaphoreType.DMA((2,))],
        compiler_params=pltpu.CompilerParams(vmem_limit_bytes=16 * MIB),
    )(core, taps, got, other, keep, theirs)


def mix_kernel(weights_ref, values_ref, keep_ref, send_ref, wide_ref):
    channels = 2 * BLOCKS
    rows = 2 * TILE
    for part in range(HALF // LANES):
        wide_ref[part] = values_ref[:, :, part * LANES:(part + 1) * LANES].astype(F32).reshape(
            channels * rows, LANES
        )
    for row in range(rows):
        piece = jnp.concatenate(
            [wide_ref[part, pl.ds(row, channels, stride=rows), :].astype(BF) for part in range(HALF // LANES)],
            axis=1,
        )
        mixed = jnp.dot(weights_ref[...], piece, preferred_element_type=F32)
        keep_ref[:, row * HALF:(row + 1) * HALF] = mixed[:TILE]
        send_ref[:, row * HALF:(row + 1) * HALF] = mixed[TILE:].astype(BF)


def mix(weights, values):
    vmem = pl.BlockSpec(memory_space=pltpu.VMEM)
    width = 2 * TILE * HALF
    return pl.pallas_call(
        mix_kernel,
        in_specs=[vmem, vmem],
        out_specs=(vmem, vmem),
        out_shape=(jax.ShapeDtypeStruct((TILE, width), F32), jax.ShapeDtypeStruct((TILE, width), BF)),
        scratch_shapes=[pltpu.VMEM((HALF // LANES, 4 * BLOCKS * TILE, LANES), F32)],
        compiler_params=pltpu.CompilerParams(vmem_limit_bytes=24 * MIB),
    )(weights, values)


def finish_kernel(core_ref, second_ref, keep_ref, theirs_ref, out_ref):
    core = core_ref[0]
    for row in range(2 * TILE):
        here = slice(row * HALF, (row + 1) * HALF)
        mine = pl.ds(pl.multiple_of(row * N2 + core * HALF, HALF), HALF)
        other = pl.ds(pl.multiple_of(row * N2 + (1 - core) * HALF, HALF), HALF)
        out_ref[:, mine] = second_ref[:, mine].astype(F32) - keep_ref[:, here]
        out_ref[:, other] = second_ref[:, other].astype(F32) - theirs_ref[:, here].astype(F32)


def finish(core, second, keep, theirs):
    vmem = pl.BlockSpec(memory_space=pltpu.VMEM)
    return pl.pallas_call(
        finish_kernel,
        in_specs=[SMEM, vmem, vmem, vmem],
        out_specs=vmem,
        out_shape=jax.ShapeDtypeStruct(second.shape, F32),
        compiler_params=pltpu.CompilerParams(vmem_limit_bytes=16 * MIB),
    )(core, second, keep, theirs)


def on_device(coupled_first, coupled_second, spectra, short_taps, mixing):
    group = lax.axis_index("ch")
    seat = lax.axis_index("seq")
    core = group % 2
    core_one = core[None].astype(jnp.int32)
    consts = tuple(jnp.asarray(t) for t in tables())

    near_taps = swap(short_taps)
    pair = jnp.where(seat // TILE == core, short_taps, near_taps)
    taps = lax.dynamic_index_in_dim(pair, seat % TILE, axis=2, keepdims=False)
    near_mixing = swap(mixing)
    near = jnp.where(core == 0, jnp.concatenate([mixing, near_mixing]), jnp.concatenate([near_mixing, mixing]))
    far = lax.ppermute(near, "ch", [(i, i ^ 2) for i in range(4)])
    ordered = jnp.where(group < 2, jnp.stack([near, far]), jnp.stack([far, near]))
    ordered = ordered.transpose(1, 0, 2).reshape(4 * TILE, 4 * TILE)
    weights = jnp.concatenate(
        [
            lax.dynamic_slice_in_dim(ordered, group * TILE, TILE, axis=1),
            lax.dynamic_slice_in_dim(ordered, (group ^ 1) * TILE, TILE, axis=1),
        ],
        axis=1,
    ).T

    send = split_channels(1 - core, jnp.zeros_like(core), TILE, coupled_first, spectra)
    theirs = swap(send)
    buffer = split_channels(core, core, BLOCKS, coupled_first, spectra)
    buffer = place(core_one, theirs, buffer)
    got = lax.all_to_all(buffer, "seq", split_axis=0, concat_axis=0, tiled=True)

    other = swap(got[:, 0])
    mine = first_conv(core_one, got, other, consts)
    theirs = swap(mine)
    keep, send = second_conv(core_one, taps, got, other, mine, theirs, consts)
    theirs = swap(send)
    spread = last_gate(core_one, taps, got, other, keep, theirs)
    values = lax.all_to_all(
        spread.reshape(4 * BLOCKS, TILE, HALF), ("seq", "ch"), split_axis=0, concat_axis=0, tiled=True
    )
    keep, send = mix(weights, values)
    theirs = swap(send)
    return finish(core_one, coupled_second, keep, theirs)


def solution(mesh):
    return jax.shard_map(
        on_device,
        mesh=mesh,
        in_specs=(
            P("ch", "seq"),
            P("ch", "seq"),
            P(None, None, "ch", "seq"),
            P(None, None, "ch"),
            P("ch", None),
        ),
        out_specs=P("ch", "seq"),
        check_vma=False,
    )
```

time: 991 us -> 115 us (0.12)
  local copies, waits for them, and re-layouts: 392 us -> 8.83 us
  matrix products: 312 us -> 0 us
  waiting for transfers between devices: 104 us -> 22.8 us
  blocking collectives: 108 us -> 41.9 us
  Pallas kernels: 0 us -> 26.1 us
  other arithmetic: 20.7 us -> 0.25 us
  starting transfers between devices: 32.3 us -> 14.8 us
  between operations: 14.7 us -> 0.16 us
    dot_general x17 -> x0, matrix products: 270 us -> none  [the longest x16 268 us: along_last(): jnp.einsum('...n,nk->...k', values, table, preferred_element_type=jnp.flo...]
    unnamed x75 -> x30, local copies, waits for them, and re-layouts: 153 us -> 8.59 us
    another operation x8 -> x0, local copies, waits for them, and re-layouts: 74 us -> none  [the longest x2 24.1 us: section_third(): return jnp.stack([out_real, out_imag]).astype(jnp.bfloat16)]
    all_to_all x14 -> x0, local copies, waits for them, and re-layouts: 67.2 us -> none  [the longest x2 19.7 us: conv_sequence(): lax.all_to_all(spectrum, 'seq', split_axis=3, concat_axis=2, tiled=True)]
    all_to_all x7 -> x1, blocking collectives: 108 us -> 41.9 us  [on_device(): got = lax.all_to_all(buffer, 'seq', split_axis=0, concat_axis=0, tiled=True)]
    all_to_all x5 -> x1, waiting for transfers between devices: 56.9 us -> 4.51 us  [on_device(): lax.all_to_all(spread.reshape(4 * BLOCKS, TILE, HALF), ('seq', 'ch'), spl...]
    reduce_scatter x1 -> x0, waiting for transfers between devices: 47.6 us -> none  [project(): lax.psum_scatter(lax.dot_general(weights, values, (((0,), (0,)), ((), ())...]
    unnamed x8 -> x0, matrix products: 41.9 us -> none
  transfers between devices with their start and end apart: 7 -> 9, of which waited for: 6 -> 9; matrix products, arithmetic and copies ran while one was open for 5% -> 0% of each run, Pallas kernels for 0% -> 2%
where the time goes in v1:
time: 115 us
  blocking collectives  41.9 us (36%)
  Pallas kernels  26.1 us (23%)
  waiting for transfers between devices  22.8 us (20%)
  starting transfers between devices  14.8 us (13%)
  local copies, waits for them, and re-layouts  8.83 us (8%)
    all_to_all x1, blocking collectives, on_device(): got = lax.all_to_all(buffer, 'seq', split_axis=0, concat_axis=0, tiled=True)  41.9 us
    ppermute x1, waiting for transfers between devices, on_device(): far = lax.ppermute(near, 'ch', [(i, i ^ 2) for i in range(4)])  10.2 us
    pallas_call x1, Pallas kernels, second_conv(): pl.pallas_call(second_conv_kernel, in_specs=[SMEM, SMEM, ANY, ANY, vmem,...  9.37 us
    unnamed x30, local copies, waits for them, and re-layouts  8.59 us
    ppermute x7, waiting for transfers between devices, swap(): lax.ppermute(value, 'ch', [(i, i ^ 1) for i in range(lax.axis_size('ch'))])  8.11 us
    ppermute x7, starting transfers between devices, swap(): lax.ppermute(value, 'ch', [(i, i ^ 1) for i in range(lax.axis_size('ch'))])  6.9 us
    pallas_call x1, Pallas kernels, first_conv(): pl.pallas_call(first_conv_kernel, in_specs=[SMEM] + [ANY] * 7, out_specs=...  6.57 us
    all_to_all x1, starting transfers between devices, on_device(): lax.all_to_all(spread.reshape(4 * BLOCKS, TILE, HALF), ('seq', 'ch'), spl...  5.67 us
  transfers between devices with their start and end apart: 9, of which 9 were waited for; matrix products, arithmetic and copies ran while one was open for 0% of the time, Pallas kernels for 2%

profile of v1, /device:TPU:1, one launch (start us, length us, event | category | flops | bytes accessed | tf_op | source)
XLA Modules:
  0.0 114.8 jit_solution(18307886724649706922)
XLA Ops:
  0.0 0.1 pad_add_fusion.half_ref
  0.1 1.6 %copy-done.2 = bf16[2,2,16,16384]{3,2,1,0:T(8,128)(2,1)S(1)} copy-done((bf16[2,2,16,16384]{3,2,1,0:T(8,128)(2,1)S(1)}, bf16[2,2,16,16384]{3,2,1,0:T(8,128)(2,1)}, u32[]{:S(2)}) %copy-start.2) | copy-done | bytes 2097176
  1.7 1.0 copy-done.9
  2.7 1.8 %shard_map.100 = bf16[16,5,16,512]{3,2,1,0:T(8,128)(2,1)S(1)} custom-call(s32[2]{0:T(128)S(1)} %pad_add_fusion.half_ref, bf16[16,16384]{1,0:T(8,128)(2,1)S(1)} %copy-done.9, bf16[2,2,16,16384]{3,2,1,0:T(8,128)(2,1)S(1)} %copy-done.2), custom_call_target="tpu_custom_call" | custom-call | bytes 8388608 | tf_op jit(solution)/shard_map/pallas_call | solution.py:94
  4.6 1.5 %collective-permute-start.3 = (bf16[16,5,16,512]{3,2,1,0:T(8,128)(2,1)S(1)}, bf16[16,5,16,512]{3,2,1,0:T(8,128)(2,1)S(1)}, u32[]{:S(2)}, u32[]{:S(2)}) collective-permute-start(bf16[16,5,16,512]{3,2,1,0:T(8,128)(2,1)S(1)} %shard_map.100), channel_id=1, source_target_pairs={{0,1},{1,0},{2,3},{3,2},{4,5},{5,4},{6,7},{7,6},{8,9},{9,8},{10,11... | collective-permute-start | bytes 3932168 | tf_op jit(solution)/shard_map/ppermute | solution.py:54
  6.1 0.1 pad_add_fusion.1.half_ref
  6.1 0.0 copy-done.3
  6.1 1.8 %shard_map.101.whole_ref = bf16[32,5,16,512]{3,2,1,0:T(8,128)(2,1)S(1)} custom-call(s32[2]{0:T(128)S(1)} %pad_add_fusion.1.half_ref, bf16[16,16384]{1,0:T(8,128)(2,1)S(1)} %copy-done.9, bf16[2,2,16,16384]{3,2,1,0:T(8,128)(2,1)S(1)} %copy-done.3), custom_call_target="tpu_custom_call" | custom-call | bytes 8388608 | tf_op jit(solution)/shard_map/pallas_call | solution.py:94
  8.0 0.7 collective-permute-done.3.piece_ref
  8.7 0.4 shard_map.102
  9.1 0.0 copy-start
  9.1 0.0 copy-start.4
  9.1 0.0 copy-start.10
  9.2 41.9 %all_to_all.10.got_ref = bf16[32,5,16,512]{3,2,1,0:T(8,128)(2,1)S(1)} all-to-all(bf16[32,5,16,512]{3,2,1,0:T(8,128)(2,1)S(1)} %shard_map.102), channel_id=1, replica_groups=mesh['seq'=32,'ch'=4] {'seq'}, dimensions={0} | all-to-all | bytes 5242880 | tf_op jit(solution)/shard_map/all_to_all | solution.py:451
  51.1 0.0 copy-start.13
  51.1 2.3 %collective-permute-start.4 = (bf16[32,16,512]{2,1,0:T(8,128)(2,1)S(1)}, bf16[32,16,512]{2,1,0:T(8,128)(2,1)S(1)}, u32[]{:S(2)}, u32[]{:S(2)}) collective-permute-start(bf16[32,16,512]{2,1,0:T(8,128)(2,1)S(1)} %slice_bitcast_fusion), channel_id=1, source_target_pairs={{0,1},{1,0},{2,3},{3,2},{4,5},{5,4},{6,7},{7,6},{8,9},{9,8},{10,11... | collective-permute-start | bytes 1572872 | tf_op jit(solution)/shard_map/ppermute | solution.py:54
  53.3 1.5 %collective-permute-done.4.other_ref = bf16[32,16,512]{2,1,0:T(8,128)(2,1)S(1)} collective-permute-done((bf16[32,16,512]{2,1,0:T(8,128)(2,1)S(1)}, bf16[32,16,512]{2,1,0:T(8,128)(2,1)S(1)}, u32[]{:S(2)}, u32[]{:S(2)}) %collective-permute-start.4) | collective-permute-done | bytes 524320 | tf_op jit(solution)/shard_map/ppermute | solution.py:54
  54.9 0.0 copy-done.6
  54.9 6.6 %shard_map.103.mine_ref = bf16[2,32,16,512]{3,2,1,0:T(8,128)(2,1)} custom-call(s32[1]{0:T(128)} %bitcast.core_ref, bf16[32,5,16,512]{3,2,1,0:T(8,128)(2,1)S(1)} %all_to_all.10.got_ref, bf16[32,16,512]{2,1,0:T(8,128)(2,1)S(1)} %collective-permute-done.4.other_ref, bf16[2,512,1024]{2,1,0:T(8,128)(2,1)S(1)} %copy-done.4, ...), custom_call_target="tpu_custom_call" | custom-call | flops 2500000000 | bytes 8388608 | tf_op jit(solution)/shard_map/pallas_call | solution.py:262
  61.5 0.5 collective-permute-start.5
  61.9 0.1 collective-permute-start.2
  62.1 2.1 %collective-permute-done.2 = f32[2,3,16]{2,0,1:T(2,128)S(1)} collective-permute-done((f32[2,3,16]{2,0,1:T(2,128)S(1)}, f32[2,3,16]{2,0,1:T(2,128)S(1)}, u32[]{:S(2)}, u32[]{:S(2)}) %collective-permute-start.2) | collective-permute-done | bytes 416 | tf_op jit(solution)/shard_map/ppermute | solution.py:54
  64.2 0.1 dynamic-slice_select_fusion
  64.3 0.1 copy.29
  64.4 0.2 collective-permute-done.5.theirs_ref
  64.6 1.6 %copy-done.1 = f32[2,2,272,512]{3,2,1,0:T(8,128)S(1)} copy-done((f32[2,2,272,512]{3,2,1,0:T(8,128)S(1)}, f32[2,2,272,512]{3,2,1,0:T(8,128)}, u32[]{:S(2)}) %copy-start.1) | copy-done | bytes 2228248
  66.2 1.6 %copy-done.5 = bf16[2,512,1024]{2,1,0:T(8,128)(2,1)S(1)} copy-done((bf16[2,512,1024]{2,1,0:T(8,128)(2,1)S(1)}, bf16[2,512,1024]{2,1,0:T(8,128)(2,1)}, u32[]{:S(2)}) %copy-start.5) | copy-done | bytes 2097176
  67.8 1.6 %copy-done.7 = bf16[2,2,512,512]{3,2,1,0:T(8,128)(2,1)S(1)} copy-done((bf16[2,2,512,512]{3,2,1,0:T(8,128)(2,1)S(1)}, bf16[2,2,512,512]{3,2,1,0:T(8,128)(2,1)}, u32[]{:S(2)}) %copy-start.7) | copy-done | bytes 2097176
  69.4 9.4 %shard_map.104 = (f32[32,16,512]{2,1,0:T(8,128)S(1)}, bf16[32,16,512]{2,1,0:T(8,128)(2,1)S(1)}) custom-call(s32[1]{0:T(128)} %bitcast.core_ref, f32[2,3]{1,0:T(2,128)S(1)} %bitcast.17, bf16[32,5,16,512]{3,2,1,0:T(8,128)(2,1)S(1)} %all_to_all.10.got_ref, bf16[32,16,512]{2,1,0:T(8,128)(2,1)S(1)} %collective-permute-done.4.other_ref, ...), custom_call_target="tpu_custom_call" | custom-call | flops 2500000000 | bytes 10485760 | tf_op jit(solution)/shard_map/pallas_call | solution.py:329
  78.8 0.5 collective-permute-start.6
  79.2 1.5 %collective-permute-done.6.theirs_ref = bf16[32,16,512]{2,1,0:T(8,128)(2,1)S(1)} collective-permute-done((bf16[32,16,512]{2,1,0:T(8,128)(2,1)S(1)}, bf16[32,16,512]{2,1,0:T(8,128)(2,1)S(1)}, u32[]{:S(2)}, u32[]{:S(2)}) %collective-permute-start.6) | collective-permute-done | bytes 524320 | tf_op jit(solution)/shard_map/ppermute | solution.py:54
  80.8 3.5 %shard_map.105 = bf16[32,4,16,256]{3,2,1,0:T(8,128)(2,1)S(1)} custom-call(s32[1]{0:T(128)} %bitcast.core_ref, f32[2,3]{1,0:T(2,128)S(1)} %bitcast.18, bf16[32,5,16,512]{3,2,1,0:T(8,128)(2,1)S(1)} %all_to_all.10.got_ref, bf16[32,16,512]{2,1,0:T(8,128)(2,1)S(1)} %collective-permute-done.4.other_ref, f32[32,16,512]{2,1,0:T(8,128)S(1)} %get-tuple-element.9.keep_ref, ...), custom_call_target="tpu_custom_call" | custom-call | tf_op jit(solution)/shard_map/pallas_call | solution.py:363
  84.3 0.0 copy-start.8
  84.3 1.0 copy-done.8
  85.3 5.7 %all-to-all-start.1 = ((bf16[128,16,256]{2,1,0:T(8,128)(2,1)}), bf16[128,16,256]{2,1,0:T(8,128)(2,1)S(1)}, u32[]{:S(2)}, u32[]{:S(2)}) async-start(bf16[128,16,256]{2,1,0:T(8,128)(2,1)} %bitcast.16), calls=%async_computation.1 | async-start | bytes 2097152 | tf_op jit(solution)/shard_map/all_to_all | solution.py:459
  90.9 0.0 copy-done.12
  90.9 1.1 collective-permute-start
  92.1 0.8 collective-permute-done
  92.9 2.2 %collective-permute-start.1 = (bf16[32,64]{1,0:T(8,128)(2,1)S(1)}, bf16[32,64]{1,0:T(8,128)(2,1)S(1)}, u32[]{:S(2)}, u32[]{:S(2)}) collective-permute-start(bf16[32,64]{1,0:T(8,128)(2,1)S(1)} %maximum_select_fusion.2), channel_id=1, source_target_pairs={{0,2},{1,3},{2,0},{3,1},{4,6},{5,7},{6,4},{7,5},{8,10},{9,11},{10,... | collective-permute-start | bytes 12296 | tf_op jit(solution)/shard_map/ppermute | solution.py:436
  95.1 10.2 %collective-permute-done.1 = bf16[32,64]{1,0:T(8,128)(2,1)S(1)} collective-permute-done((bf16[32,64]{1,0:T(8,128)(2,1)S(1)}, bf16[32,64]{1,0:T(8,128)(2,1)S(1)}, u32[]{:S(2)}, u32[]{:S(2)}) %collective-permute-start.1) | collective-permute-done | bytes 4128 | tf_op jit(solution)/shard_map/ppermute | solution.py:436
  105.4 0.1 constant_dynamic-slice_fusion.1
  105.5 0.1 copy.31
  105.5 0.1 copy.32
  105.6 4.5 %all-to-all-done.1.values_ref = bf16[128,16,256]{2,1,0:T(8,128)(2,1)S(1)} async-done(((bf16[128,16,256]{2,1,0:T(8,128)(2,1)}), bf16[128,16,256]{2,1,0:T(8,128)(2,1)S(1)}, u32[]{:S(2)}, u32[]{:S(2)}) %all-to-all-start.1) | async-done | bytes 1048608 | tf_op jit(solution)/shard_map/all_to_all | solution.py:459
  110.1 1.5 %shard_map.106 = (f32[16,8192]{1,0:T(8,128)S(1)}, bf16[16,8192]{1,0:T(8,128)(2,1)S(1)}) custom-call(bf16[32,64]{1,0:T(8,128)(2,1)S(1)} %maximum_bitcast_fusion.weights_ref, bf16[128,16,256]{2,1,0:T(8,128)(2,1)S(1)} %all-to-all-done.1.values_ref), custom_call_target="tpu_custom_call" | custom-call | tf_op jit(solution)/shard_map/pallas_call | solution.py:393
  111.6 0.9 collective-permute-start.7
  112.6 1.2 %collective-permute-done.7.theirs_ref = bf16[16,8192]{1,0:T(8,128)(2,1)S(1)} collective-permute-done((bf16[16,8192]{1,0:T(8,128)(2,1)S(1)}, bf16[16,8192]{1,0:T(8,128)(2,1)S(1)}, u32[]{:S(2)}, u32[]{:S(2)}) %collective-permute-start.7) | collective-permute-done | bytes 262176 | tf_op jit(solution)/shard_map/ppermute | solution.py:54
  113.7 1.1 shard_map.107
  (20 shorter events, 0.1 us)
Async XLA Ops:
  0.1 1.6 %copy-start.2 = (bf16[2,2,16,16384]{3,2,1,0:T(8,128)(2,1)S(1)}, bf16[2,2,16,16384]{3,2,1,0:T(8,128)(2,1)}, u32[]{:S(2)}) copy-start(bf16[2,2,16,16384]{3,2,1,0:T(8,128)(2,1)} %filter_ref.3) | copy-start | bytes 6291460
  1.7 1.0 copy-start.9
  2.7 3.4 %copy-start.3 = (bf16[2,2,16,16384]{3,2,1,0:T(8,128)(2,1)S(1)}, bf16[2,2,16,16384]{3,2,1,0:T(8,128)(2,1)}, u32[]{:S(2)}) copy-start(bf16[2,2,16,16384]{3,2,1,0:T(8,128)(2,1)} %filter_ref.3) | copy-start | bytes 6291460
  4.6 4.2 %collective-permute-start.3 = (bf16[16,5,16,512]{3,2,1,0:T(8,128)(2,1)S(1)}, bf16[16,5,16,512]{3,2,1,0:T(8,128)(2,1)S(1)}, u32[]{:S(2)}, u32[]{:S(2)}) collective-permute-start(bf16[16,5,16,512]{3,2,1,0:T(8,128)(2,1)S(1)} %shard_map.100), channel_id=1, source_target_pairs={{0,1},{1,0},{2,3},{3,2},{4,5},{5,4},{6,7},{7,6},{8,9},{9,8},{10,11... | collective-permute-start | bytes 3932168 | tf_op jit(solution)/shard_map/ppermute | solution.py:54
  8.7 46.2 %copy-start.6 = (bf16[2,2,512,512]{3,2,1,0:T(8,128)(2,1)S(1)}, bf16[2,2,512,512]{3,2,1,0:T(8,128)(2,1)}, u32[]{:S(2)}) copy-start(bf16[2,2,512,512]{3,2,1,0:T(8,128)(2,1)} %constant.65.clone.rest_1_) | copy-start | bytes 6291460
  9.1 45.8 %copy-start = (f32[2,2,272,512]{3,2,1,0:T(8,128)S(1)}, f32[2,2,272,512]{3,2,1,0:T(8,128)}, u32[]{:S(2)}) copy-start(f32[2,2,272,512]{3,2,1,0:T(8,128)} %constant.67.clone.rest_3_) | copy-start | bytes 6684676
  9.1 45.8 %copy-start.4 = (bf16[2,512,1024]{2,1,0:T(8,128)(2,1)S(1)}, bf16[2,512,1024]{2,1,0:T(8,128)(2,1)}, u32[]{:S(2)}) copy-start(bf16[2,512,1024]{2,1,0:T(8,128)(2,1)} %constant.64.clone.rest_0_) | copy-start | bytes 6291460
  9.1 45.7 %copy-start.10 = (bf16[3,256,256]{2,1,0:T(8,128)(2,1)S(1)}, bf16[3,256,256]{2,1,0:T(8,128)(2,1)}, u32[]{:S(2)}) copy-start(bf16[3,256,256]{2,1,0:T(8,128)(2,1)} %constant.68.clone.rest_4_) | copy-start | bytes 1179652
  51.1 10.9 %copy-start.13 = (f32[2,3,16]{2,0,1:T(2,128)S(1)}, f32[2,3,16]{2,0,1:T(2,128)}, u32[]{:S(2)}) copy-start(f32[2,3,16]{2,0,1:T(2,128)} %param.13) | copy-start | bytes 1156
  51.1 3.8 %collective-permute-start.4 = (bf16[32,16,512]{2,1,0:T(8,128)(2,1)S(1)}, bf16[32,16,512]{2,1,0:T(8,128)(2,1)S(1)}, u32[]{:S(2)}, u32[]{:S(2)}) collective-permute-start(bf16[32,16,512]{2,1,0:T(8,128)(2,1)S(1)} %slice_bitcast_fusion), channel_id=1, source_target_pairs={{0,1},{1,0},{2,3},{3,2},{4,5},{5,4},{6,7},{7,6},{8,9},{9,8},{10,11... | collective-permute-start | bytes 1572872 | tf_op jit(solution)/shard_map/ppermute | solution.py:54
  61.5 3.1 %collective-permute-start.5 = (bf16[2,32,16,512]{3,2,1,0:T(8,128)(2,1)}, bf16[2,32,16,512]{3,2,1,0:T(8,128)(2,1)}, u32[]{:S(2)}, u32[]{:S(2)}) collective-permute-start(bf16[2,32,16,512]{3,2,1,0:T(8,128)(2,1)} %shard_map.103.mine_ref), channel_id=1, source_target_pairs={{0,1},{1,0},{2,3},{3,2},{4,5},{5,4},{6,7},{7,6},{8,9},{9,8},{10,11... | collective-permute-start | bytes 3145736 | tf_op jit(solution)/shard_map/ppermute | solution.py:54
  61.9 2.3 %collective-permute-start.2 = (f32[2,3,16]{2,0,1:T(2,128)S(1)}, f32[2,3,16]{2,0,1:T(2,128)S(1)}, u32[]{:S(2)}, u32[]{:S(2)}) collective-permute-start(f32[2,3,16]{2,0,1:T(2,128)S(1)} %copy-done.13), channel_id=1, source_target_pairs={{0,1},{1,0},{2,3},{3,2},{4,5},{5,4},{6,7},{7,6},{8,9},{9,8},{10,11... | collective-permute-start | bytes 1160 | tf_op jit(solution)/shard_map/ppermute | solution.py:54
  64.6 1.6 %copy-start.1 = (f32[2,2,272,512]{3,2,1,0:T(8,128)S(1)}, f32[2,2,272,512]{3,2,1,0:T(8,128)}, u32[]{:S(2)}) copy-start(f32[2,2,272,512]{3,2,1,0:T(8,128)} %constant.67.clone.rest_3_) | copy-start | bytes 6684676
  66.2 1.6 %copy-start.5 = (bf16[2,512,1024]{2,1,0:T(8,128)(2,1)S(1)}, bf16[2,512,1024]{2,1,0:T(8,128)(2,1)}, u32[]{:S(2)}) copy-start(bf16[2,512,1024]{2,1,0:T(8,128)(2,1)} %constant.64.clone.rest_0_) | copy-start | bytes 6291460
  67.8 1.6 %copy-start.7 = (bf16[2,2,512,512]{3,2,1,0:T(8,128)(2,1)S(1)}, bf16[2,2,512,512]{3,2,1,0:T(8,128)(2,1)}, u32[]{:S(2)}) copy-start(bf16[2,2,512,512]{3,2,1,0:T(8,128)(2,1)} %constant.65.clone.rest_1_) | copy-start | bytes 6291460
  78.8 2.0 %collective-permute-start.6 = (bf16[32,16,512]{2,1,0:T(8,128)(2,1)S(1)}, bf16[32,16,512]{2,1,0:T(8,128)(2,1)S(1)}, u32[]{:S(2)}, u32[]{:S(2)}) collective-permute-start(bf16[32,16,512]{2,1,0:T(8,128)(2,1)S(1)} %get-tuple-element.10), channel_id=1, source_target_pairs={{0,1},{1,0},{2,3},{3,2},{4,5},{5,4},{6,7},{7,6},{8,9},{9,8},{10,11... | collective-permute-start | bytes 1572872 | tf_op jit(solution)/shard_map/ppermute | solution.py:54
  80.7 10.2 %copy-start.12 = (bf16[16,64]{1,0:T(8,128)(2,1)S(1)}, bf16[16,64]{1,0:T(8,128)(2,1)}, u32[]{:S(2)}) copy-start(bf16[16,64]{1,0:T(8,128)(2,1)} %param.14) | copy-start | bytes 6148
  84.3 1.0 copy-start.8
  85.3 28.5 %copy-start.11 = (bf16[16,16384]{1,0:T(8,128)(2,1)S(1)}, bf16[16,16384]{1,0:T(8,128)(2,1)}, u32[]{:S(2)}) copy-start(bf16[16,16384]{1,0:T(8,128)(2,1)} %second_ref.1) | copy-start | bytes 1572868
  85.3 24.9 %all-to-all-start.1 = ((bf16[128,16,256]{2,1,0:T(8,128)(2,1)}), bf16[128,16,256]{2,1,0:T(8,128)(2,1)S(1)}, u32[]{:S(2)}, u32[]{:S(2)}) async-start(bf16[128,16,256]{2,1,0:T(8,128)(2,1)} %bitcast.16), calls=%async_computation.1 | async-start | bytes 2097152 | tf_op jit(solution)/shard_map/all_to_all | solution.py:459
  90.9 2.0 %collective-permute-start = (bf16[16,64]{1,0:T(8,128)(2,1)S(1)}, bf16[16,64]{1,0:T(8,128)(2,1)S(1)}, u32[]{:S(2)}, u32[]{:S(2)}) collective-permute-start(bf16[16,64]{1,0:T(8,128)(2,1)S(1)} %copy-done.12), channel_id=1, source_target_pairs={{0,1},{1,0},{2,3},{3,2},{4,5},{5,4},{6,7},{7,6},{8,9},{9,8},{10,11... | collective-permute-start | bytes 6152 | tf_op jit(solution)/shard_map/ppermute | solution.py:54
  92.9 12.4 %collective-permute-start.1 = (bf16[32,64]{1,0:T(8,128)(2,1)S(1)}, bf16[32,64]{1,0:T(8,128)(2,1)S(1)}, u32[]{:S(2)}, u32[]{:S(2)}) collective-permute-start(bf16[32,64]{1,0:T(8,128)(2,1)S(1)} %maximum_select_fusion.2), channel_id=1, source_target_pairs={{0,2},{1,3},{2,0},{3,1},{4,6},{5,7},{6,4},{7,5},{8,10},{9,11},{10,... | collective-permute-start | bytes 12296 | tf_op jit(solution)/shard_map/ppermute | solution.py:436
  111.6 2.1 %collective-permute-start.7 = (bf16[16,8192]{1,0:T(8,128)(2,1)S(1)}, bf16[16,8192]{1,0:T(8,128)(2,1)S(1)}, u32[]{:S(2)}, u32[]{:S(2)}) collective-permute-start(bf16[16,8192]{1,0:T(8,128)(2,1)S(1)} %get-tuple-element.12), channel_id=1, source_target_pairs={{0,1},{1,0},{2,3},{3,2},{4,5},{5,4},{6,7},{7,6},{8,9},{9,8},{10,11... | collective-permute-start | bytes 786440 | tf_op jit(solution)/shard_map/ppermute | solution.py:54

commit v2 on v0

v2 whole, which is shorter than its diff:
```python
import functools

import jax
import jax.numpy as jnp
import numpy as np
from jax import lax
from jax.experimental import pallas as pl
from jax.experimental.pallas import tpu as pltpu
from jax.sharding import PartitionSpec as P

BF = jnp.bfloat16
F32 = jnp.float32
LANES = 128
N2 = 512
N1 = 1024
HALF = N1 // 4
EXTRA = 16
ROWS = HALF + EXTRA
SCALE = 1.0 / (N1 * N2)
TILE = 16
PLANES = (None, (0, 0), (0, 1), (1, 0), (1, 1))
BLOCKS = 32
ANY = pl.BlockSpec(memory_space=pl.ANY)
VMEM = pl.BlockSpec(memory_space=pltpu.VMEM)
SMEM = pl.BlockSpec(memory_space=pltpu.SMEM)
MIB = 1 << 20


def tables():
    rows = np.arange(N1).reshape(BLOCKS, 2, TILE).transpose(1, 0, 2).reshape(2, -1)
    order = np.stack([rows.reshape(-1), rows[::-1].reshape(-1)])
    freq = np.arange(HALF)[None, :] + HALF * np.arange(2)[:, None]
    angle = (freq[:, :, None] * order[:, None, :] % N1) * (2.0 * np.pi / N1)
    forward = np.concatenate([np.cos(angle), -np.sin(angle)], axis=1)
    forward[0, HALF] = 1.0 - 2.0 * (order[0] % 2)
    inner = np.arange(N2)
    angle = (inner[:, None] * inner[None, :] % N2) * (2.0 * np.pi / N2)
    cosine, sine = np.cos(angle), np.sin(angle)
    wave = np.concatenate([cosine, sine], axis=1)
    angle = freq[:, :, None] * inner[None, None, :] * (2.0 * np.pi / (N1 * N2))
    twist = np.stack([np.cos(angle), np.sin(angle)], axis=1)
    special = np.zeros((2, 2, EXTRA, N2))
    special[0, 0, 0] = np.cos(inner * (2.0 * np.pi / N1))
    special[0, 1, 0] = np.sin(inner * (2.0 * np.pi / N1))
    twist = np.concatenate([twist, special], axis=2)
    bf = lambda a: np.asarray(a, dtype=np.float32).astype(jnp.bfloat16)
    return (
        bf(forward), bf(wave), bf(twist),
    )


def swap(value):
    return lax.ppermute(value, "ch", [(i, i ^ 1) for i in range(lax.axis_size("ch"))])


def params(mib):
    return pltpu.CompilerParams(vmem_limit_bytes=mib * MIB)


def cost(gflop, mib):
    return pl.CostEstimate(flops=int(gflop * 1e9), bytes_accessed=int(mib * MIB), transcendentals=0)


def in_hbm(value):
    return pltpu.with_memory_space_constraint(value, pltpu.HBM)


def fetch(source, target, sems, index):
    copy = pltpu.make_async_copy(source, target, sems.at[index])
    copy.start()
    return copy


def split_field(source, wide_ref):
    for row in range(TILE):
        piece = source[:, row * N2:(row + 1) * N2].astype(F32)
        for part in range(N2 // LANES):
            wide_ref[part, row * TILE:(row + 1) * TILE, :] = piece[:, part * LANES:(part + 1) * LANES]


def split_filter(half, source, wide_ref):
    lane = lax.broadcasted_iota(jnp.int32, (TILE, LANES), 1)
    for row in range(TILE):
        low = pl.multiple_of(row * N1 + half * HALF, HALF)
        high = pl.multiple_of(row * N1 + (3 - half) * HALF, HALF)
        across = pl.multiple_of(row * N1 + (2 + half) * HALF, HALF)
        low_piece = source[:, pl.ds(low, HALF)].astype(F32)
        high_piece = source[:, pl.ds(high, HALF)].astype(F32)
        across_piece = source[:, pl.ds(across, LANES)].astype(F32)
        rows = slice(row * TILE, (row + 1) * TILE)
        wide_ref[0, rows, :] = low_piece[:, :LANES]
        wide_ref[1, rows, :] = low_piece[:, LANES:]
        wide_ref[2, rows, :] = jnp.where(lane == 0, across_piece, high_piece[:, :LANES])
        wide_ref[3, rows, :] = high_piece[:, LANES:]


def split_kernel(keep, core_ref, signal_ref, filter_ref, *refs):
    if keep:
        forward_hbm, out_ref, forward_ref, wide_ref, out_vmem, in_vmem, sems = refs
    else:
        out_ref, wide_ref, out_vmem, in_vmem, sems = refs
    core = core_ref[0]
    half = core if keep else 1 - core
    target = out_ref.at[pl.ds(core * TILE, TILE)] if keep else out_ref
    here = pl.ds(pl.multiple_of(half * (TILE * N2), TILE * N2), TILE * N2)
    count = len(PLANES)
    loads = [fetch(signal_ref.at[:, here], in_vmem.at[0, :, :TILE * N2], sems, 0)]
    for plane in range(1, count):
        loads.append(fetch(filter_ref.at[PLANES[plane]], in_vmem.at[plane], sems, plane))
    stores = [fetch(forward_hbm.at[core], forward_ref, sems, 2 * count)] if keep else []
    for plane in range(count):
        loads[plane].wait()
        wide = wide_ref.at[plane % 2]
        if plane == 0:
            split_field(in_vmem.at[plane], wide)
        else:
            split_filter(half, in_vmem.at[plane], wide)
        for channel in range(TILE):
            for lanes in range(N2 // LANES):
                out_vmem[channel, plane, :, lanes * LANES:(lanes + 1) * LANES] = wide[
                    lanes, pl.ds(channel, TILE, stride=TILE), :
                ].astype(BF)
        stores.append(fetch(out_vmem.at[:, plane], target.at[:, plane], sems, count + plane))
    for store in stores:
        store.wait()


def split(keep, core, signal, spectra, *forward):
    count = len(PLANES)
    shape = jax.ShapeDtypeStruct((BLOCKS if keep else TILE, count, TILE, N2), BF)
    return pl.pallas_call(
        functools.partial(split_kernel, keep),
        in_specs=[SMEM, ANY, ANY] + [ANY] * len(forward),
        out_specs=(ANY, VMEM) if keep else ANY,
        out_shape=(shape, jax.ShapeDtypeStruct((2 * HALF, N1), BF)) if keep else shape,
        scratch_shapes=[
            pltpu.VMEM((2, N2 // LANES, TILE * TILE, LANES), F32),
            pltpu.VMEM((TILE, count, TILE, N2), BF),
            pltpu.VMEM((count, *signal.shape), BF),
            pltpu.SemaphoreType.DMA((2 * count + 1,)),
        ],
        compiler_params=params(7),
        cost_estimate=cost(0, 8),
    )(core, signal, spectra, *forward)


def place_kernel(core_ref, piece_ref, whole_ref, out_ref, piece, sems):
    del whole_ref
    planes = piece.shape[1]
    target = out_ref.at[pl.ds((1 - core_ref[0]) * TILE, TILE)]
    loads = [fetch(piece_ref.at[:, plane], piece.at[:, plane], sems, plane) for plane in range(planes)]
    stores = []
    for plane in range(planes):
        loads[plane].wait()
        stores.append(fetch(piece.at[:, plane], target.at[:, plane], sems, planes + plane))
    for store in stores:
        store.wait()


def place(core, piece, whole):
    return pl.pallas_call(
        place_kernel,
        in_specs=[SMEM, ANY, ANY],
        out_specs=ANY,
        out_shape=jax.ShapeDtypeStruct(whole.shape, whole.dtype),
        scratch_shapes=[pltpu.VMEM(piece.shape, piece.dtype), pltpu.SemaphoreType.DMA((2 * len(PLANES),))],
        input_output_aliases={2: 0},
        compiler_params=params(2),
        cost_estimate=cost(0, 0),
    )(core, piece, whole)


def field_kernel(got_ref, out_ref):
    out_ref[...] = got_ref[:, 0]


def field_of(got):
    return pl.pallas_call(
        field_kernel,
        in_specs=[VMEM],
        out_specs=VMEM,
        out_shape=jax.ShapeDtypeStruct((BLOCKS, TILE, N2), BF),
        compiler_params=params(2),
        cost_estimate=cost(0, 0),
    )(got)


def fold_filter(core, parts, gain_ref):
    place = lax.broadcasted_iota(jnp.int32, (HALF, HALF), 0)
    other = lax.broadcasted_iota(jnp.int32, (HALF, HALF), 1)
    pick = lambda there: (other == there).astype(F32).astype(BF)
    straight, turn, mirror = pick(place), pick((HALF - place) % HALF), pick(HALF - 1 - place)
    dims = (((1,), (1,)), ((), ()))
    row = lax.broadcasted_iota(jnp.int32, (HALF, 1), 0)
    for part in range(2):
        low = lax.dot_general(straight, parts[part][:, :HALF], dims, preferred_element_type=F32)
        high = lax.dot_general(turn, parts[part][:, HALF:], dims, preferred_element_type=F32)
        high_bf = high.astype(BF)
        keep = jnp.where((row == 0) & (core == 0), 0.0, 1.0 if part == 0 else -1.0)
        for side in range(2):
            reversed_high = jnp.dot(
                high_bf[:, (1 - side) * HALF:(2 - side) * HALF], mirror, preferred_element_type=F32
            )
            here = slice(side * HALF, (side + 1) * HALF)
            gain_ref[part, :HALF, here] = ((low[:, here] + keep * reversed_high) * SCALE).astype(BF)
        gain_ref[part, HALF:, :] = (high[:EXTRA] * SCALE).astype(BF)


def fold_kernel(core_ref, got_ref, first_ref, second_ref):
    for which, gain_ref in enumerate((first_ref, second_ref)):
        fold_filter(
            core_ref[0], [got_ref[:, 1 + 2 * which + part].reshape(N2, N2) for part in range(2)], gain_ref
        )


def fold(core, got):
    return pl.pallas_call(
        fold_kernel,
        in_specs=[SMEM, VMEM],
        out_specs=(VMEM, VMEM),
        out_shape=(jax.ShapeDtypeStruct((2, ROWS, N2), BF),) * 2,
        compiler_params=params(4),
        cost_estimate=cost(0, 0),
    )(core, got)


def outer_forward(core, own, other, forward_ref, twist_ref, sum_ref, mid_ref, twist_load):
    half = N1 // 2
    both = jnp.dot(forward_ref[:, :half], own, preferred_element_type=F32) + jnp.dot(
        forward_ref[:, half:], other, preferred_element_type=F32
    )
    sum_ref[:HALF, :N2] = both[:HALF]
    sum_ref[:HALF, N2:] = both[HALF:]
    twist_load.wait()
    top = (lax.broadcasted_iota(jnp.int32, (TILE, 1), 0) == 0) & (core == 0)
    for start in range(0, HALF, TILE):
        rows = slice(start, start + TILE)
        real, imag = sum_ref[rows, :N2], sum_ref[rows, N2:]
        cosine, sine = twist_ref[0, rows].astype(F32), twist_ref[1, rows].astype(F32)
        out_imag = imag * cosine - real * sine
        if start == 0:
            out_imag = jnp.where(top, 0.0, out_imag)
            mid_ref[HALF:, :N2] = (imag * twist_ref[0, HALF:].astype(F32)).astype(BF)
            mid_ref[HALF:, N2:] = (-imag * twist_ref[1, HALF:].astype(F32)).astype(BF)
        mid_ref[rows, :N2] = (real * cosine + imag * sine).astype(BF)
        mid_ref[rows, N2:] = out_imag.astype(BF)


def inner(mid_ref, wave_ref, sum_ref, sign):
    real = jnp.dot(mid_ref[:, :N2], wave_ref[...], preferred_element_type=F32)
    imag = jnp.dot(mid_ref[:, N2:], wave_ref[...], preferred_element_type=F32)
    sum_ref[:, :N2] = real[:, :N2] + sign * imag[:, N2:]
    sum_ref[:, N2:] = imag[:, :N2] - sign * real[:, N2:]


def times_filter(spectrum_ref, gain_ref, mid_ref):
    for start in range(0, ROWS, TILE):
        rows = slice(start, start + TILE)
        real, imag = spectrum_ref[rows, :N2], spectrum_ref[rows, N2:]
        gain_real, gain_imag = gain_ref[0, rows].astype(F32), gain_ref[1, rows].astype(F32)
        mid_ref[rows, :N2] = (gain_real * real - gain_imag * imag).astype(BF)
        mid_ref[rows, N2:] = (gain_real * imag + gain_imag * real).astype(BF)


def untwist(core, sum_ref, twist_ref, back_ref):
    top = (lax.broadcasted_iota(jnp.int32, (TILE, 1), 0) == 0) & (core == 0)
    for start in range(0, HALF, TILE):
        rows = slice(start, start + TILE)
        real, imag = sum_ref[rows, :N2], sum_ref[rows, N2:]
        cosine, sine = twist_ref[0, rows].astype(F32), twist_ref[1, rows].astype(F32)
        out_imag = imag * cosine + real * sine
        if start == 0:
            extra = (
                sum_ref[HALF:, :N2] * twist_ref[0, HALF:].astype(F32)
                - sum_ref[HALF:, N2:] * twist_ref[1, HALF:].astype(F32)
            )
            out_imag = jnp.where(top, extra, out_imag)
        back_ref[rows] = (real * cosine - imag * sine).astype(BF)
        back_ref[HALF + start:HALF + start + TILE] = out_imag.astype(BF)


def outer_backward(forward, back, out_ref, place):
    half = N1 // 2
    out_ref[...] = lax.dot_general(
        forward[:, place * half:(place + 1) * half], back[...], (((0,), (0,)), ((), ())), preferred_element_type=F32
    ).astype(BF).reshape(BLOCKS, TILE, N2)


CONV_SCRATCH = [
    pltpu.VMEM((N2, 2 * N2), BF),
    pltpu.VMEM((2, ROWS, N2), BF),
    pltpu.VMEM((ROWS, 2 * N2), BF),
    pltpu.VMEM((ROWS, 2 * N2), F32),
    pltpu.VMEM((2 * HALF, N2), BF),
    pltpu.SemaphoreType.DMA((2,)),
]


def convolve(
    core, own, other, gain, forward, wave_hbm, twist_hbm, own_ref, other_ref, wave, twist, mid, total, back, sems,
):
    twist_load = fetch(twist_hbm.at[core], twist, sems, 0)
    wave_load = fetch(wave_hbm, wave, sems, 1)
    outer_forward(core, own(), other(), forward, twist, total, mid, twist_load)
    wave_load.wait()
    inner(mid, wave, total, 1)
    times_filter(total, gain, mid)
    inner(mid, wave, total, -1)
    untwist(core, total, twist, back)
    outer_backward(forward, back, other_ref, 1)
    outer_backward(forward, back, own_ref, 0)


def first_conv_kernel(core_ref, own_ref, other_ref, *refs):
    convolve(core_ref[0], lambda: own_ref[...].reshape(N2, N2), lambda: other_ref[...].reshape(N2, N2), *refs)


def first_conv(core, own, other, *rest):
    return pl.pallas_call(
        first_conv_kernel,
        in_specs=[SMEM] + [VMEM] * 4 + [ANY] * 2,
        out_specs=(VMEM, VMEM),
        out_shape=(jax.ShapeDtypeStruct((BLOCKS, TILE, N2), BF),) * 2,
        scratch_shapes=CONV_SCRATCH,
        compiler_params=params(8),
        cost_estimate=cost(0, 0),
    )(core, own, other, *rest)


def lagged(here, before):
    row = lax.broadcasted_iota(jnp.int32, (TILE, LANES), 0)
    lane = lax.broadcasted_iota(jnp.int32, (TILE, LANES), 1)
    above = jnp.where(row == 0, pltpu.roll(before, 1, 0), pltpu.roll(here[:, N2 - LANES:], 1, 0))
    tiles = [here]
    for lag in (1, 2):
        moved = pltpu.roll(here, lag, 1)
        edge = jnp.where(lane < lag, pltpu.roll(above, lag, 1), moved[:, :LANES])
        tiles.append(jnp.concatenate([edge, moved[:, LANES:]], axis=1))
    return tiles


def gates_kernel(core_ref, seat_ref, own_taps, near_taps, field_ref, other_ref, all_own_ref, all_other_ref, own_ref):
    core = core_ref[0]
    mine = seat_ref[0] // TILE == core
    channel = seat_ref[0] % TILE
    taps = [
        [jnp.where(mine, own_taps[gate, lag, channel], near_taps[gate, lag, channel]) for lag in range(3)]
        for gate in range(2)
    ]

    def gate(index, tiles):
        return taps[index][0] * tiles[0] + taps[index][1] * tiles[1] + taps[index][2] * tiles[2]

    @pl.loop(0, BLOCKS, unroll=4)
    def _(block):
        last = (block + BLOCKS - 1) % BLOCKS
        own = field_ref[block].astype(F32)
        other = other_ref[block].astype(F32)
        ahead_of_own = other_ref[jnp.where(core == 0, last, block), :, N2 - LANES:].astype(F32)
        ahead_of_other = field_ref[jnp.where(core == 0, block, last), :, N2 - LANES:].astype(F32)
        tiles = lagged(own, ahead_of_own)
        all_own_ref[block] = gate(0, tiles).astype(BF)
        own_ref[block] = gate(1, tiles).astype(BF)
        all_other_ref[block] = gate(0, lagged(other, ahead_of_other)).astype(BF)


def gates(core, seat, taps, near_taps, own, other):
    return pl.pallas_call(
        gates_kernel,
        in_specs=[SMEM] * 4 + [VMEM, VMEM],
        out_specs=(VMEM,) * 3,
        out_shape=(jax.ShapeDtypeStruct((BLOCKS, TILE, N2), BF),) * 3,
        compiler_params=params(4),
        cost_estimate=cost(0, 0),
    )(core, seat, taps, near_taps, own, other)


def second_conv_kernel(
    core_ref, gate_own, gate_other, mine_own, mine_other, theirs_own, theirs_other, *refs,
):
    rest, middle, scratch = refs[:6], refs[6], refs[7:]

    def first_half():
        middle[0] = gate_own[...] * (mine_own[...] + theirs_other[...])
        return middle[0].reshape(N2, N2)

    def second_half():
        middle[1] = gate_other[...] * (mine_other[...] + theirs_own[...])
        return middle[1].reshape(N2, N2)

    convolve(core_ref[0], first_half, second_half, *rest, *scratch)


def second_conv(core, gate, mine, theirs, *rest):
    return pl.pallas_call(
        second_conv_kernel,
        in_specs=[SMEM] + [VMEM] * 8 + [ANY] * 2,
        out_specs=(VMEM, VMEM),
        out_shape=(jax.ShapeDtypeStruct((BLOCKS, TILE, N2), BF),) * 2,
        scratch_shapes=[pltpu.VMEM((2, BLOCKS, TILE, N2), BF)] + CONV_SCRATCH,
        compiler_params=params(9),
        cost_estimate=cost(0, 0),
    )(core, *gate, *mine, *theirs, *rest)


def last_kernel(gate_ref, keep_ref, theirs_ref, out_ref):
    last = gate_ref[...] * (keep_ref[...] + theirs_ref[...])
    out_ref[0] = last
    out_ref[1] = last


def last_gate(gate, keep, theirs):
    return pl.pallas_call(
        last_kernel,
        in_specs=[VMEM] * 3,
        out_specs=VMEM,
        out_shape=jax.ShapeDtypeStruct((2, BLOCKS, TILE, N2), BF),
        compiler_params=params(4),
        cost_estimate=cost(0, 0),
    )(gate, keep, theirs)


def mix_kernel(group_ref, own, near, far, across, values_ref, keep_ref, send_ref, wide_ref):
    channels = 2 * BLOCKS
    group = group_ref[0]
    places = [own[...], near[...], far[...], across[...]]
    rows = []
    for member in range(4):
        apart = member ^ group
        chosen = places[3]
        for index in (2, 1, 0):
            chosen = jnp.where(apart == index, places[index], chosen)
        rows.append(chosen)
    whole = jnp.concatenate(rows, axis=0)
    wanted = lax.broadcasted_iota(jnp.int32, (2 * TILE, 4 * TILE), 0)
    wanted = jnp.where(wanted < TILE, wanted + group * TILE, wanted - TILE + (group ^ 1) * TILE)
    picks = (lax.broadcasted_iota(jnp.int32, (2 * TILE, 4 * TILE), 1) == wanted).astype(F32).astype(BF)
    weights = lax.dot_general(
        picks, whole, (((1,), (1,)), ((), ())), preferred_element_type=F32
    ).astype(BF)
    for part in range(N2 // LANES):
        wide_ref[part] = values_ref[:, :, part * LANES:(part + 1) * LANES].astype(F32).reshape(
            channels * TILE, LANES
        )
    for row in range(TILE):
        piece = jnp.concatenate(
            [wide_ref[part, pl.ds(row, channels, stride=TILE), :].astype(BF) for part in range(N2 // LANES)],
            axis=1,
        )
        mixed = jnp.dot(weights, piece, preferred_element_type=F32)
        keep_ref[:, row * N2:(row + 1) * N2] = mixed[:TILE]
        send_ref[:, row * N2:(row + 1) * N2] = mixed[TILE:].astype(BF)


def mix(group, mixings, values):
    width = TILE * N2
    return pl.pallas_call(
        mix_kernel,
        in_specs=[SMEM] + [VMEM] * 5,
        out_specs=(VMEM, VMEM),
        out_shape=(jax.ShapeDtypeStruct((TILE, width), F32), jax.ShapeDtypeStruct((TILE, width), BF)),
        scratch_shapes=[pltpu.VMEM((N2 // LANES, 2 * BLOCKS * TILE, LANES), F32)],
        compiler_params=params(5),
        cost_estimate=cost(0, 0),
    )(group, *mixings, values)


def finish_kernel(core_ref, second_ref, keep_ref, theirs_ref, out_ref):
    core = core_ref[0]
    width = TILE * N2
    mine = pl.multiple_of(core * width, width)
    other = pl.multiple_of((1 - core) * width, width)
    out_ref[:, pl.ds(mine, width)] = second_ref[:, pl.ds(mine, width)].astype(F32) - keep_ref[...]
    out_ref[:, pl.ds(other, width)] = second_ref[:, pl.ds(other, width)].astype(F32) - theirs_ref[...].astype(F32)


def finish(core, second, keep, theirs):
    return pl.pallas_call(
        finish_kernel,
        in_specs=[SMEM, VMEM, VMEM, VMEM],
        out_specs=VMEM,
        out_shape=jax.ShapeDtypeStruct(second.shape, F32),
        compiler_params=params(4),
        cost_estimate=cost(0, 0),
    )(core, second, keep, theirs)


def on_device(coupled_first, coupled_second, spectra, short_taps, mixing):
    group = lax.axis_index("ch").astype(jnp.int32)[None]
    seat = lax.axis_index("seq").astype(jnp.int32)[None]
    core = group % 2
    forward, wave, twist = (in_hbm(jnp.asarray(t)) for t in tables())
    first_hbm, spectra_hbm = in_hbm(coupled_first), in_hbm(spectra)

    near_taps, near = swap(short_taps), swap(mixing)
    theirs = swap(split(False, core, first_hbm, spectra_hbm))
    buffer, forward = split(True, core, first_hbm, spectra_hbm, forward)
    buffer, near_taps, near = lax.optimization_barrier((place(core, theirs, buffer), near_taps, near))
    got = lax.all_to_all(buffer, "seq", split_axis=0, concat_axis=0, tiled=True)

    own = field_of(got)
    other = swap(own)
    gain, second_gain = fold(core, got)
    mine = first_conv(core, own, other, gain, forward, wave, twist)
    theirs = [swap(half) for half in mine]
    *gate_all, gate_own = gates(core, seat, short_taps, near_taps, own, other)
    keep, send = second_conv(core, gate_all, mine, theirs, second_gain, forward, wave, twist)
    theirs = swap(send)
    spread = last_gate(gate_own, keep, theirs)
    members = [[4 * j + 2 * high + side for high in range(2) for j in range(BLOCKS)] for side in range(2)]
    values = lax.all_to_all(
        spread.reshape(2 * BLOCKS, TILE, N2), ("seq", "ch"), split_axis=0, concat_axis=0, tiled=True,
        axis_index_groups=members,
    )
    far, across = (lax.ppermute(value, "ch", [(i, i ^ 2) for i in range(4)]) for value in (mixing, near))
    keep, send = mix(group, (mixing, near, far, across), values)
    theirs = swap(send)
    return finish(core, coupled_second, keep, theirs)


def solution(mesh):
    return jax.shard_map(
        on_device,
        mesh=mesh,
        in_specs=(
            P("ch", "seq"),
            P("ch", "seq"),
            P(None, None, "ch", "seq"),
            P(None, None, "ch"),
            P("ch", None),
        ),
        out_specs=P("ch", "seq"),
        check_vma=False,
    )
```

time: 991 us -> 98.7 us (0.10)
  local copies, waits for them, and re-layouts: 392 us -> 0.01 us
  matrix products: 312 us -> 0 us
  waiting for transfers between devices: 104 us -> 18 us
  blocking collectives: 108 us -> 41.8 us
  Pallas kernels: 0 us -> 21.4 us
  other arithmetic: 20.7 us -> 0 us
  starting transfers between devices: 32.3 us -> 17.1 us
  between operations: 14.7 us -> 0.11 us
    dot_general x17 -> x0, matrix products: 270 us -> none  [the longest x16 268 us: along_last(): jnp.einsum('...n,nk->...k', values, table, preferred_element_type=jnp.flo...]
    unnamed x75 -> x7, local copies, waits for them, and re-layouts: 153 us -> 0.01 us
    another operation x8 -> x0, local copies, waits for them, and re-layouts: 74 us -> none  [the longest x2 24.1 us: section_third(): return jnp.stack([out_real, out_imag]).astype(jnp.bfloat16)]
    all_to_all x14 -> x0, local copies, waits for them, and re-layouts: 67.2 us -> none  [the longest x2 19.7 us: conv_sequence(): lax.all_to_all(spectrum, 'seq', split_axis=3, concat_axis=2, tiled=True)]
    all_to_all x7 -> x1, blocking collectives: 108 us -> 41.8 us  [on_device(): got = lax.all_to_all(buffer, 'seq', split_axis=0, concat_axis=0, tiled=True)]
    all_to_all x5 -> x1, waiting for transfers between devices: 56.9 us -> 3.8 us  [on_device(): lax.all_to_all(spread.reshape(2 * BLOCKS, TILE, N2), ('seq', 'ch'), split...]
    reduce_scatter x1 -> x0, waiting for transfers between devices: 47.6 us -> none  [project(): lax.psum_scatter(lax.dot_general(weights, values, (((0,), (0,)), ((), ())...]
    unnamed x8 -> x0, matrix products: 41.9 us -> none
  transfers between devices with their start and end apart: 7 -> 11, of which waited for: 6 -> 7; matrix products, arithmetic and copies ran while one was open for 5% -> 0% of each run, Pallas kernels for 0% -> 6%
where the time goes in v2:
time: 98.7 us; the launch traced here: 98.3 us
  blocking collectives  41.8 us (42%)
  Pallas kernels  21.4 us (22%)
  waiting for transfers between devices  18 us (18%)
  starting transfers between devices  17.1 us (17%)
    all_to_all x1, blocking collectives, on_device(): got = lax.all_to_all(buffer, 'seq', split_axis=0, concat_axis=0, tiled=True)  41.8 us
    ppermute x2, waiting for transfers between devices, on_device(): lax.ppermute(value, 'ch', [(i, i ^ 2) for i in range(4)])  10.9 us
    ppermute x8, starting transfers between devices, swap(): lax.ppermute(value, 'ch', [(i, i ^ 1) for i in range(lax.axis_size('ch'))])  7.18 us
    all_to_all x1, starting transfers between devices, on_device(): lax.all_to_all(spread.reshape(2 * BLOCKS, TILE, N2), ('seq', 'ch'), split...  6.82 us
    pallas_call x1, Pallas kernels, second_conv(): pl.pallas_call(second_conv_kernel, in_specs=[SMEM] + [VMEM] * 8 + [ANY] *...  5.53 us
    pallas_call x2, Pallas kernels, split(): pl.pallas_call(functools.partial(split_kernel, keep), in_specs=[SMEM, ANY...  4.56 us
    pallas_call x1, Pallas kernels, first_conv(): pl.pallas_call(first_conv_kernel, in_specs=[SMEM] + [VMEM] * 4 + [ANY] *...  4.38 us
    all_to_all x1, waiting for transfers between devices, on_device(): lax.all_to_all(spread.reshape(2 * BLOCKS, TILE, N2), ('seq', 'ch'), split...  3.8 us
  transfers between devices with their start and end apart: 11, of which 7 were waited for; matrix products, arithmetic and copies ran while one was open for 0% of the time, Pallas kernels for 6%

profile of v2, /device:TPU:1, one launch (start us, length us, event | category | flops | bytes accessed | tf_op | source)
XLA Modules:
  0.0 98.3 jit_solution(993385652787120335)
XLA Ops:
  0.0 0.0 copy-start.1
  0.0 0.0 copy-start.2
  0.0 2.3 %shard_map.82 = bf16[16,5,16,512]{3,2,1,0:T(8,128)(2,1)S(1)} custom-call(s32[1]{0:T(128)S(6)} %select_n.7.core_ref, bf16[16,16384]{1,0:T(8,128)(2,1)} %signal_ref.3, bf16[2,2,16,16384]{3,2,1,0:T(8,128)(2,1)} %filter_ref.3), custom_call_target="tpu_custom_call" | custom-call | bytes 8388608 | tf_op jit(solution)/shard_map/pallas_call | solution.py:131
  2.3 1.5 %collective-permute-start = (bf16[16,5,16,512]{3,2,1,0:T(8,128)(2,1)S(1)}, bf16[16,5,16,512]{3,2,1,0:T(8,128)(2,1)S(1)}, u32[]{:S(2)}, u32[]{:S(2)}) collective-permute-start(bf16[16,5,16,512]{3,2,1,0:T(8,128)(2,1)S(1)} %shard_map.82), channel_id=1, source_target_pairs={{0,1},{1,0},{2,3},{3,2},{4,5},{5,4},{6,7},{7,6},{8,9},{9,8},{10,11... | collective-permute-start | bytes 3932168 | tf_op jit(solution)/shard_map/ppermute | solution.py:53
  3.8 0.0 copy-done.1
  3.8 0.1 collective-permute-start.2
  3.9 0.0 copy-done.2
  3.9 0.4 collective-permute-start.1
  4.3 2.3 %shard_map.83 = (bf16[32,5,16,512]{3,2,1,0:T(8,128)(2,1)S(1)}, bf16[512,1024]{1,0:T(8,128)(2,1)S(1)}) custom-call(s32[1]{0:T(128)S(6)} %select_n.7.core_ref, bf16[16,16384]{1,0:T(8,128)(2,1)} %signal_ref.3, bf16[2,2,16,16384]{3,2,1,0:T(8,128)(2,1)} %filter_ref.3, bf16[2,512,1024]{2,1,0:T(8,128)(2,1)} %constant.34.clone.refs_0_), custom_call_target="tpu_custom_call" | custom-call | bytes 8388608 | tf_op jit(solution)/shard_map/pallas_call | solution.py:131
  6.6 0.0 collective-permute-done.piece_ref
  6.6 0.3 shard_map.84
  6.9 0.0 collective-permute-done.1.near_taps
  6.9 0.0 collective-permute-done.2.near
  6.9 41.8 %all_to_all.10.got_ref = bf16[32,5,16,512]{3,2,1,0:T(8,128)(2,1)S(1)} all-to-all(bf16[32,5,16,512]{3,2,1,0:T(8,128)(2,1)S(1)} %shard_map.84), channel_id=1, replica_groups=mesh['seq'=32,'ch'=4] {'seq'}, dimensions={0} | all-to-all | bytes 5242880 | tf_op jit(solution)/shard_map/all_to_all | solution.py:499
  48.8 2.0 %collective-permute-start.5 = (bf16[32,16,512]{2,1,0:T(8,128)(2,1)S(1)}, bf16[32,16,512]{2,1,0:T(8,128)(2,1)S(1)}, u32[]{:S(2)}, u32[]{:S(2)}) collective-permute-start(bf16[32,16,512]{2,1,0:T(8,128)(2,1)S(1)} %shard_map.85.field_ref.own_ref), channel_id=1, source_target_pairs={{0,1},{1,0},{2,3},{3,2},{4,5},{5,4},{6,7},{7,6},{8,9},{9,8},{10,11... | collective-permute-start | bytes 1572872 | tf_op jit(solution)/shard_map/ppermute | solution.py:53
  50.8 1.3 %shard_map.87 = (bf16[2,272,512]{2,1,0:T(8,128)(2,1)S(1)}, bf16[2,272,512]{2,1,0:T(8,128)(2,1)S(1)}) custom-call(s32[1]{0:T(128)S(6)} %select_n.7.core_ref, bf16[32,5,16,512]{3,2,1,0:T(8,128)(2,1)S(1)} %all_to_all.10.got_ref), custom_call_target="tpu_custom_call" | custom-call | tf_op jit(solution)/shard_map/pallas_call | solution.py:217
  52.1 0.2 collective-permute-done.5.other_ref
  52.3 4.4 %shard_map.88 = (bf16[32,16,512]{2,1,0:T(8,128)(2,1)S(1)}, bf16[32,16,512]{2,1,0:T(8,128)(2,1)}) custom-call(s32[1]{0:T(128)S(6)} %select_n.7.core_ref, bf16[32,16,512]{2,1,0:T(8,128)(2,1)S(1)} %shard_map.85.field_ref.own_ref, bf16[32,16,512]{2,1,0:T(8,128)(2,1)S(1)} %collective-permute-done.5.other_ref, bf16[2,272,512]{2,1,0:T(8,128)(2,1)S(1)} %get-tuple-element.28.refs_0_, ...), custom_call_target="tpu_custom_call" | custom-call | tf_op jit(solution)/shard_map/pallas_call | solution.py:319
  56.7 0.5 collective-permute-start.6
  57.2 0.1 collective-permute-start.7
  57.3 2.1 %shard_map.86 = (bf16[32,16,512]{2,1,0:T(8,128)(2,1)S(1)}, bf16[32,16,512]{2,1,0:T(8,128)(2,1)S(1)}, bf16[32,16,512]{2,1,0:T(8,128)(2,1)S(1)}) custom-call(s32[1]{0:T(128)S(6)} %select_n.7.core_ref, s32[1]{0:T(128)} %bitcast.1.seat_ref, f32[2,3,16]{2,1,0:T(4,128)S(1)} %copy.10.own_taps, f32[2,3,16]{2,1,0:T(4,128)S(1)} %collective-permute-done.1.near_taps, ...), custom_call_target="tpu_custom_call" | custom-call | tf_op jit(solution)/shard_map/pallas_call | solution.py:368
  59.4 0.0 collective-permute-done.6.theirs_own
  59.5 0.3 collective-permute-done.7.theirs_other
  59.8 5.5 %shard_map.89 = (bf16[32,16,512]{2,1,0:T(8,128)(2,1)S(1)}, bf16[32,16,512]{2,1,0:T(8,128)(2,1)S(1)}) custom-call(s32[1]{0:T(128)S(6)} %select_n.7.core_ref, bf16[32,16,512]{2,1,0:T(8,128)(2,1)S(1)} %get-tuple-element.26.gate_own, bf16[32,16,512]{2,1,0:T(8,128)(2,1)S(1)} %get-tuple-element.27.gate_other, bf16[32,16,512]{2,1,0:T(8,128)(2,1)S(1)} %get-tuple-element.30.mine_own, ...), custom_call_target="tpu_custom_call" | custom-call | tf_op jit(solution)/shard_map/pallas_call | solution.py:395
  65.3 0.5 collective-permute-start.8
  65.8 1.5 %collective-permute-done.8.theirs_ref = bf16[32,16,512]{2,1,0:T(8,128)(2,1)S(1)} collective-permute-done((bf16[32,16,512]{2,1,0:T(8,128)(2,1)S(1)}, bf16[32,16,512]{2,1,0:T(8,128)(2,1)S(1)}, u32[]{:S(2)}, u32[]{:S(2)}) %collective-permute-start.8) | collective-permute-done | bytes 524320 | tf_op jit(solution)/shard_map/ppermute | solution.py:53
  67.3 1.1 %shard_map.90 = bf16[2,32,16,512]{3,2,1,0:T(8,128)(2,1)} custom-call(bf16[32,16,512]{2,1,0:T(8,128)(2,1)S(1)} %get-tuple-element.25.gate_ref, bf16[32,16,512]{2,1,0:T(8,128)(2,1)S(1)} %get-tuple-element.33.keep_ref, bf16[32,16,512]{2,1,0:T(8,128)(2,1)S(1)} %collective-permute-done.8.theirs_ref), custom_call_target="tpu_custom_call" | custom-call | tf_op jit(solution)/shard_map/pallas_call | solution.py:413
  68.4 0.0 copy-start
  68.4 6.8 %all-to-all-start.1 = ((bf16[64,16,512]{2,1,0:T(8,128)(2,1)}), bf16[64,16,512]{2,1,0:T(8,128)(2,1)S(1)}, u32[]{:S(2)}, u32[]{:S(2)}) async-start(bf16[64,16,512]{2,1,0:T(8,128)(2,1)} %bitcast.2), calls=%async_computation.1 | async-start | bytes 2097152 | tf_op jit(solution)/shard_map/all_to_all | solution.py:511
  75.2 2.7 %collective-permute-start.3 = (bf16[16,64]{1,0:T(8,128)(2,1)S(1)}, bf16[16,64]{1,0:T(8,128)(2,1)S(1)}, u32[]{:S(2)}, u32[]{:S(2)}) collective-permute-start(bf16[16,64]{1,0:T(8,128)(2,1)S(1)} %copy-done.1), channel_id=1, source_target_pairs={{0,2},{1,3},{2,0},{3,1},{4,6},{5,7},{6,4},{7,5},{8,10},{9,11},{10,... | collective-permute-start | bytes 6152 | tf_op jit(solution)/shard_map/ppermute | solution.py:515
  77.9 0.4 collective-permute-start.4
  78.3 10.8 %collective-permute-done.3.far = bf16[16,64]{1,0:T(8,128)(2,1)S(1)} collective-permute-done((bf16[16,64]{1,0:T(8,128)(2,1)S(1)}, bf16[16,64]{1,0:T(8,128)(2,1)S(1)}, u32[]{:S(2)}, u32[]{:S(2)}) %collective-permute-start.3) | collective-permute-done | bytes 2080 | tf_op jit(solution)/shard_map/ppermute | solution.py:515
  89.1 0.1 collective-permute-done.4.across
  89.2 3.8 %all-to-all-done.1.values_ref = bf16[64,16,512]{2,1,0:T(8,128)(2,1)S(1)} async-done(((bf16[64,16,512]{2,1,0:T(8,128)(2,1)}), bf16[64,16,512]{2,1,0:T(8,128)(2,1)S(1)}, u32[]{:S(2)}, u32[]{:S(2)}) %all-to-all-start.1) | async-done | bytes 1048608 | tf_op jit(solution)/shard_map/all_to_all | solution.py:511
  93.0 1.0 shard_map.91
  94.0 2.1 %collective-permute-start.9 = (bf16[16,8192]{1,0:T(8,128)(2,1)S(1)}, bf16[16,8192]{1,0:T(8,128)(2,1)S(1)}, u32[]{:S(2)}, u32[]{:S(2)}) collective-permute-start(bf16[16,8192]{1,0:T(8,128)(2,1)S(1)} %get-tuple-element.36), channel_id=1, source_target_pairs={{0,1},{1,0},{2,3},{3,2},{4,5},{5,4},{6,7},{7,6},{8,9},{9,8},{10,11... | collective-permute-start | bytes 786440 | tf_op jit(solution)/shard_map/ppermute | solution.py:53
  96.1 1.2 %collective-permute-done.9.theirs_ref = bf16[16,8192]{1,0:T(8,128)(2,1)S(1)} collective-permute-done((bf16[16,8192]{1,0:T(8,128)(2,1)S(1)}, bf16[16,8192]{1,0:T(8,128)(2,1)S(1)}, u32[]{:S(2)}, u32[]{:S(2)}) %collective-permute-start.9) | collective-permute-done | bytes 262176 | tf_op jit(solution)/shard_map/ppermute | solution.py:53
  97.2 0.0 copy-done
  97.2 1.1 %shard_map.92 = f32[16,16384]{1,0:T(8,128)} custom-call(s32[1]{0:T(128)S(6)} %select_n.7.core_ref, bf16[16,16384]{1,0:T(8,128)(2,1)S(1)} %copy-done, f32[16,8192]{1,0:T(8,128)S(1)} %get-tuple-element.35.keep_ref, bf16[16,8192]{1,0:T(8,128)(2,1)S(1)} %collective-permute-done.9.theirs_ref), custom_call_target="tpu_custom_call" | custom-call | tf_op jit(solution)/shard_map/pallas_call | solution.py:478
  (2 shorter events, 0.0 us)
Async XLA Ops:
  0.0 3.8 %copy-start.1 = (bf16[16,64]{1,0:T(8,128)(2,1)S(1)}, bf16[16,64]{1,0:T(8,128)(2,1)}, u32[]{:S(2)}) copy-start(bf16[16,64]{1,0:T(8,128)(2,1)} %own.1) | copy-start | bytes 6148
  0.0 3.9 %copy-start.2 = (f32[2,3,16]{2,0,1:T(2,128)S(1)}, f32[2,3,16]{2,0,1:T(2,128)}, u32[]{:S(2)}) copy-start(f32[2,3,16]{2,0,1:T(2,128)} %param.11) | copy-start | bytes 1156
  2.3 4.3 %collective-permute-start = (bf16[16,5,16,512]{3,2,1,0:T(8,128)(2,1)S(1)}, bf16[16,5,16,512]{3,2,1,0:T(8,128)(2,1)S(1)}, u32[]{:S(2)}, u32[]{:S(2)}) collective-permute-start(bf16[16,5,16,512]{3,2,1,0:T(8,128)(2,1)S(1)} %shard_map.82), channel_id=1, source_target_pairs={{0,1},{1,0},{2,3},{3,2},{4,5},{5,4},{6,7},{7,6},{8,9},{9,8},{10,11... | collective-permute-start | bytes 3932168 | tf_op jit(solution)/shard_map/ppermute | solution.py:53
  3.8 3.1 %collective-permute-start.2 = (bf16[16,64]{1,0:T(8,128)(2,1)S(1)}, bf16[16,64]{1,0:T(8,128)(2,1)S(1)}, u32[]{:S(2)}, u32[]{:S(2)}) collective-permute-start(bf16[16,64]{1,0:T(8,128)(2,1)S(1)} %copy-done.1), channel_id=1, source_target_pairs={{0,1},{1,0},{2,3},{3,2},{4,5},{5,4},{6,7},{7,6},{8,9},{9,8},{10,11... | collective-permute-start | bytes 6152 | tf_op jit(solution)/shard_map/ppermute | solution.py:53
  3.9 3.0 %collective-permute-start.1 = (f32[2,3,16]{2,1,0:T(4,128)S(1)}, f32[2,3,16]{2,1,0:T(4,128)S(1)}, u32[]{:S(2)}, u32[]{:S(2)}) collective-permute-start(f32[2,3,16]{2,1,0:T(4,128)S(1)} %copy.10.own_taps), channel_id=1, source_target_pairs={{0,1},{1,0},{2,3},{3,2},{4,5},{5,4},{6,7},{7,6},{8,9},{9,8},{10,11... | collective-permute-start | bytes 1160 | tf_op jit(solution)/shard_map/ppermute | solution.py:53
  48.8 3.6 %collective-permute-start.5 = (bf16[32,16,512]{2,1,0:T(8,128)(2,1)S(1)}, bf16[32,16,512]{2,1,0:T(8,128)(2,1)S(1)}, u32[]{:S(2)}, u32[]{:S(2)}) collective-permute-start(bf16[32,16,512]{2,1,0:T(8,128)(2,1)S(1)} %shard_map.85.field_ref.own_ref), channel_id=1, source_target_pairs={{0,1},{1,0},{2,3},{3,2},{4,5},{5,4},{6,7},{7,6},{8,9},{9,8},{10,11... | collective-permute-start | bytes 1572872 | tf_op jit(solution)/shard_map/ppermute | solution.py:53
  56.7 2.7 %collective-permute-start.6 = (bf16[32,16,512]{2,1,0:T(8,128)(2,1)S(1)}, bf16[32,16,512]{2,1,0:T(8,128)(2,1)}, u32[]{:S(2)}, u32[]{:S(2)}) collective-permute-start(bf16[32,16,512]{2,1,0:T(8,128)(2,1)S(1)} %get-tuple-element.30.mine_own), channel_id=1, source_target_pairs={{0,1},{1,0},{2,3},{3,2},{4,5},{5,4},{6,7},{7,6},{8,9},{9,8},{10,11... | collective-permute-start | bytes 1572872 | tf_op jit(solution)/shard_map/ppermute | solution.py:53
  57.2 2.6 %collective-permute-start.7 = (bf16[32,16,512]{2,1,0:T(8,128)(2,1)}, bf16[32,16,512]{2,1,0:T(8,128)(2,1)}, u32[]{:S(2)}, u32[]{:S(2)}) collective-permute-start(bf16[32,16,512]{2,1,0:T(8,128)(2,1)} %get-tuple-element.31.mine_other), channel_id=1, source_target_pairs={{0,1},{1,0},{2,3},{3,2},{4,5},{5,4},{6,7},{7,6},{8,9},{9,8},{10,11... | collective-permute-start | bytes 1572872 | tf_op jit(solution)/shard_map/ppermute | solution.py:53
  65.3 2.0 %collective-permute-start.8 = (bf16[32,16,512]{2,1,0:T(8,128)(2,1)S(1)}, bf16[32,16,512]{2,1,0:T(8,128)(2,1)S(1)}, u32[]{:S(2)}, u32[]{:S(2)}) collective-permute-start(bf16[32,16,512]{2,1,0:T(8,128)(2,1)S(1)} %get-tuple-element.34), channel_id=1, source_target_pairs={{0,1},{1,0},{2,3},{3,2},{4,5},{5,4},{6,7},{7,6},{8,9},{9,8},{10,11... | collective-permute-start | bytes 1572872 | tf_op jit(solution)/shard_map/ppermute | solution.py:53
  68.4 28.9 %copy-start = (bf16[16,16384]{1,0:T(8,128)(2,1)S(1)}, bf16[16,16384]{1,0:T(8,128)(2,1)}, u32[]{:S(2)}) copy-start(bf16[16,16384]{1,0:T(8,128)(2,1)} %second_ref.1) | copy-start | bytes 1572868
  68.4 24.6 %all-to-all-start.1 = ((bf16[64,16,512]{2,1,0:T(8,128)(2,1)}), bf16[64,16,512]{2,1,0:T(8,128)(2,1)S(1)}, u32[]{:S(2)}, u32[]{:S(2)}) async-start(bf16[64,16,512]{2,1,0:T(8,128)(2,1)} %bitcast.2), calls=%async_computation.1 | async-start | bytes 2097152 | tf_op jit(solution)/shard_map/all_to_all | solution.py:511
  75.2 13.9 %collective-permute-start.3 = (bf16[16,64]{1,0:T(8,128)(2,1)S(1)}, bf16[16,64]{1,0:T(8,128)(2,1)S(1)}, u32[]{:S(2)}, u32[]{:S(2)}) collective-permute-start(bf16[16,64]{1,0:T(8,128)(2,1)S(1)} %copy-done.1), channel_id=1, source_target_pairs={{0,2},{1,3},{2,0},{3,1},{4,6},{5,7},{6,4},{7,5},{8,10},{9,11},{10,... | collective-permute-start | bytes 6152 | tf_op jit(solution)/shard_map/ppermute | solution.py:515
  77.9 11.3 %collective-permute-start.4 = (bf16[16,64]{1,0:T(8,128)(2,1)S(1)}, bf16[16,64]{1,0:T(8,128)(2,1)S(1)}, u32[]{:S(2)}, u32[]{:S(2)}) collective-permute-start(bf16[16,64]{1,0:T(8,128)(2,1)S(1)} %collective-permute-done.2.near), channel_id=1, source_target_pairs={{0,2},{1,3},{2,0},{3,1},{4,6},{5,7},{6,4},{7,5},{8,10},{9,11},{10,... | collective-permute-start | bytes 6152 | tf_op jit(solution)/shard_map/ppermute | solution.py:515
  94.0 3.3 %collective-permute-start.9 = (bf16[16,8192]{1,0:T(8,128)(2,1)S(1)}, bf16[16,8192]{1,0:T(8,128)(2,1)S(1)}, u32[]{:S(2)}, u32[]{:S(2)}) collective-permute-start(bf16[16,8192]{1,0:T(8,128)(2,1)S(1)} %get-tuple-element.36), channel_id=1, source_target_pairs={{0,1},{1,0},{2,3},{3,2},{4,5},{5,4},{6,7},{7,6},{8,9},{9,8},{10,11... | collective-permute-start | bytes 786440 | tf_op jit(solution)/shard_map/ppermute | solution.py:53

commit v3 on v2

--- a/solution.py
+++ b/solution.py
@@ -27,12 +27,13 @@
 
 
 def tables():
-    rows = np.arange(N1).reshape(BLOCKS, 2, TILE).transpose(1, 0, 2).reshape(2, -1)
+    rows = np.arange(N1 // 2).reshape(BLOCKS // 2, 2, TILE).transpose(1, 0, 2).reshape(2, -1)
     order = np.stack([rows.reshape(-1), rows[::-1].reshape(-1)])
-    freq = np.arange(HALF)[None, :] + HALF * np.arange(2)[:, None]
+    freq = np.concatenate([np.arange(0, HALF, 2), np.arange(1, HALF, 2)])[None, :] + HALF * np.arange(2)[:, None]
     angle = (freq[:, :, None] * order[:, None, :] % N1) * (2.0 * np.pi / N1)
-    forward = np.concatenate([np.cos(angle), -np.sin(angle)], axis=1)
-    forward[0, HALF] = 1.0 - 2.0 * (order[0] % 2)
+    forward = np.stack([np.cos(angle), -np.sin(angle)], axis=1)
+    forward[0, 1, 0] = 1.0 - 2.0 * (order[0] % 2)
+    forward = forward.reshape(2, 2, 2, HALF // 2, N1 // 2).transpose(0, 2, 1, 3, 4).reshape(2, 2 * HALF, N1 // 2)
     inner = np.arange(N2)
     angle = (inner[:, None] * inner[None, :] % N2) * (2.0 * np.pi / N2)
     cosine, sine = np.cos(angle), np.sin(angle)
@@ -96,18 +97,18 @@
 
 def split_kernel(keep, core_ref, signal_ref, filter_ref, *refs):
     if keep:
-        forward_hbm, out_ref, forward_ref, wide_ref, out_vmem, in_vmem, sems = refs
+        forward_hbm, out_ref, forward_ref, wide_ref, in_vmem, sems = refs
     else:
-        out_ref, wide_ref, out_vmem, in_vmem, sems = refs
+        out_ref, wide_ref, in_vmem, sems = refs
     core = core_ref[0]
     half = core if keep else 1 - core
-    target = out_ref.at[pl.ds(core * TILE, TILE)] if keep else out_ref
+    target = pl.ds(core * TILE, TILE) if keep else slice(None)
     here = pl.ds(pl.multiple_of(half * (TILE * N2), TILE * N2), TILE * N2)
     count = len(PLANES)
     loads = [fetch(signal_ref.at[:, here], in_vmem.at[0, :, :TILE * N2], sems, 0)]
     for plane in range(1, count):
         loads.append(fetch(filter_ref.at[PLANES[plane]], in_vmem.at[plane], sems, plane))
-    stores = [fetch(forward_hbm.at[core], forward_ref, sems, 2 * count)] if keep else []
+    table = fetch(forward_hbm.at[core], forward_ref, sems, count) if keep else None
     for plane in range(count):
         loads[plane].wait()
         wide = wide_ref.at[plane % 2]
@@ -115,14 +116,11 @@
             split_field(in_vmem.at[plane], wide)
         else:
             split_filter(half, in_vmem.at[plane], wide)
-        for channel in range(TILE):
-            for lanes in range(N2 // LANES):
-                out_vmem[channel, plane, :, lanes * LANES:(lanes + 1) * LANES] = wide[
-                    lanes, pl.ds(channel, TILE, stride=TILE), :
-                ].astype(BF)
-        stores.append(fetch(out_vmem.at[:, plane], target.at[:, plane], sems, count + plane))
-    for store in stores:
-        store.wait()
+        for lanes in range(N2 // LANES):
+            turned = jnp.swapaxes(wide[lanes].reshape(TILE, TILE, LANES), 0, 1)
+            out_ref[target, plane, :, lanes * LANES:(lanes + 1) * LANES] = turned.astype(BF)
+    if keep:
+        table.wait()
 
 
 def split(keep, core, signal, spectra, *forward):
@@ -131,13 +129,12 @@
     return pl.pallas_call(
         functools.partial(split_kernel, keep),
         in_specs=[SMEM, ANY, ANY] + [ANY] * len(forward),
-        out_specs=(ANY, VMEM) if keep else ANY,
-        out_shape=(shape, jax.ShapeDtypeStruct((2 * HALF, N1), BF)) if keep else shape,
+        out_specs=(VMEM, VMEM) if keep else VMEM,
+        out_shape=(shape, jax.ShapeDtypeStruct((2 * HALF, N1 // 2), BF)) if keep else shape,
         scratch_shapes=[
             pltpu.VMEM((2, N2 // LANES, TILE * TILE, LANES), F32),
-            pltpu.VMEM((TILE, count, TILE, N2), BF),
             pltpu.VMEM((count, *signal.shape), BF),
-            pltpu.SemaphoreType.DMA((2 * count + 1,)),
+            pltpu.SemaphoreType.DMA((count + 1,)),
         ],
         compiler_params=params(7),
         cost_estimate=cost(0, 8),
@@ -189,7 +186,8 @@
     place = lax.broadcasted_iota(jnp.int32, (HALF, HALF), 0)
     other = lax.broadcasted_iota(jnp.int32, (HALF, HALF), 1)
     pick = lambda there: (other == there).astype(F32).astype(BF)
-    straight, turn, mirror = pick(place), pick((HALF - place) % HALF), pick(HALF - 1 - place)
+    order = 2 * place % HALF + place // (HALF // 2)
+    straight, turn, mirror = pick(order), pick((HALF - order) % HALF), pick(HALF - 1 - place)
     dims = (((1,), (1,)), ((), ()))
     row = lax.broadcasted_iota(jnp.int32, (HALF, 1), 0)
     for part in range(2):
@@ -206,32 +204,43 @@
         gain_ref[part, HALF:, :] = (high[:EXTRA] * SCALE).astype(BF)
 
 
-def fold_kernel(core_ref, got_ref, first_ref, second_ref):
+def fold_kernel(core_ref, got_ref, wave_hbm, twist_hbm, first_ref, second_ref, wave_ref, twist_ref, sems):
+    core = core_ref[0]
+    loads = [fetch(twist_hbm.at[core], twist_ref, sems, 0), fetch(wave_hbm, wave_ref, sems, 1)]
     for which, gain_ref in enumerate((first_ref, second_ref)):
-        fold_filter(
-            core_ref[0], [got_ref[:, 1 + 2 * which + part].reshape(N2, N2) for part in range(2)], gain_ref
+        fold_filter(core, [got_ref[:, 1 + 2 * which + part].reshape(N2, N2) for part in range(2)], gain_ref)
+    for load in loads:
+        load.wait()
+
+
+def fold(core, got, wave, twist):
+    gain = jax.ShapeDtypeStruct((2, ROWS, N2), BF)
+    return pl.pallas_call(
+        fold_kernel,
+        in_specs=[SMEM, VMEM, ANY, ANY],
+        out_specs=(VMEM,) * 4,
+        out_shape=(gain, gain, jax.ShapeDtypeStruct(wave.shape, BF), gain),
+        scratch_shapes=[pltpu.SemaphoreType.DMA((2,))],
+        compiler_params=params(4),
+        cost_estimate=cost(0, 0),
+    )(core, got, wave, twist)
+
+
+def fold_time(value, fold_ref, place):
+    half = BLOCKS // 2
+    fold_ref[0, place] = value[:half] + value[half:]
+    fold_ref[1, place] = value[:half] - value[half:]
+
+
+def outer_forward(core, fold_ref, forward_ref, twist_ref, sum_ref, mid_ref):
+    half = HALF // 2
+    for parity in range(2):
+        both = jnp.dot(
+            forward_ref[parity * HALF:(parity + 1) * HALF], fold_ref[parity].reshape(N2, N2),
+            preferred_element_type=F32,
         )
-
-
-def fold(core, got):
-    return pl.pallas_call(
-        fold_kernel,
-        in_specs=[SMEM, VMEM],
-        out_specs=(VMEM, VMEM),
-        out_shape=(jax.ShapeDtypeStruct((2, ROWS, N2), BF),) * 2,
-        compiler_params=params(4),
-        cost_estimate=cost(0, 0),
-    )(core, got)
-
-
-def outer_forward(core, own, other, forward_ref, twist_ref, sum_ref, mid_ref, twist_load):
-    half = N1 // 2
-    both = jnp.dot(forward_ref[:, :half], own, preferred_element_type=F32) + jnp.dot(
-        forward_ref[:, half:], other, preferred_element_type=F32
-    )
-    sum_ref[:HALF, :N2] = both[:HALF]
-    sum_ref[:HALF, N2:] = both[HALF:]
-    twist_load.wait()
+        sum_ref[parity * half:(parity + 1) * half, :N2] = both[:half]
+        sum_ref[parity * half:(parity + 1) * half, N2:] = both[half:]
     top = (lax.broadcasted_iota(jnp.int32, (TILE, 1), 0) == 0) & (core == 0)
     for start in range(0, HALF, TILE):
         rows = slice(start, start + TILE)
@@ -263,6 +272,7 @@
 
 
 def untwist(core, sum_ref, twist_ref, back_ref):
+    half = HALF // 2
     top = (lax.broadcasted_iota(jnp.int32, (TILE, 1), 0) == 0) & (core == 0)
     for start in range(0, HALF, TILE):
         rows = slice(start, start + TILE)
@@ -275,34 +285,34 @@
                 - sum_ref[HALF:, N2:] * twist_ref[1, HALF:].astype(F32)
             )
             out_imag = jnp.where(top, extra, out_imag)
-        back_ref[rows] = (real * cosine - imag * sine).astype(BF)
-        back_ref[HALF + start:HALF + start + TILE] = out_imag.astype(BF)
+        first = start + start // half * half
+        back_ref[first:first + TILE] = (real * cosine - imag * sine).astype(BF)
+        back_ref[first + half:first + half + TILE] = out_imag.astype(BF)
 
 
 def outer_backward(forward, back, out_ref, place):
-    half = N1 // 2
-    out_ref[...] = lax.dot_general(
-        forward[:, place * half:(place + 1) * half], back[...], (((0,), (0,)), ((), ())), preferred_element_type=F32
-    ).astype(BF).reshape(BLOCKS, TILE, N2)
+    half, cols = BLOCKS // 2, slice(place * HALF, (place + 1) * HALF)
+    even, odd = (
+        lax.dot_general(
+            forward[rows, cols], back[rows], (((0,), (0,)), ((), ())), preferred_element_type=F32
+        ).reshape(half, TILE, N2)
+        for rows in (slice(0, HALF), slice(HALF, 2 * HALF))
+    )
+    out_ref[:half] = (even + odd).astype(BF)
+    out_ref[half:] = (even - odd).astype(BF)
 
 
 CONV_SCRATCH = [
-    pltpu.VMEM((N2, 2 * N2), BF),
-    pltpu.VMEM((2, ROWS, N2), BF),
+    pltpu.VMEM((2, 2, BLOCKS // 2, TILE, N2), BF),
     pltpu.VMEM((ROWS, 2 * N2), BF),
     pltpu.VMEM((ROWS, 2 * N2), F32),
     pltpu.VMEM((2 * HALF, N2), BF),
-    pltpu.SemaphoreType.DMA((2,)),
 ]
 
 
-def convolve(
-    core, own, other, gain, forward, wave_hbm, twist_hbm, own_ref, other_ref, wave, twist, mid, total, back, sems,
-):
-    twist_load = fetch(twist_hbm.at[core], twist, sems, 0)
-    wave_load = fetch(wave_hbm, wave, sems, 1)
-    outer_forward(core, own(), other(), forward, twist, total, mid, twist_load)
-    wave_load.wait()
+def convolve(core, gain, forward, wave, twist, own_ref, other_ref, folded, mid, total, back, ready=lambda: None):
+    outer_forward(core, folded, forward, twist, total, mid)
+    ready()
     inner(mid, wave, total, 1)
     times_filter(total, gain, mid)
     inner(mid, wave, total, -1)
@@ -311,18 +321,20 @@
     outer_backward(forward, back, own_ref, 0)
 
 
-def first_conv_kernel(core_ref, own_ref, other_ref, *refs):
-    convolve(core_ref[0], lambda: own_ref[...].reshape(N2, N2), lambda: other_ref[...].reshape(N2, N2), *refs)
+def first_conv_kernel(core_ref, own, other, gain, forward, wave, twist, own_ref, other_ref, folded, *scratch):
+    fold_time(own, folded, 0)
+    fold_time(other, folded, 1)
+    convolve(core_ref[0], gain, forward, wave, twist, own_ref, other_ref, folded, *scratch)
 
 
 def first_conv(core, own, other, *rest):
     return pl.pallas_call(
         first_conv_kernel,
-        in_specs=[SMEM] + [VMEM] * 4 + [ANY] * 2,
+        in_specs=[SMEM] + [VMEM] * 6,
         out_specs=(VMEM, VMEM),
         out_shape=(jax.ShapeDtypeStruct((BLOCKS, TILE, N2), BF),) * 2,
         scratch_shapes=CONV_SCRATCH,
-        compiler_params=params(8),
+        compiler_params=params(6),
         cost_estimate=cost(0, 0),
     )(core, own, other, *rest)
 
@@ -339,68 +351,70 @@
     return tiles
 
 
-def gates_kernel(core_ref, seat_ref, own_taps, near_taps, field_ref, other_ref, all_own_ref, all_other_ref, own_ref):
-    core = core_ref[0]
+def taps_of(index, core, seat_ref, own_taps, near_taps):
     mine = seat_ref[0] // TILE == core
     channel = seat_ref[0] % TILE
-    taps = [
-        [jnp.where(mine, own_taps[gate, lag, channel], near_taps[gate, lag, channel]) for lag in range(3)]
-        for gate in range(2)
-    ]
-
-    def gate(index, tiles):
-        return taps[index][0] * tiles[0] + taps[index][1] * tiles[1] + taps[index][2] * tiles[2]
-
-    @pl.loop(0, BLOCKS, unroll=4)
+    return [jnp.where(mine, own_taps[index, lag, channel], near_taps[index, lag, channel]) for lag in range(3)]
+
+
+def gate(taps, tiles):
+    return (taps[0] * tiles[0] + taps[1] * tiles[1] + taps[2] * tiles[2]).astype(BF)
+
+
+def gates_kernel(index, core_ref, seat_ref, own_taps, near_taps, own, other, *outs):
+    core = core_ref[0]
+    taps = taps_of(index, core, seat_ref, own_taps, near_taps)
+
+    @pl.loop(0, BLOCKS, unroll=8)
     def _(block):
         last = (block + BLOCKS - 1) % BLOCKS
-        own = field_ref[block].astype(F32)
-        other = other_ref[block].astype(F32)
-        ahead_of_own = other_ref[jnp.where(core == 0, last, block), :, N2 - LANES:].astype(F32)
-        ahead_of_other = field_ref[jnp.where(core == 0, block, last), :, N2 - LANES:].astype(F32)
-        tiles = lagged(own, ahead_of_own)
-        all_own_ref[block] = gate(0, tiles).astype(BF)
-        own_ref[block] = gate(1, tiles).astype(BF)
-        all_other_ref[block] = gate(0, lagged(other, ahead_of_other)).astype(BF)
-
-
-def gates(core, seat, taps, near_taps, own, other):
-    return pl.pallas_call(
-        gates_kernel,
+        ahead = other[jnp.where(core == 0, last, block), :, N2 - LANES:].astype(F32)
+        outs[0][block] = gate(taps, lagged(own[block].astype(F32), ahead))
+        if len(outs) > 1:
+            ahead = own[jnp.where(core == 0, block, last), :, N2 - LANES:].astype(F32)
+            outs[1][block] = gate(taps, lagged(other[block].astype(F32), ahead))
+
+
+def gates(index, count, core, seat, taps, near_taps, own, other):
+    return pl.pallas_call(
+        functools.partial(gates_kernel, index),
         in_specs=[SMEM] * 4 + [VMEM, VMEM],
-        out_specs=(VMEM,) * 3,
-        out_shape=(jax.ShapeDtypeStruct((BLOCKS, TILE, N2), BF),) * 3,
+        out_specs=(VMEM,) * count,
+        out_shape=(jax.ShapeDtypeStruct((BLOCKS, TILE, N2), BF),) * count,
         compiler_params=params(4),
         cost_estimate=cost(0, 0),
     )(core, seat, taps, near_taps, own, other)
 
 
 def second_conv_kernel(
-    core_ref, gate_own, gate_other, mine_own, mine_other, theirs_own, theirs_other, *refs,
+    core_ref, gate_own, gate_other, mine_own, mine_other, gain, forward, theirs_own, theirs_other, wave_hbm, twist_hbm,
+    own_ref, other_ref, theirs, wave, twist, sems, folded, *scratch,
 ):
-    rest, middle, scratch = refs[:6], refs[6], refs[7:]
-
-    def first_half():
-        middle[0] = gate_own[...] * (mine_own[...] + theirs_other[...])
-        return middle[0].reshape(N2, N2)
-
-    def second_half():
-        middle[1] = gate_other[...] * (mine_other[...] + theirs_own[...])
-        return middle[1].reshape(N2, N2)
-
-    convolve(core_ref[0], first_half, second_half, *rest, *scratch)
-
-
-def second_conv(core, gate, mine, theirs, *rest):
+    core = core_ref[0]
+    loads = [fetch(theirs_other, theirs.at[0], sems, 2), fetch(theirs_own, theirs.at[1], sems, 3)]
+    twist_load = fetch(twist_hbm.at[core], twist, sems, 0)
+    wave_load = fetch(wave_hbm, wave, sems, 1)
+    loads[0].wait()
+    fold_time(gate_own[...] * (mine_own[...] + theirs[0]), folded, 0)
+    loads[1].wait()
+    fold_time(gate_other[...] * (mine_other[...] + theirs[1]), folded, 1)
+    twist_load.wait()
+    convolve(core, gain, forward, wave, twist, own_ref, other_ref, folded, *scratch, ready=wave_load.wait)
+
+
+def second_conv(core, gate, mine, theirs, gain, forward, wave, twist):
     return pl.pallas_call(
         second_conv_kernel,
-        in_specs=[SMEM] + [VMEM] * 8 + [ANY] * 2,
+        in_specs=[SMEM] + [VMEM] * 6 + [ANY] * 4,
         out_specs=(VMEM, VMEM),
         out_shape=(jax.ShapeDtypeStruct((BLOCKS, TILE, N2), BF),) * 2,
-        scratch_shapes=[pltpu.VMEM((2, BLOCKS, TILE, N2), BF)] + CONV_SCRATCH,
-        compiler_params=params(9),
-        cost_estimate=cost(0, 0),
-    )(core, *gate, *mine, *theirs, *rest)
+        scratch_shapes=[
+            pltpu.VMEM((2, BLOCKS, TILE, N2), BF), pltpu.VMEM((N2, 2 * N2), BF), pltpu.VMEM((2, ROWS, N2), BF),
+            pltpu.SemaphoreType.DMA((4,)),
+        ] + CONV_SCRATCH,
+        compiler_params=params(10),
+        cost_estimate=cost(0, 0),
+    )(core, *gate, *mine, gain, forward, *theirs, wave, twist)
 
 
 def last_kernel(gate_ref, keep_ref, theirs_ref, out_ref):
@@ -439,14 +453,12 @@
         picks, whole, (((1,), (1,)), ((), ())), preferred_element_type=F32
     ).astype(BF)
     for part in range(N2 // LANES):
-        wide_ref[part] = values_ref[:, :, part * LANES:(part + 1) * LANES].astype(F32).reshape(
-            channels * TILE, LANES
-        )
+        here = slice(part * LANES, (part + 1) * LANES)
+        for start in range(0, channels, TILE):
+            piece = values_ref[start:start + TILE, :, here].astype(F32)
+            wide_ref[:, start:start + TILE, here] = jnp.swapaxes(piece, 0, 1).astype(BF)
     for row in range(TILE):
-        piece = jnp.concatenate(
-            [wide_ref[part, pl.ds(row, channels, stride=TILE), :].astype(BF) for part in range(N2 // LANES)],
-            axis=1,
-        )
+        piece = wide_ref[row]
         mixed = jnp.dot(weights, piece, preferred_element_type=F32)
         keep_ref[:, row * N2:(row + 1) * N2] = mixed[:TILE]
         send_ref[:, row * N2:(row + 1) * N2] = mixed[TILE:].astype(BF)
@@ -459,30 +471,33 @@
         in_specs=[SMEM] + [VMEM] * 5,
         out_specs=(VMEM, VMEM),
         out_shape=(jax.ShapeDtypeStruct((TILE, width), F32), jax.ShapeDtypeStruct((TILE, width), BF)),
-        scratch_shapes=[pltpu.VMEM((N2 // LANES, 2 * BLOCKS * TILE, LANES), F32)],
+        scratch_shapes=[pltpu.VMEM((TILE, 2 * BLOCKS, N2), BF)],
         compiler_params=params(5),
         cost_estimate=cost(0, 0),
     )(group, *mixings, values)
 
 
-def finish_kernel(core_ref, second_ref, keep_ref, theirs_ref, out_ref):
-    core = core_ref[0]
+def finish_kernel(other, core_ref, second_ref, update_ref, *refs):
+    out_ref, second, result, sems = refs[-4:]
     width = TILE * N2
-    mine = pl.multiple_of(core * width, width)
-    other = pl.multiple_of((1 - core) * width, width)
-    out_ref[:, pl.ds(mine, width)] = second_ref[:, pl.ds(mine, width)].astype(F32) - keep_ref[...]
-    out_ref[:, pl.ds(other, width)] = second_ref[:, pl.ds(other, width)].astype(F32) - theirs_ref[...].astype(F32)
-
-
-def finish(core, second, keep, theirs):
-    return pl.pallas_call(
-        finish_kernel,
-        in_specs=[SMEM, VMEM, VMEM, VMEM],
-        out_specs=VMEM,
+    here = pl.ds(pl.multiple_of((1 - core_ref[0] if other else core_ref[0]) * width, width), width)
+    fetch(second_ref.at[:, here], second, sems, 0).wait()
+    result[...] = second[...].astype(F32) - update_ref[...].astype(F32)
+    fetch(result, out_ref.at[:, here], sems, 1).wait()
+
+
+def finish(other, core, second, update, *out):
+    width = TILE * N2
+    return pl.pallas_call(
+        functools.partial(finish_kernel, other),
+        in_specs=[SMEM, ANY, VMEM] + [ANY] * len(out),
+        out_specs=ANY,
         out_shape=jax.ShapeDtypeStruct(second.shape, F32),
+        scratch_shapes=[pltpu.VMEM((TILE, width), BF), pltpu.VMEM((TILE, width), F32), pltpu.SemaphoreType.DMA((2,))],
+        input_output_aliases={3: 0} if other else {},
         compiler_params=params(4),
         cost_estimate=cost(0, 0),
-    )(core, second, keep, theirs)
+    )(core, second, update, *out)
 
 
 def on_device(coupled_first, coupled_second, spectra, short_taps, mixing):
@@ -500,12 +515,13 @@
 
     own = field_of(got)
     other = swap(own)
-    gain, second_gain = fold(core, got)
-    mine = first_conv(core, own, other, gain, forward, wave, twist)
+    gain, second_gain, wave_now, twist_now = fold(core, got, wave, twist)
+    mine = first_conv(core, own, other, gain, forward, wave_now, twist_now)
     theirs = [swap(half) for half in mine]
-    *gate_all, gate_own = gates(core, seat, short_taps, near_taps, own, other)
+    gate_all = gates(0, 2, core, seat, short_taps, near_taps, own, other)
     keep, send = second_conv(core, gate_all, mine, theirs, second_gain, forward, wave, twist)
     theirs = swap(send)
+    gate_own, = gates(1, 1, core, seat, short_taps, near_taps, own, other)
     spread = last_gate(gate_own, keep, theirs)
     members = [[4 * j + 2 * high + side for high in range(2) for j in range(BLOCKS)] for side in range(2)]
     values = lax.all_to_all(
@@ -515,7 +531,8 @@
     far, across = (lax.ppermute(value, "ch", [(i, i ^ 2) for i in range(4)]) for value in (mixing, near))
     keep, send = mix(group, (mixing, near, far, across), values)
     theirs = swap(send)
-    return finish(core, coupled_second, keep, theirs)
+    out = finish(False, core, coupled_second, keep)
+    return finish(True, core, coupled_second, theirs, out)
 
 
 def solution(mesh):

time: 98.7 us -> 94.1 us (0.953)
  Pallas kernels: 21.4 us -> 18.8 us
  waiting for transfers between devices: 18 us -> 16.2 us
    ppermute x8, waiting for transfers between devices: 3.25 us -> 1.43 us  [swap(): lax.ppermute(value, 'ch', [(i, i ^ 1) for i in range(lax.axis_size('ch'))])]
    pallas_call x5 -> x7, Pallas kernels: 14.5 us -> 12.9 us  [the longest x1 4.02 us: second_conv(): pl.pallas_call(second_conv_kernel, in_specs=[SMEM] + [VMEM] * 6 + [ANY] *...]
  transfers between devices with their start and end apart: 11 -> 11, of which waited for: 7 -> 8; matrix products, arithmetic and copies ran while one was open for 0% -> 0% of each run, Pallas kernels for 6% -> 8%
where the time goes in v3:
time: 94.1 us; the launch traced here: 93.7 us
  blocking collectives  41.6 us (44%)
  Pallas kernels  18.8 us (20%)
  starting transfers between devices  17 us (18%)
  waiting for transfers between devices  16.2 us (17%)
    all_to_all x1, blocking collectives, on_device(): got = lax.all_to_all(buffer, 'seq', split_axis=0, concat_axis=0, tiled=True)  41.6 us
    ppermute x2, waiting for transfers between devices, on_device(): lax.ppermute(value, 'ch', [(i, i ^ 2) for i in range(4)])  10.9 us
    ppermute x8, starting transfers between devices, swap(): lax.ppermute(value, 'ch', [(i, i ^ 1) for i in range(lax.axis_size('ch'))])  7.43 us
    all_to_all x1, starting transfers between devices, on_device(): lax.all_to_all(spread.reshape(2 * BLOCKS, TILE, N2), ('seq', 'ch'), split...  6.57 us
    pallas_call x1, Pallas kernels, second_conv(): pl.pallas_call(second_conv_kernel, in_specs=[SMEM] + [VMEM] * 6 + [ANY] *...  4.02 us
    all_to_all x1, waiting for transfers between devices, on_device(): lax.all_to_all(spread.reshape(2 * BLOCKS, TILE, N2), ('seq', 'ch'), split...  3.81 us
    pallas_call x2, Pallas kernels, split(): pl.pallas_call(functools.partial(split_kernel, keep), in_specs=[SMEM, ANY...  3.61 us
    pallas_call x2, Pallas kernels, gates(): pl.pallas_call(functools.partial(gates_kernel, index), in_specs=[SMEM] *...  3.06 us
  transfers between devices with their start and end apart: 11, of which 8 were waited for; matrix products, arithmetic and copies ran while one was open for 0% of the time, Pallas kernels for 8%

profile of v3, /device:TPU:1, one launch (start us, length us, event | category | flops | bytes accessed | tf_op | source)
XLA Modules:
  0.0 93.7 jit_solution(12790348849368179436)
XLA Ops:
  0.0 0.0 copy-start.1
  0.0 0.0 copy-start.2
  0.0 1.8 %shard_map.82 = bf16[16,5,16,512]{3,2,1,0:T(8,128)(2,1)S(1)} custom-call(s32[1]{0:T(128)S(6)} %select_n.7.core_ref, bf16[16,16384]{1,0:T(8,128)(2,1)} %signal_ref.3, bf16[2,2,16,16384]{3,2,1,0:T(8,128)(2,1)} %filter_ref.3), custom_call_target="tpu_custom_call" | custom-call | bytes 8388608 | tf_op jit(solution)/shard_map/pallas_call | solution.py:129
  1.8 1.5 %collective-permute-start = (bf16[16,5,16,512]{3,2,1,0:T(8,128)(2,1)S(1)}, bf16[16,5,16,512]{3,2,1,0:T(8,128)(2,1)S(1)}, u32[]{:S(2)}, u32[]{:S(2)}) collective-permute-start(bf16[16,5,16,512]{3,2,1,0:T(8,128)(2,1)S(1)} %shard_map.82), channel_id=1, source_target_pairs={{0,1},{1,0},{2,3},{3,2},{4,5},{5,4},{6,7},{7,6},{8,9},{9,8},{10,11... | collective-permute-start | bytes 3932168 | tf_op jit(solution)/shard_map/ppermute | solution.py:54
  3.3 0.0 copy-done.1
  3.3 0.1 collective-permute-start.2
  3.4 0.0 copy-done.2
  3.4 0.4 collective-permute-start.1
  3.8 1.8 %shard_map.83 = (bf16[32,5,16,512]{3,2,1,0:T(8,128)(2,1)S(1)}, bf16[512,512]{1,0:T(8,128)(2,1)S(1)}) custom-call(s32[1]{0:T(128)S(6)} %select_n.7.core_ref, bf16[16,16384]{1,0:T(8,128)(2,1)} %signal_ref.3, bf16[2,2,16,16384]{3,2,1,0:T(8,128)(2,1)} %filter_ref.3, bf16[2,512,512]{2,1,0:T(8,128)(2,1)} %constant.34.clone.refs_0_), custom_call_target="tpu_custom_call" | custom-call | bytes 8388608 | tf_op jit(solution)/shard_map/pallas_call | solution.py:129
  5.7 0.3 collective-permute-done.piece_ref
  6.0 0.3 shard_map.84
  6.3 0.0 collective-permute-done.1.near_taps
  6.3 0.0 collective-permute-done.2.near
  6.3 41.6 %all_to_all.10.got_ref = bf16[32,5,16,512]{3,2,1,0:T(8,128)(2,1)S(1)} all-to-all(bf16[32,5,16,512]{3,2,1,0:T(8,128)(2,1)S(1)} %shard_map.84), channel_id=1, replica_groups=mesh['seq'=32,'ch'=4] {'seq'}, dimensions={0} | all-to-all | bytes 5242880 | tf_op jit(solution)/shard_map/all_to_all | solution.py:514
  47.9 2.3 %collective-permute-start.5 = (bf16[32,16,512]{2,1,0:T(8,128)(2,1)S(1)}, bf16[32,16,512]{2,1,0:T(8,128)(2,1)S(1)}, u32[]{:S(2)}, u32[]{:S(2)}) collective-permute-start(bf16[32,16,512]{2,1,0:T(8,128)(2,1)S(1)} %shard_map.85.own), channel_id=1, source_target_pairs={{0,1},{1,0},{2,3},{3,2},{4,5},{5,4},{6,7},{7,6},{8,9},{9,8},{10,11... | collective-permute-start | bytes 1572872 | tf_op jit(solution)/shard_map/ppermute | solution.py:54
  50.2 1.4 %shard_map.88 = (bf16[2,272,512]{2,1,0:T(8,128)(2,1)S(1)}, bf16[2,272,512]{2,1,0:T(8,128)(2,1)S(1)}, bf16[512,1024]{1,0:T(8,128)(2,1)S(1)}, bf16[2,272,512]{2,1,0:T(8,128)(2,1)S(1)}) custom-call(s32[1]{0:T(128)S(6)} %select_n.7.core_ref, bf16[32,5,16,512]{3,2,1,0:T(8,128)(2,1)S(1)} %all_to_all.10.got_ref, bf16[512,1024]{1,0:T(8,128)(2,1)} %constant.35.clone.wave_hbm, ...), custom_call_target="tpu_custom_call" | custom-call | tf_op jit(solution)/shard_map/pallas_call | solution.py:218
  51.6 0.1 collective-permute-done.5.other
  51.7 2.6 %shard_map.89 = (bf16[32,16,512]{2,1,0:T(8,128)(2,1)S(1)}, bf16[32,16,512]{2,1,0:T(8,128)(2,1)S(1)}) custom-call(s32[1]{0:T(128)S(6)} %select_n.7.core_ref, bf16[32,16,512]{2,1,0:T(8,128)(2,1)S(1)} %shard_map.85.own, bf16[32,16,512]{2,1,0:T(8,128)(2,1)S(1)} %collective-permute-done.5.other, bf16[2,272,512]{2,1,0:T(8,128)(2,1)S(1)} %get-tuple-element.28.gain, ...), custom_call_target="tpu_custom_call" | custom-call | tf_op jit(solution)/shard_map/pallas_call | solution.py:331
  54.3 0.4 collective-permute-start.6
  54.8 0.1 collective-permute-start.7
  54.9 1.7 %shard_map.87 = (bf16[32,16,512]{2,1,0:T(8,128)(2,1)S(1)}, bf16[32,16,512]{2,1,0:T(8,128)(2,1)S(1)}) custom-call(s32[1]{0:T(128)S(6)} %select_n.7.core_ref, s32[1]{0:T(128)} %bitcast.1.seat_ref, f32[2,3,16]{2,1,0:T(4,128)S(1)} %copy.11.own_taps, f32[2,3,16]{2,1,0:T(4,128)S(1)} %collective-permute-done.1.near_taps, bf16[32,16,512]{2,1,0:T(8,128)(2,1)S(1)} %shard_map.85.own, ...), custom_call_target="tpu_custom_call" | custom-call | tf_op jit(solution)/shard_map/pallas_call | solution.py:379
  56.7 0.0 collective-permute-done.6.theirs_own
  56.7 0.5 collective-permute-done.7.theirs_other
  57.2 4.0 %shard_map.90 = (bf16[32,16,512]{2,1,0:T(8,128)(2,1)S(1)}, bf16[32,16,512]{2,1,0:T(8,128)(2,1)S(1)}) custom-call(s32[1]{0:T(128)S(6)} %select_n.7.core_ref, bf16[32,16,512]{2,1,0:T(8,128)(2,1)S(1)} %get-tuple-element.26.gate_own, bf16[32,16,512]{2,1,0:T(8,128)(2,1)S(1)} %get-tuple-element.27.gate_other, bf16[32,16,512]{2,1,0:T(8,128)(2,1)S(1)} %get-tuple-element.32.mine_own, ...), custom_call_target="tpu_custom_call" | custom-call | tf_op jit(solution)/shard_map/pallas_call | solution.py:406
  61.2 0.5 collective-permute-start.8
  61.7 1.3 %shard_map.86.gate_ref = bf16[32,16,512]{2,1,0:T(8,128)(2,1)S(1)} custom-call(s32[1]{0:T(128)S(6)} %select_n.7.core_ref, s32[1]{0:T(128)} %bitcast.1.seat_ref, f32[2,3,16]{2,1,0:T(4,128)S(1)} %copy.11.own_taps, f32[2,3,16]{2,1,0:T(4,128)S(1)} %collective-permute-done.1.near_taps, bf16[32,16,512]{2,1,0:T(8,128)(2,1)S(1)} %shard_map.85.own, ...), custom_call_target="tpu_custom_call" | custom-call | tf_op jit(solution)/shard_map/pallas_call | solution.py:379
  63.0 0.2 collective-permute-done.8.theirs_ref
  63.2 1.1 %shard_map.91 = bf16[2,32,16,512]{3,2,1,0:T(8,128)(2,1)} custom-call(bf16[32,16,512]{2,1,0:T(8,128)(2,1)S(1)} %shard_map.86.gate_ref, bf16[32,16,512]{2,1,0:T(8,128)(2,1)S(1)} %get-tuple-element.35.keep_ref, bf16[32,16,512]{2,1,0:T(8,128)(2,1)S(1)} %collective-permute-done.8.theirs_ref), custom_call_target="tpu_custom_call" | custom-call | tf_op jit(solution)/shard_map/pallas_call | solution.py:427
  64.3 0.0 copy-start
  64.3 6.6 %all-to-all-start.1 = ((bf16[64,16,512]{2,1,0:T(8,128)(2,1)}), bf16[64,16,512]{2,1,0:T(8,128)(2,1)S(1)}, u32[]{:S(2)}, u32[]{:S(2)}) async-start(bf16[64,16,512]{2,1,0:T(8,128)(2,1)} %bitcast.2), calls=%async_computation.1 | async-start | bytes 2097152 | tf_op jit(solution)/shard_map/all_to_all | solution.py:527
  70.9 2.7 %collective-permute-start.3 = (bf16[16,64]{1,0:T(8,128)(2,1)S(1)}, bf16[16,64]{1,0:T(8,128)(2,1)S(1)}, u32[]{:S(2)}, u32[]{:S(2)}) collective-permute-start(bf16[16,64]{1,0:T(8,128)(2,1)S(1)} %copy-done.1), channel_id=1, source_target_pairs={{0,2},{1,3},{2,0},{3,1},{4,6},{5,7},{6,4},{7,5},{8,10},{9,11},{10,... | collective-permute-start | bytes 6152 | tf_op jit(solution)/shard_map/ppermute | solution.py:531
  73.6 0.4 collective-permute-start.4
  73.9 10.8 %collective-permute-done.3.far = bf16[16,64]{1,0:T(8,128)(2,1)S(1)} collective-permute-done((bf16[16,64]{1,0:T(8,128)(2,1)S(1)}, bf16[16,64]{1,0:T(8,128)(2,1)S(1)}, u32[]{:S(2)}, u32[]{:S(2)}) %collective-permute-start.3) | collective-permute-done | bytes 2080 | tf_op jit(solution)/shard_map/ppermute | solution.py:531
  84.8 0.1 collective-permute-done.4.across
  84.9 3.8 %all-to-all-done.1.values_ref = bf16[64,16,512]{2,1,0:T(8,128)(2,1)S(1)} async-done(((bf16[64,16,512]{2,1,0:T(8,128)(2,1)}), bf16[64,16,512]{2,1,0:T(8,128)(2,1)S(1)}, u32[]{:S(2)}, u32[]{:S(2)}) %all-to-all-start.1) | async-done | bytes 1048608 | tf_op jit(solution)/shard_map/all_to_all | solution.py:527
  88.7 0.9 shard_map.92
  89.6 2.1 %collective-permute-start.9 = (bf16[16,8192]{1,0:T(8,128)(2,1)S(1)}, bf16[16,8192]{1,0:T(8,128)(2,1)S(1)}, u32[]{:S(2)}, u32[]{:S(2)}) collective-permute-start(bf16[16,8192]{1,0:T(8,128)(2,1)S(1)} %get-tuple-element.37), channel_id=1, source_target_pairs={{0,1},{1,0},{2,3},{3,2},{4,5},{5,4},{6,7},{7,6},{8,9},{9,8},{10,11... | collective-permute-start | bytes 786440 | tf_op jit(solution)/shard_map/ppermute | solution.py:54
  91.7 0.0 copy-done
  91.7 0.9 shard_map.93.refs_0_
  92.6 0.3 collective-permute-done.9.update_ref
  92.8 0.9 shard_map.94
  (2 shorter events, 0.0 us)
Async XLA Ops:
  0.0 3.3 %copy-start.1 = (bf16[16,64]{1,0:T(8,128)(2,1)S(1)}, bf16[16,64]{1,0:T(8,128)(2,1)}, u32[]{:S(2)}) copy-start(bf16[16,64]{1,0:T(8,128)(2,1)} %own.1) | copy-start | bytes 6148
  0.0 3.4 %copy-start.2 = (f32[2,3,16]{2,0,1:T(2,128)S(1)}, f32[2,3,16]{2,0,1:T(2,128)}, u32[]{:S(2)}) copy-start(f32[2,3,16]{2,0,1:T(2,128)} %param.11) | copy-start | bytes 1156
  1.8 4.2 %collective-permute-start = (bf16[16,5,16,512]{3,2,1,0:T(8,128)(2,1)S(1)}, bf16[16,5,16,512]{3,2,1,0:T(8,128)(2,1)S(1)}, u32[]{:S(2)}, u32[]{:S(2)}) collective-permute-start(bf16[16,5,16,512]{3,2,1,0:T(8,128)(2,1)S(1)} %shard_map.82), channel_id=1, source_target_pairs={{0,1},{1,0},{2,3},{3,2},{4,5},{5,4},{6,7},{7,6},{8,9},{9,8},{10,11... | collective-permute-start | bytes 3932168 | tf_op jit(solution)/shard_map/ppermute | solution.py:54
  3.3 3.0 %collective-permute-start.2 = (bf16[16,64]{1,0:T(8,128)(2,1)S(1)}, bf16[16,64]{1,0:T(8,128)(2,1)S(1)}, u32[]{:S(2)}, u32[]{:S(2)}) collective-permute-start(bf16[16,64]{1,0:T(8,128)(2,1)S(1)} %copy-done.1), channel_id=1, source_target_pairs={{0,1},{1,0},{2,3},{3,2},{4,5},{5,4},{6,7},{7,6},{8,9},{9,8},{10,11... | collective-permute-start | bytes 6152 | tf_op jit(solution)/shard_map/ppermute | solution.py:54
  3.4 2.8 %collective-permute-start.1 = (f32[2,3,16]{2,1,0:T(4,128)S(1)}, f32[2,3,16]{2,1,0:T(4,128)S(1)}, u32[]{:S(2)}, u32[]{:S(2)}) collective-permute-start(f32[2,3,16]{2,1,0:T(4,128)S(1)} %copy.11.own_taps), channel_id=1, source_target_pairs={{0,1},{1,0},{2,3},{3,2},{4,5},{5,4},{6,7},{7,6},{8,9},{9,8},{10,11... | collective-permute-start | bytes 1160 | tf_op jit(solution)/shard_map/ppermute | solution.py:54
  47.9 3.8 %collective-permute-start.5 = (bf16[32,16,512]{2,1,0:T(8,128)(2,1)S(1)}, bf16[32,16,512]{2,1,0:T(8,128)(2,1)S(1)}, u32[]{:S(2)}, u32[]{:S(2)}) collective-permute-start(bf16[32,16,512]{2,1,0:T(8,128)(2,1)S(1)} %shard_map.85.own), channel_id=1, source_target_pairs={{0,1},{1,0},{2,3},{3,2},{4,5},{5,4},{6,7},{7,6},{8,9},{9,8},{10,11... | collective-permute-start | bytes 1572872 | tf_op jit(solution)/shard_map/ppermute | solution.py:54
  54.3 2.3 %collective-permute-start.6 = (bf16[32,16,512]{2,1,0:T(8,128)(2,1)S(1)}, bf16[32,16,512]{2,1,0:T(8,128)(2,1)}, u32[]{:S(2)}, u32[]{:S(2)}) collective-permute-start(bf16[32,16,512]{2,1,0:T(8,128)(2,1)S(1)} %get-tuple-element.32.mine_own), channel_id=1, source_target_pairs={{0,1},{1,0},{2,3},{3,2},{4,5},{5,4},{6,7},{7,6},{8,9},{9,8},{10,11... | collective-permute-start | bytes 1572872 | tf_op jit(solution)/shard_map/ppermute | solution.py:54
  54.8 2.4 %collective-permute-start.7 = (bf16[32,16,512]{2,1,0:T(8,128)(2,1)S(1)}, bf16[32,16,512]{2,1,0:T(8,128)(2,1)}, u32[]{:S(2)}, u32[]{:S(2)}) collective-permute-start(bf16[32,16,512]{2,1,0:T(8,128)(2,1)S(1)} %get-tuple-element.33.mine_other), channel_id=1, source_target_pairs={{0,1},{1,0},{2,3},{3,2},{4,5},{5,4},{6,7},{7,6},{8,9},{9,8},{10,11... | collective-permute-start | bytes 1572872 | tf_op jit(solution)/shard_map/ppermute | solution.py:54
  61.2 2.0 %collective-permute-start.8 = (bf16[32,16,512]{2,1,0:T(8,128)(2,1)S(1)}, bf16[32,16,512]{2,1,0:T(8,128)(2,1)S(1)}, u32[]{:S(2)}, u32[]{:S(2)}) collective-permute-start(bf16[32,16,512]{2,1,0:T(8,128)(2,1)S(1)} %get-tuple-element.36), channel_id=1, source_target_pairs={{0,1},{1,0},{2,3},{3,2},{4,5},{5,4},{6,7},{7,6},{8,9},{9,8},{10,11... | collective-permute-start | bytes 1572872 | tf_op jit(solution)/shard_map/ppermute | solution.py:54
  64.3 27.4 %copy-start = (bf16[16,16384]{1,0:T(8,128)(2,1)S(1)}, bf16[16,16384]{1,0:T(8,128)(2,1)}, u32[]{:S(2)}) copy-start(bf16[16,16384]{1,0:T(8,128)(2,1)} %second_ref.3) | copy-start | bytes 1572868
  64.3 24.4 %all-to-all-start.1 = ((bf16[64,16,512]{2,1,0:T(8,128)(2,1)}), bf16[64,16,512]{2,1,0:T(8,128)(2,1)S(1)}, u32[]{:S(2)}, u32[]{:S(2)}) async-start(bf16[64,16,512]{2,1,0:T(8,128)(2,1)} %bitcast.2), calls=%async_computation.1 | async-start | bytes 2097152 | tf_op jit(solution)/shard_map/all_to_all | solution.py:527
  70.9 13.9 %collective-permute-start.3 = (bf16[16,64]{1,0:T(8,128)(2,1)S(1)}, bf16[16,64]{1,0:T(8,128)(2,1)S(1)}, u32[]{:S(2)}, u32[]{:S(2)}) collective-permute-start(bf16[16,64]{1,0:T(8,128)(2,1)S(1)} %copy-done.1), channel_id=1, source_target_pairs={{0,2},{1,3},{2,0},{3,1},{4,6},{5,7},{6,4},{7,5},{8,10},{9,11},{10,... | collective-permute-start | bytes 6152 | tf_op jit(solution)/shard_map/ppermute | solution.py:531
  73.6 11.3 %collective-permute-start.4 = (bf16[16,64]{1,0:T(8,128)(2,1)S(1)}, bf16[16,64]{1,0:T(8,128)(2,1)S(1)}, u32[]{:S(2)}, u32[]{:S(2)}) collective-permute-start(bf16[16,64]{1,0:T(8,128)(2,1)S(1)} %collective-permute-done.2.near), channel_id=1, source_target_pairs={{0,2},{1,3},{2,0},{3,1},{4,6},{5,7},{6,4},{7,5},{8,10},{9,11},{10,... | collective-permute-start | bytes 6152 | tf_op jit(solution)/shard_map/ppermute | solution.py:531
  89.6 3.3 %collective-permute-start.9 = (bf16[16,8192]{1,0:T(8,128)(2,1)S(1)}, bf16[16,8192]{1,0:T(8,128)(2,1)S(1)}, u32[]{:S(2)}, u32[]{:S(2)}) collective-permute-start(bf16[16,8192]{1,0:T(8,128)(2,1)S(1)} %get-tuple-element.37), channel_id=1, source_target_pairs={{0,1},{1,0},{2,3},{3,2},{4,5},{5,4},{6,7},{7,6},{8,9},{9,8},{10,11... | collective-permute-start | bytes 786440 | tf_op jit(solution)/shard_map/ppermute | solution.py:54

commit v4 on v3

--- a/solution.py
+++ b/solution.py
@@ -141,28 +141,19 @@
     )(core, signal, spectra, *forward)
 
 
-def place_kernel(core_ref, piece_ref, whole_ref, out_ref, piece, sems):
+def place_kernel(core_ref, piece_ref, whole_ref, out_ref):
     del whole_ref
-    planes = piece.shape[1]
-    target = out_ref.at[pl.ds((1 - core_ref[0]) * TILE, TILE)]
-    loads = [fetch(piece_ref.at[:, plane], piece.at[:, plane], sems, plane) for plane in range(planes)]
-    stores = []
-    for plane in range(planes):
-        loads[plane].wait()
-        stores.append(fetch(piece.at[:, plane], target.at[:, plane], sems, planes + plane))
-    for store in stores:
-        store.wait()
+    out_ref[pl.ds((1 - core_ref[0]) * TILE, TILE)] = piece_ref[...]
 
 
 def place(core, piece, whole):
     return pl.pallas_call(
         place_kernel,
-        in_specs=[SMEM, ANY, ANY],
-        out_specs=ANY,
+        in_specs=[SMEM, VMEM, VMEM],
+        out_specs=VMEM,
         out_shape=jax.ShapeDtypeStruct(whole.shape, whole.dtype),
-        scratch_shapes=[pltpu.VMEM(piece.shape, piece.dtype), pltpu.SemaphoreType.DMA((2 * len(PLANES),))],
         input_output_aliases={2: 0},
-        compiler_params=params(2),
+        compiler_params=params(8),
         cost_estimate=cost(0, 0),
     )(core, piece, whole)
 
@@ -200,8 +191,8 @@
                 high_bf[:, (1 - side) * HALF:(2 - side) * HALF], mirror, preferred_element_type=F32
             )
             here = slice(side * HALF, (side + 1) * HALF)
-            gain_ref[part, :HALF, here] = ((low[:, here] + keep * reversed_high) * SCALE).astype(BF)
-        gain_ref[part, HALF:, :] = (high[:EXTRA] * SCALE).astype(BF)
+            gain_ref[part, :HALF, here] = (low[:, here] + keep * reversed_high).astype(BF)
+        gain_ref[part, HALF:, :] = high_bf[:EXTRA]
 
 
 def fold_kernel(core_ref, got_ref, wave_hbm, twist_hbm, first_ref, second_ref, wave_ref, twist_ref, sems):
@@ -298,8 +289,8 @@
         ).reshape(half, TILE, N2)
         for rows in (slice(0, HALF), slice(HALF, 2 * HALF))
     )
-    out_ref[:half] = (even + odd).astype(BF)
-    out_ref[half:] = (even - odd).astype(BF)
+    out_ref[:half] = ((even + odd) * SCALE).astype(BF)
+    out_ref[half:] = ((even - odd) * SCALE).astype(BF)
 
 
 CONV_SCRATCH = [
@@ -321,18 +312,18 @@
     outer_backward(forward, back, own_ref, 0)
 
 
-def first_conv_kernel(core_ref, own, other, gain, forward, wave, twist, own_ref, other_ref, folded, *scratch):
+def first_conv_kernel(core_ref, own, other, gain, forward, wave, twist, out_ref, folded, *scratch):
     fold_time(own, folded, 0)
     fold_time(other, folded, 1)
-    convolve(core_ref[0], gain, forward, wave, twist, own_ref, other_ref, folded, *scratch)
+    convolve(core_ref[0], gain, forward, wave, twist, out_ref.at[0], out_ref.at[1], folded, *scratch)
 
 
 def first_conv(core, own, other, *rest):
     return pl.pallas_call(
         first_conv_kernel,
         in_specs=[SMEM] + [VMEM] * 6,
-        out_specs=(VMEM, VMEM),
-        out_shape=(jax.ShapeDtypeStruct((BLOCKS, TILE, N2), BF),) * 2,
+        out_specs=VMEM,
+        out_shape=jax.ShapeDtypeStruct((2, BLOCKS, TILE, N2), BF),
         scratch_shapes=CONV_SCRATCH,
         compiler_params=params(6),
         cost_estimate=cost(0, 0),
@@ -361,9 +352,14 @@
     return (taps[0] * tiles[0] + taps[1] * tiles[1] + taps[2] * tiles[2]).astype(BF)
 
 
-def gates_kernel(index, core_ref, seat_ref, own_taps, near_taps, own, other, *outs):
+def gates_kernel(index, core_ref, seat_ref, own_taps, near_taps, own, other, *refs):
     core = core_ref[0]
     taps = taps_of(index, core, seat_ref, own_taps, near_taps)
+    if index == 0:
+        wave_hbm, twist_hbm, *outs, wave, twist, sems = refs
+        loads = [fetch(twist_hbm.at[core], twist, sems, 0), fetch(wave_hbm, wave, sems, 1)]
+    else:
+        outs, loads = refs, []
 
     @pl.loop(0, BLOCKS, unroll=8)
     def _(block):
@@ -374,62 +370,67 @@
             ahead = own[jnp.where(core == 0, block, last), :, N2 - LANES:].astype(F32)
             outs[1][block] = gate(taps, lagged(other[block].astype(F32), ahead))
 
-
-def gates(index, count, core, seat, taps, near_taps, own, other):
+    for load in loads:
+        load.wait()
+
+
+def gates(index, core, seat, taps, near_taps, own, other, *tables):
+    count = 2 if index == 0 else 1
+    field = jax.ShapeDtypeStruct((BLOCKS, TILE, N2), BF)
+    brought = [jax.ShapeDtypeStruct((N2, 2 * N2), BF), jax.ShapeDtypeStruct((2, ROWS, N2), BF)] if tables else []
     return pl.pallas_call(
         functools.partial(gates_kernel, index),
-        in_specs=[SMEM] * 4 + [VMEM, VMEM],
-        out_specs=(VMEM,) * count,
-        out_shape=(jax.ShapeDtypeStruct((BLOCKS, TILE, N2), BF),) * count,
+        in_specs=[SMEM] * 4 + [VMEM, VMEM] + [ANY] * len(tables),
+        out_specs=(VMEM,) * (count + len(tables)),
+        out_shape=[field] * count + brought,
+        scratch_shapes=[pltpu.SemaphoreType.DMA((2,))] if tables else [],
         compiler_params=params(4),
         cost_estimate=cost(0, 0),
-    )(core, seat, taps, near_taps, own, other)
+    )(core, seat, taps, near_taps, own, other, *tables)
 
 
 def second_conv_kernel(
-    core_ref, gate_own, gate_other, mine_own, mine_other, gain, forward, theirs_own, theirs_other, wave_hbm, twist_hbm,
-    own_ref, other_ref, theirs, wave, twist, sems, folded, *scratch,
+    core_ref, gate_own, gate_other, mine, gain, forward, wave, twist, theirs_any, own_ref, other_ref, theirs, sems, folded,
+    *scratch,
 ):
-    core = core_ref[0]
-    loads = [fetch(theirs_other, theirs.at[0], sems, 2), fetch(theirs_own, theirs.at[1], sems, 3)]
-    twist_load = fetch(twist_hbm.at[core], twist, sems, 0)
-    wave_load = fetch(wave_hbm, wave, sems, 1)
-    loads[0].wait()
-    fold_time(gate_own[...] * (mine_own[...] + theirs[0]), folded, 0)
-    loads[1].wait()
-    fold_time(gate_other[...] * (mine_other[...] + theirs[1]), folded, 1)
-    twist_load.wait()
-    convolve(core, gain, forward, wave, twist, own_ref, other_ref, folded, *scratch, ready=wave_load.wait)
+    loads = [fetch(theirs_any.at[1 - place], theirs.at[place], sems, place) for place in range(2)]
+    for place, gate_ref in enumerate((gate_own, gate_other)):
+        loads[place].wait()
+        fold_time(gate_ref[...] * (mine[place] + theirs[place]), folded, place)
+    convolve(core_ref[0], gain, forward, wave, twist, own_ref, other_ref, folded, *scratch)
 
 
 def second_conv(core, gate, mine, theirs, gain, forward, wave, twist):
     return pl.pallas_call(
         second_conv_kernel,
-        in_specs=[SMEM] + [VMEM] * 6 + [ANY] * 4,
+        in_specs=[SMEM] + [VMEM] * 7 + [ANY],
         out_specs=(VMEM, VMEM),
         out_shape=(jax.ShapeDtypeStruct((BLOCKS, TILE, N2), BF),) * 2,
-        scratch_shapes=[
-            pltpu.VMEM((2, BLOCKS, TILE, N2), BF), pltpu.VMEM((N2, 2 * N2), BF), pltpu.VMEM((2, ROWS, N2), BF),
-            pltpu.SemaphoreType.DMA((4,)),
-        ] + CONV_SCRATCH,
-        compiler_params=params(10),
-        cost_estimate=cost(0, 0),
-    )(core, *gate, *mine, gain, forward, *theirs, wave, twist)
-
-
-def last_kernel(gate_ref, keep_ref, theirs_ref, out_ref):
-    last = gate_ref[...] * (keep_ref[...] + theirs_ref[...])
-    out_ref[0] = last
-    out_ref[1] = last
+        scratch_shapes=[pltpu.VMEM((2, BLOCKS, TILE, N2), BF), pltpu.SemaphoreType.DMA((2,))] + CONV_SCRATCH,
+        compiler_params=params(8),
+        cost_estimate=cost(0, 0),
+    )(core, *gate, mine, gain, forward, wave, twist, theirs)
+
+
+def last_kernel(gate_ref, keep_ref, theirs_ref, out_ref, last, sems):
+    parts, copies = 4, []
+    for part in range(parts):
+        blocks = slice(part * BLOCKS // parts, (part + 1) * BLOCKS // parts)
+        last[blocks] = gate_ref[blocks] * (keep_ref[blocks] + theirs_ref[blocks])
+        for high in range(2):
+            copies.append(fetch(last.at[blocks], out_ref.at[high, blocks], sems, 2 * part + high))
+    for copy in copies:
+        copy.wait()
 
 
 def last_gate(gate, keep, theirs):
     return pl.pallas_call(
         last_kernel,
         in_specs=[VMEM] * 3,
-        out_specs=VMEM,
+        out_specs=ANY,
         out_shape=jax.ShapeDtypeStruct((2, BLOCKS, TILE, N2), BF),
-        compiler_params=params(4),
+        scratch_shapes=[pltpu.VMEM((BLOCKS, TILE, N2), BF), pltpu.SemaphoreType.DMA((8,))],
+        compiler_params=params(2),
         cost_estimate=cost(0, 0),
     )(gate, keep, theirs)
 
@@ -478,22 +479,26 @@
 
 
 def finish_kernel(other, core_ref, second_ref, update_ref, *refs):
-    out_ref, second, result, sems = refs[-4:]
-    width = TILE * N2
-    here = pl.ds(pl.multiple_of((1 - core_ref[0] if other else core_ref[0]) * width, width), width)
-    fetch(second_ref.at[:, here], second, sems, 0).wait()
-    result[...] = second[...].astype(F32) - update_ref[...].astype(F32)
-    fetch(result, out_ref.at[:, here], sems, 1).wait()
+    out_ref, result, sems = refs[-3:]
+    parts, width = 4, TILE * N2
+    base = (1 - core_ref[0] if other else core_ref[0]) * width
+    copies = []
+    for part in range(parts):
+        here = slice(part * width // parts, (part + 1) * width // parts)
+        there = pl.ds(pl.multiple_of(base + part * width // parts, width // parts), width // parts)
+        result[:, here] = second_ref[:, there].astype(F32) - update_ref[:, here].astype(F32)
+        copies.append(fetch(result.at[:, here], out_ref.at[:, there], sems, part))
+    for copy in copies:
+        copy.wait()
 
 
 def finish(other, core, second, update, *out):
-    width = TILE * N2
     return pl.pallas_call(
         functools.partial(finish_kernel, other),
-        in_specs=[SMEM, ANY, VMEM] + [ANY] * len(out),
+        in_specs=[SMEM, VMEM, VMEM] + [ANY] * len(out),
         out_specs=ANY,
         out_shape=jax.ShapeDtypeStruct(second.shape, F32),
-        scratch_shapes=[pltpu.VMEM((TILE, width), BF), pltpu.VMEM((TILE, width), F32), pltpu.SemaphoreType.DMA((2,))],
+        scratch_shapes=[pltpu.VMEM((TILE, TILE * N2), F32), pltpu.SemaphoreType.DMA((4,))],
         input_output_aliases={3: 0} if other else {},
         compiler_params=params(4),
         cost_estimate=cost(0, 0),
@@ -507,28 +512,30 @@
     forward, wave, twist = (in_hbm(jnp.asarray(t)) for t in tables())
     first_hbm, spectra_hbm = in_hbm(coupled_first), in_hbm(spectra)
 
-    near_taps, near = swap(short_taps), swap(mixing)
+    near_taps = swap(short_taps)
     theirs = swap(split(False, core, first_hbm, spectra_hbm))
     buffer, forward = split(True, core, first_hbm, spectra_hbm, forward)
-    buffer, near_taps, near = lax.optimization_barrier((place(core, theirs, buffer), near_taps, near))
+    buffer, near_taps = lax.optimization_barrier((place(core, theirs, buffer), near_taps))
     got = lax.all_to_all(buffer, "seq", split_axis=0, concat_axis=0, tiled=True)
 
     own = field_of(got)
     other = swap(own)
     gain, second_gain, wave_now, twist_now = fold(core, got, wave, twist)
     mine = first_conv(core, own, other, gain, forward, wave_now, twist_now)
-    theirs = [swap(half) for half in mine]
-    gate_all = gates(0, 2, core, seat, short_taps, near_taps, own, other)
+    theirs = swap(mine)
+    *gate_all, wave, twist = gates(0, core, seat, short_taps, near_taps, own, other, wave, twist)
     keep, send = second_conv(core, gate_all, mine, theirs, second_gain, forward, wave, twist)
     theirs = swap(send)
-    gate_own, = gates(1, 1, core, seat, short_taps, near_taps, own, other)
+    gate_own, = gates(1, core, seat, short_taps, near_taps, own, other)
     spread = last_gate(gate_own, keep, theirs)
     members = [[4 * j + 2 * high + side for high in range(2) for j in range(BLOCKS)] for side in range(2)]
     values = lax.all_to_all(
         spread.reshape(2 * BLOCKS, TILE, N2), ("seq", "ch"), split_axis=0, concat_axis=0, tiled=True,
         axis_index_groups=members,
     )
-    far, across = (lax.ppermute(value, "ch", [(i, i ^ 2) for i in range(4)]) for value in (mixing, near))
+    near, far, across = (
+        lax.ppermute(mixing, "ch", [(i, i ^ apart) for i in range(4)]) for apart in (1, 2, 3)
+    )
     keep, send = mix(group, (mixing, near, far, across), values)
     theirs = swap(send)
     out = finish(False, core, coupled_second, keep)

time: 94.1 us -> 93.7 us (level)
    all_to_all x1, waiting for transfers between devices: 3.81 us -> 2.68 us  [on_device(): lax.all_to_all(spread.reshape(2 * BLOCKS, TILE, N2), ('seq', 'ch'), split...]
    ppermute x2 -> x3, starting transfers between devices: 3.05 us -> 3.91 us  [on_device(): lax.ppermute(mixing, 'ch', [(i, i ^ apart) for i in range(4)])]
    ppermute x8 -> x6, starting transfers between devices: 7.43 us -> 6.88 us  [swap(): lax.ppermute(value, 'ch', [(i, i ^ 1) for i in range(lax.axis_size('ch'))])]
    ppermute x2 -> x3, waiting for transfers between devices: 10.9 us -> 11.2 us  [on_device(): lax.ppermute(mixing, 'ch', [(i, i ^ apart) for i in range(4)])]
  transfers between devices with their start and end apart: 11 -> 10, of which waited for: 8 -> 8; matrix products, arithmetic and copies ran while one was open for 0% -> 0% of each run, Pallas kernels for 8% -> 8%
where the time goes in v4:
time: 93.7 us; the launch traced here: 93.3 us
  blocking collectives  41.6 us (44%)
  Pallas kernels  18.6 us (20%)
  starting transfers between devices  17.4 us (19%)
  waiting for transfers between devices  15.6 us (17%)
    all_to_all x1, blocking collectives, on_device(): got = lax.all_to_all(buffer, 'seq', split_axis=0, concat_axis=0, tiled=True)  41.6 us
    ppermute x3, waiting for transfers between devices, on_device(): lax.ppermute(mixing, 'ch', [(i, i ^ apart) for i in range(4)])  11.2 us
    ppermute x6, starting transfers between devices, swap(): lax.ppermute(value, 'ch', [(i, i ^ 1) for i in range(lax.axis_size('ch'))])  6.88 us
    all_to_all x1, starting transfers between devices, on_device(): lax.all_to_all(spread.reshape(2 * BLOCKS, TILE, N2), ('seq', 'ch'), split...  6.58 us
    ppermute x3, starting transfers between devices, on_device(): lax.ppermute(mixing, 'ch', [(i, i ^ apart) for i in range(4)])  3.91 us
    pallas_call x1, Pallas kernels, second_conv(): pl.pallas_call(second_conv_kernel, in_specs=[SMEM] + [VMEM] * 7 + [ANY],...  3.85 us
    pallas_call x2, Pallas kernels, split(): pl.pallas_call(functools.partial(split_kernel, keep), in_specs=[SMEM, ANY...  3.6 us
    pallas_call x2, Pallas kernels, gates(): pl.pallas_call(functools.partial(gates_kernel, index), in_specs=[SMEM] *...  3.42 us
  transfers between devices with their start and end apart: 10, of which 8 were waited for; matrix products, arithmetic and copies ran while one was open for 0% of the time, Pallas kernels for 8%

profile of v4, /device:TPU:1, one launch (start us, length us, event | category | flops | bytes accessed | tf_op | source)
XLA Modules:
  0.0 93.3 jit_solution(8995038876277949216)
XLA Ops:
  0.0 0.0 copy-start.2
  0.0 1.8 %shard_map.82 = bf16[16,5,16,512]{3,2,1,0:T(8,128)(2,1)S(1)} custom-call(s32[1]{0:T(128)S(6)} %select_n.7.core_ref, bf16[16,16384]{1,0:T(8,128)(2,1)} %signal_ref.3, bf16[2,2,16,16384]{3,2,1,0:T(8,128)(2,1)} %filter_ref.3), custom_call_target="tpu_custom_call" | custom-call | bytes 8388608 | tf_op jit(solution)/shard_map/pallas_call | solution.py:129
  1.8 1.5 %collective-permute-start.3 = (bf16[16,5,16,512]{3,2,1,0:T(8,128)(2,1)S(1)}, bf16[16,5,16,512]{3,2,1,0:T(8,128)(2,1)S(1)}, u32[]{:S(2)}, u32[]{:S(2)}) collective-permute-start(bf16[16,5,16,512]{3,2,1,0:T(8,128)(2,1)S(1)} %shard_map.82), channel_id=1, source_target_pairs={{0,1},{1,0},{2,3},{3,2},{4,5},{5,4},{6,7},{7,6},{8,9},{9,8},{10,11... | collective-permute-start | bytes 3932168 | tf_op jit(solution)/shard_map/ppermute | solution.py:54
  3.3 0.0 copy-done.2
  3.3 0.1 collective-permute-start.4
  3.4 1.8 %shard_map.83 = (bf16[32,5,16,512]{3,2,1,0:T(8,128)(2,1)S(1)}, bf16[512,512]{1,0:T(8,128)(2,1)S(1)}) custom-call(s32[1]{0:T(128)S(6)} %select_n.7.core_ref, bf16[16,16384]{1,0:T(8,128)(2,1)} %signal_ref.3, bf16[2,2,16,16384]{3,2,1,0:T(8,128)(2,1)} %filter_ref.3, bf16[2,512,512]{2,1,0:T(8,128)(2,1)} %constant.34.clone.refs_0_), custom_call_target="tpu_custom_call" | custom-call | bytes 8388608 | tf_op jit(solution)/shard_map/pallas_call | solution.py:129
  5.2 0.7 collective-permute-done.3.piece_ref
  6.0 0.1 shard_map.84
  6.1 0.0 collective-permute-done.4.near_taps
  6.1 41.6 %all_to_all.10.got_ref = bf16[32,5,16,512]{3,2,1,0:T(8,128)(2,1)S(1)} all-to-all(bf16[32,5,16,512]{3,2,1,0:T(8,128)(2,1)S(1)} %shard_map.84), channel_id=1, replica_groups=mesh['seq'=32,'ch'=4] {'seq'}, dimensions={0} | all-to-all | bytes 5242880 | tf_op jit(solution)/shard_map/all_to_all | solution.py:519
  47.7 2.3 %collective-permute-start.5 = (bf16[32,16,512]{2,1,0:T(8,128)(2,1)S(1)}, bf16[32,16,512]{2,1,0:T(8,128)(2,1)S(1)}, u32[]{:S(2)}, u32[]{:S(2)}) collective-permute-start(bf16[32,16,512]{2,1,0:T(8,128)(2,1)S(1)} %shard_map.85.own), channel_id=1, source_target_pairs={{0,1},{1,0},{2,3},{3,2},{4,5},{5,4},{6,7},{7,6},{8,9},{9,8},{10,11... | collective-permute-start | bytes 1572872 | tf_op jit(solution)/shard_map/ppermute | solution.py:54
  50.0 1.4 %shard_map.88 = (bf16[2,272,512]{2,1,0:T(8,128)(2,1)S(1)}, bf16[2,272,512]{2,1,0:T(8,128)(2,1)S(1)}, bf16[512,1024]{1,0:T(8,128)(2,1)S(1)}, bf16[2,272,512]{2,1,0:T(8,128)(2,1)S(1)}) custom-call(s32[1]{0:T(128)S(6)} %select_n.7.core_ref, bf16[32,5,16,512]{3,2,1,0:T(8,128)(2,1)S(1)} %all_to_all.10.got_ref, bf16[512,1024]{1,0:T(8,128)(2,1)} %constant.35.clone.refs_0_.wave_hbm, ...), custom_call_target="tpu_custom_call" | custom-call | tf_op jit(solution)/shard_map/pallas_call | solution.py:209
  51.4 0.1 collective-permute-done.5.other
  51.5 2.6 %shard_map.89.mine = bf16[2,32,16,512]{3,2,1,0:T(8,128)(2,1)S(1)} custom-call(s32[1]{0:T(128)S(6)} %select_n.7.core_ref, bf16[32,16,512]{2,1,0:T(8,128)(2,1)S(1)} %shard_map.85.own, bf16[32,16,512]{2,1,0:T(8,128)(2,1)S(1)} %collective-permute-done.5.other, bf16[2,272,512]{2,1,0:T(8,128)(2,1)S(1)} %get-tuple-element.26.gain, ...), custom_call_target="tpu_custom_call" | custom-call | tf_op jit(solution)/shard_map/pallas_call | solution.py:322
  54.1 0.5 collective-permute-start.6
  54.6 2.1 %shard_map.87 = (bf16[32,16,512]{2,1,0:T(8,128)(2,1)S(1)}, bf16[32,16,512]{2,1,0:T(8,128)(2,1)S(1)}, bf16[512,1024]{1,0:T(8,128)(2,1)S(1)}, bf16[2,272,512]{2,1,0:T(8,128)(2,1)S(1)}) custom-call(s32[1]{0:T(128)S(6)} %select_n.7.core_ref, s32[1]{0:T(128)} %bitcast.1.seat_ref, f32[2,3,16]{2,1,0:T(4,128)S(1)} %copy.12.own_taps, ...), custom_call_target="tpu_custom_call" | custom-call | tf_op jit(solution)/shard_map/pallas_call | solution.py:381
  56.7 0.3 collective-permute-done.6.theirs_any
  57.0 3.9 %shard_map.90 = (bf16[32,16,512]{2,1,0:T(8,128)(2,1)S(1)}, bf16[32,16,512]{2,1,0:T(8,128)(2,1)S(1)}) custom-call(s32[1]{0:T(128)S(6)} %select_n.7.core_ref, bf16[32,16,512]{2,1,0:T(8,128)(2,1)S(1)} %get-tuple-element.24.gate_own, bf16[32,16,512]{2,1,0:T(8,128)(2,1)S(1)} %get-tuple-element.25.gate_other, bf16[2,32,16,512]{3,2,1,0:T(8,128)(2,1)S(1)} %shard_map.89.mine, ...), custom_call_target="tpu_custom_call" | custom-call | tf_op jit(solution)/shard_map/pallas_call | solution.py:404
  60.9 0.5 collective-permute-start.7
  61.3 1.3 %shard_map.86.gate_ref = bf16[32,16,512]{2,1,0:T(8,128)(2,1)S(1)} custom-call(s32[1]{0:T(128)S(6)} %select_n.7.core_ref, s32[1]{0:T(128)} %bitcast.1.seat_ref, f32[2,3,16]{2,1,0:T(4,128)S(1)} %copy.12.own_taps, f32[2,3,16]{2,1,0:T(4,128)S(1)} %collective-permute-done.4.near_taps, bf16[32,16,512]{2,1,0:T(8,128)(2,1)S(1)} %shard_map.85.own, ...), custom_call_target="tpu_custom_call" | custom-call | tf_op jit(solution)/shard_map/pallas_call | solution.py:381
  62.7 0.2 collective-permute-done.7.theirs_ref
  62.9 0.0 copy-start.1
  62.9 1.1 %shard_map.91 = bf16[2,32,16,512]{3,2,1,0:T(8,128)(2,1)} custom-call(bf16[32,16,512]{2,1,0:T(8,128)(2,1)S(1)} %shard_map.86.gate_ref, bf16[32,16,512]{2,1,0:T(8,128)(2,1)S(1)} %get-tuple-element.33.keep_ref, bf16[32,16,512]{2,1,0:T(8,128)(2,1)S(1)} %collective-permute-done.7.theirs_ref), custom_call_target="tpu_custom_call" | custom-call | tf_op jit(solution)/shard_map/pallas_call | solution.py:427
  63.9 0.0 copy-start
  63.9 6.6 %all-to-all-start.1 = ((bf16[64,16,512]{2,1,0:T(8,128)(2,1)}), bf16[64,16,512]{2,1,0:T(8,128)(2,1)S(1)}, u32[]{:S(2)}, u32[]{:S(2)}) async-start(bf16[64,16,512]{2,1,0:T(8,128)(2,1)} %bitcast.2), calls=%async_computation.1 | async-start | bytes 2097152 | tf_op jit(solution)/shard_map/all_to_all | solution.py:532
  70.5 0.0 copy-done.1
  70.5 2.7 %collective-permute-start.1 = (bf16[16,64]{1,0:T(8,128)(2,1)S(1)}, bf16[16,64]{1,0:T(8,128)(2,1)S(1)}, u32[]{:S(2)}, u32[]{:S(2)}) collective-permute-start(bf16[16,64]{1,0:T(8,128)(2,1)S(1)} %copy-done.1), channel_id=1, source_target_pairs={{0,2},{1,3},{2,0},{3,1},{4,6},{5,7},{6,4},{7,5},{8,10},{9,11},{10,... | collective-permute-start | bytes 6152 | tf_op jit(solution)/shard_map/ppermute | solution.py:537
  73.2 1.2 %collective-permute-start = (bf16[16,64]{1,0:T(8,128)(2,1)S(1)}, bf16[16,64]{1,0:T(8,128)(2,1)S(1)}, u32[]{:S(2)}, u32[]{:S(2)}) collective-permute-start(bf16[16,64]{1,0:T(8,128)(2,1)S(1)} %copy-done.1), channel_id=1, source_target_pairs={{0,1},{1,0},{2,3},{3,2},{4,5},{5,4},{6,7},{7,6},{8,9},{9,8},{10,11... | collective-permute-start | bytes 6152 | tf_op jit(solution)/shard_map/ppermute | solution.py:537
  74.4 0.0 collective-permute-start.2
  74.4 10.0 %collective-permute-done.1.far = bf16[16,64]{1,0:T(8,128)(2,1)S(1)} collective-permute-done((bf16[16,64]{1,0:T(8,128)(2,1)S(1)}, bf16[16,64]{1,0:T(8,128)(2,1)S(1)}, u32[]{:S(2)}, u32[]{:S(2)}) %collective-permute-start.1) | collective-permute-done | bytes 2080 | tf_op jit(solution)/shard_map/ppermute | solution.py:537
  84.4 0.0 collective-permute-done.near
  84.4 1.2 %collective-permute-done.2.across = bf16[16,64]{1,0:T(8,128)(2,1)S(1)} collective-permute-done((bf16[16,64]{1,0:T(8,128)(2,1)S(1)}, bf16[16,64]{1,0:T(8,128)(2,1)S(1)}, u32[]{:S(2)}, u32[]{:S(2)}) %collective-permute-start.2) | collective-permute-done | bytes 2080 | tf_op jit(solution)/shard_map/ppermute | solution.py:537
  85.6 2.7 %all-to-all-done.1.values_ref = bf16[64,16,512]{2,1,0:T(8,128)(2,1)S(1)} async-done(((bf16[64,16,512]{2,1,0:T(8,128)(2,1)}), bf16[64,16,512]{2,1,0:T(8,128)(2,1)S(1)}, u32[]{:S(2)}, u32[]{:S(2)}) %all-to-all-start.1) | async-done | bytes 1048608 | tf_op jit(solution)/shard_map/all_to_all | solution.py:532
  88.3 0.9 shard_map.92
  89.2 2.1 %collective-permute-start.8 = (bf16[16,8192]{1,0:T(8,128)(2,1)S(1)}, bf16[16,8192]{1,0:T(8,128)(2,1)S(1)}, u32[]{:S(2)}, u32[]{:S(2)}) collective-permute-start(bf16[16,8192]{1,0:T(8,128)(2,1)S(1)} %get-tuple-element.35), channel_id=1, source_target_pairs={{0,1},{1,0},{2,3},{3,2},{4,5},{5,4},{6,7},{7,6},{8,9},{9,8},{10,11... | collective-permute-start | bytes 786440 | tf_op jit(solution)/shard_map/ppermute | solution.py:54
  91.3 0.0 copy-done
  91.3 0.8 shard_map.93.refs_0_
  92.1 0.3 collective-permute-done.8.update_ref
  92.5 0.8 shard_map.94
  (2 shorter events, 0.0 us)
Async XLA Ops:
  0.0 3.3 %copy-start.2 = (f32[2,3,16]{2,0,1:T(2,128)S(1)}, f32[2,3,16]{2,0,1:T(2,128)}, u32[]{:S(2)}) copy-start(f32[2,3,16]{2,0,1:T(2,128)} %param.11) | copy-start | bytes 1156
  1.8 4.2 %collective-permute-start.3 = (bf16[16,5,16,512]{3,2,1,0:T(8,128)(2,1)S(1)}, bf16[16,5,16,512]{3,2,1,0:T(8,128)(2,1)S(1)}, u32[]{:S(2)}, u32[]{:S(2)}) collective-permute-start(bf16[16,5,16,512]{3,2,1,0:T(8,128)(2,1)S(1)} %shard_map.82), channel_id=1, source_target_pairs={{0,1},{1,0},{2,3},{3,2},{4,5},{5,4},{6,7},{7,6},{8,9},{9,8},{10,11... | collective-permute-start | bytes 3932168 | tf_op jit(solution)/shard_map/ppermute | solution.py:54
  3.3 2.8 %collective-permute-start.4 = (f32[2,3,16]{2,1,0:T(4,128)S(1)}, f32[2,3,16]{2,1,0:T(4,128)S(1)}, u32[]{:S(2)}, u32[]{:S(2)}) collective-permute-start(f32[2,3,16]{2,1,0:T(4,128)S(1)} %copy.12.own_taps), channel_id=1, source_target_pairs={{0,1},{1,0},{2,3},{3,2},{4,5},{5,4},{6,7},{7,6},{8,9},{9,8},{10,11... | collective-permute-start | bytes 1160 | tf_op jit(solution)/shard_map/ppermute | solution.py:54
  47.7 3.8 %collective-permute-start.5 = (bf16[32,16,512]{2,1,0:T(8,128)(2,1)S(1)}, bf16[32,16,512]{2,1,0:T(8,128)(2,1)S(1)}, u32[]{:S(2)}, u32[]{:S(2)}) collective-permute-start(bf16[32,16,512]{2,1,0:T(8,128)(2,1)S(1)} %shard_map.85.own), channel_id=1, source_target_pairs={{0,1},{1,0},{2,3},{3,2},{4,5},{5,4},{6,7},{7,6},{8,9},{9,8},{10,11... | collective-permute-start | bytes 1572872 | tf_op jit(solution)/shard_map/ppermute | solution.py:54
  54.1 2.9 %collective-permute-start.6 = (bf16[2,32,16,512]{3,2,1,0:T(8,128)(2,1)S(1)}, bf16[2,32,16,512]{3,2,1,0:T(8,128)(2,1)}, u32[]{:S(2)}, u32[]{:S(2)}) collective-permute-start(bf16[2,32,16,512]{3,2,1,0:T(8,128)(2,1)S(1)} %shard_map.89.mine), channel_id=1, source_target_pairs={{0,1},{1,0},{2,3},{3,2},{4,5},{5,4},{6,7},{7,6},{8,9},{9,8},{10,11... | collective-permute-start | bytes 3145736 | tf_op jit(solution)/shard_map/ppermute | solution.py:54
  60.9 2.0 %collective-permute-start.7 = (bf16[32,16,512]{2,1,0:T(8,128)(2,1)S(1)}, bf16[32,16,512]{2,1,0:T(8,128)(2,1)S(1)}, u32[]{:S(2)}, u32[]{:S(2)}) collective-permute-start(bf16[32,16,512]{2,1,0:T(8,128)(2,1)S(1)} %get-tuple-element.34), channel_id=1, source_target_pairs={{0,1},{1,0},{2,3},{3,2},{4,5},{5,4},{6,7},{7,6},{8,9},{9,8},{10,11... | collective-permute-start | bytes 1572872 | tf_op jit(solution)/shard_map/ppermute | solution.py:54
  62.9 7.7 %copy-start.1 = (bf16[16,64]{1,0:T(8,128)(2,1)S(1)}, bf16[16,64]{1,0:T(8,128)(2,1)}, u32[]{:S(2)}) copy-start(bf16[16,64]{1,0:T(8,128)(2,1)} %own.1) | copy-start | bytes 6148
  63.9 27.4 %copy-start = (bf16[16,16384]{1,0:T(8,128)(2,1)S(1)}, bf16[16,16384]{1,0:T(8,128)(2,1)}, u32[]{:S(2)}) copy-start(bf16[16,16384]{1,0:T(8,128)(2,1)} %second_ref.3) | copy-start | bytes 1572868
  63.9 24.4 %all-to-all-start.1 = ((bf16[64,16,512]{2,1,0:T(8,128)(2,1)}), bf16[64,16,512]{2,1,0:T(8,128)(2,1)S(1)}, u32[]{:S(2)}, u32[]{:S(2)}) async-start(bf16[64,16,512]{2,1,0:T(8,128)(2,1)} %bitcast.2), calls=%async_computation.1 | async-start | bytes 2097152 | tf_op jit(solution)/shard_map/all_to_all | solution.py:532
  70.5 13.9 %collective-permute-start.1 = (bf16[16,64]{1,0:T(8,128)(2,1)S(1)}, bf16[16,64]{1,0:T(8,128)(2,1)S(1)}, u32[]{:S(2)}, u32[]{:S(2)}) collective-permute-start(bf16[16,64]{1,0:T(8,128)(2,1)S(1)} %copy-done.1), channel_id=1, source_target_pairs={{0,2},{1,3},{2,0},{3,1},{4,6},{5,7},{6,4},{7,5},{8,10},{9,11},{10,... | collective-permute-start | bytes 6152 | tf_op jit(solution)/shard_map/ppermute | solution.py:537
  73.2 11.2 %collective-permute-start = (bf16[16,64]{1,0:T(8,128)(2,1)S(1)}, bf16[16,64]{1,0:T(8,128)(2,1)S(1)}, u32[]{:S(2)}, u32[]{:S(2)}) collective-permute-start(bf16[16,64]{1,0:T(8,128)(2,1)S(1)} %copy-done.1), channel_id=1, source_target_pairs={{0,1},{1,0},{2,3},{3,2},{4,5},{5,4},{6,7},{7,6},{8,9},{9,8},{10,11... | collective-permute-start | bytes 6152 | tf_op jit(solution)/shard_map/ppermute | solution.py:537
  74.4 11.2 %collective-permute-start.2 = (bf16[16,64]{1,0:T(8,128)(2,1)S(1)}, bf16[16,64]{1,0:T(8,128)(2,1)S(1)}, u32[]{:S(2)}, u32[]{:S(2)}) collective-permute-start(bf16[16,64]{1,0:T(8,128)(2,1)S(1)} %copy-done.1), channel_id=1, source_target_pairs={{0,3},{1,2},{2,1},{3,0},{4,7},{5,6},{6,5},{7,4},{8,11},{9,10},{10,... | collective-permute-start | bytes 6152 | tf_op jit(solution)/shard_map/ppermute | solution.py:537
  89.2 3.3 %collective-permute-start.8 = (bf16[16,8192]{1,0:T(8,128)(2,1)S(1)}, bf16[16,8192]{1,0:T(8,128)(2,1)S(1)}, u32[]{:S(2)}, u32[]{:S(2)}) collective-permute-start(bf16[16,8192]{1,0:T(8,128)(2,1)S(1)} %get-tuple-element.35), channel_id=1, source_target_pairs={{0,1},{1,0},{2,3},{3,2},{4,5},{5,4},{6,7},{7,6},{8,9},{9,8},{10,11... | collective-permute-start | bytes 786440 | tf_op jit(solution)/shard_map/ppermute | solution.py:54

commit v5 on v4

--- a/solution.py
+++ b/solution.py
@@ -301,21 +301,20 @@
 ]
 
 
-def convolve(core, gain, forward, wave, twist, own_ref, other_ref, folded, mid, total, back, ready=lambda: None):
+def convolve(core, gain, forward, wave, twist, other_ref, folded, mid, total, back):
     outer_forward(core, folded, forward, twist, total, mid)
-    ready()
     inner(mid, wave, total, 1)
     times_filter(total, gain, mid)
     inner(mid, wave, total, -1)
     untwist(core, total, twist, back)
     outer_backward(forward, back, other_ref, 1)
-    outer_backward(forward, back, own_ref, 0)
-
-
-def first_conv_kernel(core_ref, own, other, gain, forward, wave, twist, out_ref, folded, *scratch):
+
+
+def first_conv_kernel(core_ref, own, other, gain, forward, wave, twist, out_ref, folded, mid, total, back):
     fold_time(own, folded, 0)
     fold_time(other, folded, 1)
-    convolve(core_ref[0], gain, forward, wave, twist, out_ref.at[0], out_ref.at[1], folded, *scratch)
+    convolve(core_ref[0], gain, forward, wave, twist, out_ref.at[1], folded, mid, total, back)
+    outer_backward(forward, back, out_ref.at[0], 0)
 
 
 def first_conv(core, own, other, *rest):
@@ -352,37 +351,37 @@
     return (taps[0] * tiles[0] + taps[1] * tiles[1] + taps[2] * tiles[2]).astype(BF)
 
 
-def gates_kernel(index, core_ref, seat_ref, own_taps, near_taps, own, other, *refs):
+def gates_kernel(core_ref, seat_ref, own_taps, near_taps, own, other, *refs):
     core = core_ref[0]
-    taps = taps_of(index, core, seat_ref, own_taps, near_taps)
-    if index == 0:
-        wave_hbm, twist_hbm, *outs, wave, twist, sems = refs
+    taps = [taps_of(index, core, seat_ref, own_taps, near_taps) for index in range(2)]
+    first_own, first_other, second_own = refs[2:5] if len(refs) > 3 else refs
+    loads = []
+    if len(refs) > 3:
+        wave_hbm, twist_hbm, *_, wave, twist, sems = refs
         loads = [fetch(twist_hbm.at[core], twist, sems, 0), fetch(wave_hbm, wave, sems, 1)]
-    else:
-        outs, loads = refs, []
 
     @pl.loop(0, BLOCKS, unroll=8)
     def _(block):
         last = (block + BLOCKS - 1) % BLOCKS
         ahead = other[jnp.where(core == 0, last, block), :, N2 - LANES:].astype(F32)
-        outs[0][block] = gate(taps, lagged(own[block].astype(F32), ahead))
-        if len(outs) > 1:
-            ahead = own[jnp.where(core == 0, block, last), :, N2 - LANES:].astype(F32)
-            outs[1][block] = gate(taps, lagged(other[block].astype(F32), ahead))
+        tiles = lagged(own[block].astype(F32), ahead)
+        first_own[block] = gate(taps[0], tiles)
+        second_own[block] = gate(taps[1], tiles)
+        ahead = own[jnp.where(core == 0, block, last), :, N2 - LANES:].astype(F32)
+        first_other[block] = gate(taps[0], lagged(other[block].astype(F32), ahead))
 
     for load in loads:
         load.wait()
 
 
-def gates(index, core, seat, taps, near_taps, own, other, *tables):
-    count = 2 if index == 0 else 1
+def gates(core, seat, taps, near_taps, own, other, *tables):
     field = jax.ShapeDtypeStruct((BLOCKS, TILE, N2), BF)
     brought = [jax.ShapeDtypeStruct((N2, 2 * N2), BF), jax.ShapeDtypeStruct((2, ROWS, N2), BF)] if tables else []
     return pl.pallas_call(
-        functools.partial(gates_kernel, index),
+        gates_kernel,
         in_specs=[SMEM] * 4 + [VMEM, VMEM] + [ANY] * len(tables),
-        out_specs=(VMEM,) * (count + len(tables)),
-        out_shape=[field] * count + brought,
+        out_specs=(VMEM,) * (3 + len(tables)),
+        out_shape=[field] * 3 + brought,
         scratch_shapes=[pltpu.SemaphoreType.DMA((2,))] if tables else [],
         compiler_params=params(4),
         cost_estimate=cost(0, 0),
@@ -390,14 +389,14 @@
 
 
 def second_conv_kernel(
-    core_ref, gate_own, gate_other, mine, gain, forward, wave, twist, theirs_any, own_ref, other_ref, theirs, sems, folded,
-    *scratch,
+    core_ref, gate_own, gate_other, mine, gain, forward, wave, twist, theirs_any, other_ref, back, theirs, sems, folded,
+    mid, total,
 ):
     loads = [fetch(theirs_any.at[1 - place], theirs.at[place], sems, place) for place in range(2)]
     for place, gate_ref in enumerate((gate_own, gate_other)):
         loads[place].wait()
         fold_time(gate_ref[...] * (mine[place] + theirs[place]), folded, place)
-    convolve(core_ref[0], gain, forward, wave, twist, own_ref, other_ref, folded, *scratch)
+    convolve(core_ref[0], gain, forward, wave, twist, other_ref, folded, mid, total, back)
 
 
 def second_conv(core, gate, mine, theirs, gain, forward, wave, twist):
@@ -405,11 +404,30 @@
         second_conv_kernel,
         in_specs=[SMEM] + [VMEM] * 7 + [ANY],
         out_specs=(VMEM, VMEM),
-        out_shape=(jax.ShapeDtypeStruct((BLOCKS, TILE, N2), BF),) * 2,
-        scratch_shapes=[pltpu.VMEM((2, BLOCKS, TILE, N2), BF), pltpu.SemaphoreType.DMA((2,))] + CONV_SCRATCH,
+        out_shape=(
+            jax.ShapeDtypeStruct((BLOCKS, TILE, N2), BF), jax.ShapeDtypeStruct((2 * HALF, N2), BF),
+        ),
+        scratch_shapes=[
+            pltpu.VMEM((2, BLOCKS, TILE, N2), BF), pltpu.SemaphoreType.DMA((2,)), *CONV_SCRATCH[:3],
+        ],
         compiler_params=params(8),
         cost_estimate=cost(0, 0),
     )(core, *gate, mine, gain, forward, wave, twist, theirs)
+
+
+def own_half_kernel(forward, back, out_ref):
+    outer_backward(forward, back, out_ref, 0)
+
+
+def own_half(forward, back):
+    return pl.pallas_call(
+        own_half_kernel,
+        in_specs=[VMEM, VMEM],
+        out_specs=VMEM,
+        out_shape=jax.ShapeDtypeStruct((BLOCKS, TILE, N2), BF),
+        compiler_params=params(4),
+        cost_estimate=cost(0, 0),
+    )(forward, back)
 
 
 def last_kernel(gate_ref, keep_ref, theirs_ref, out_ref, last, sems):
@@ -523,10 +541,10 @@
     gain, second_gain, wave_now, twist_now = fold(core, got, wave, twist)
     mine = first_conv(core, own, other, gain, forward, wave_now, twist_now)
     theirs = swap(mine)
-    *gate_all, wave, twist = gates(0, core, seat, short_taps, near_taps, own, other, wave, twist)
-    keep, send = second_conv(core, gate_all, mine, theirs, second_gain, forward, wave, twist)
+    *gate_all, gate_own, wave, twist = gates(core, seat, short_taps, near_taps, own, other, wave, twist)
+    send, back = second_conv(core, gate_all, mine, theirs, second_gain, forward, wave, twist)
     theirs = swap(send)
-    gate_own, = gates(1, core, seat, short_taps, near_taps, own, other)
+    keep = own_half(forward, back)
     spread = last_gate(gate_own, keep, theirs)
     members = [[4 * j + 2 * high + side for high in range(2) for j in range(BLOCKS)] for side in range(2)]
     values = lax.all_to_all(

time: 93.7 us -> 93.5 us (level)
  Pallas kernels: 18.6 us -> 17.5 us
    ppermute x6, waiting for transfers between devices: 1.68 us -> 2.67 us  [swap(): lax.ppermute(value, 'ch', [(i, i ^ 1) for i in range(lax.axis_size('ch'))])]
    pallas_call x2, Pallas kernels: 3.42 us -> 2.43 us  [the longest x1 2.09 us: gates(): pl.pallas_call(gates_kernel, in_specs=[SMEM] * 4 + [VMEM, VMEM] + [ANY] *...]
  transfers between devices with their start and end apart: 10 -> 10, of which waited for: 8 -> 8; matrix products, arithmetic and copies ran while one was open for 0% -> 0% of each run, Pallas kernels for 8% -> 7%
where the time goes in v5:
time: 93.5 us; the launch traced here: 93.2 us
  blocking collectives  41.6 us (44%)
  Pallas kernels  17.5 us (19%)
  starting transfers between devices  17.4 us (19%)
  waiting for transfers between devices  16.5 us (18%)
    all_to_all x1, blocking collectives, on_device(): got = lax.all_to_all(buffer, 'seq', split_axis=0, concat_axis=0, tiled=True)  41.6 us
    ppermute x3, waiting for transfers between devices, on_device(): lax.ppermute(mixing, 'ch', [(i, i ^ apart) for i in range(4)])  11.1 us
    ppermute x6, starting transfers between devices, swap(): lax.ppermute(value, 'ch', [(i, i ^ 1) for i in range(lax.axis_size('ch'))])  6.88 us
    all_to_all x1, starting transfers between devices, on_device(): lax.all_to_all(spread.reshape(2 * BLOCKS, TILE, N2), ('seq', 'ch'), split...  6.57 us
    ppermute x3, starting transfers between devices, on_device(): lax.ppermute(mixing, 'ch', [(i, i ^ apart) for i in range(4)])  3.96 us
    pallas_call x1, Pallas kernels, second_conv(): pl.pallas_call(second_conv_kernel, in_specs=[SMEM] + [VMEM] * 7 + [ANY],...  3.72 us
    pallas_call x2, Pallas kernels, split(): pl.pallas_call(functools.partial(split_kernel, keep), in_specs=[SMEM, ANY...  3.6 us
    all_to_all x1, waiting for transfers between devices, on_device(): lax.all_to_all(spread.reshape(2 * BLOCKS, TILE, N2), ('seq', 'ch'), split...  2.68 us
  transfers between devices with their start and end apart: 10, of which 8 were waited for; matrix products, arithmetic and copies ran while one was open for 0% of the time, Pallas kernels for 7%

profile of v5, /device:TPU:1, one launch (start us, length us, event | category | flops | bytes accessed | tf_op | source)
XLA Modules:
  0.0 93.2 jit_solution(8380780120327556408)
XLA Ops:
  0.0 0.0 copy-start.2
  0.0 1.8 %shard_map.82 = bf16[16,5,16,512]{3,2,1,0:T(8,128)(2,1)S(1)} custom-call(s32[1]{0:T(128)S(6)} %select_n.7.core_ref, bf16[16,16384]{1,0:T(8,128)(2,1)} %signal_ref.3, bf16[2,2,16,16384]{3,2,1,0:T(8,128)(2,1)} %filter_ref.3), custom_call_target="tpu_custom_call" | custom-call | bytes 8388608 | tf_op jit(solution)/shard_map/pallas_call | solution.py:129
  1.8 1.5 %collective-permute-start.3 = (bf16[16,5,16,512]{3,2,1,0:T(8,128)(2,1)S(1)}, bf16[16,5,16,512]{3,2,1,0:T(8,128)(2,1)S(1)}, u32[]{:S(2)}, u32[]{:S(2)}) collective-permute-start(bf16[16,5,16,512]{3,2,1,0:T(8,128)(2,1)S(1)} %shard_map.82), channel_id=1, source_target_pairs={{0,1},{1,0},{2,3},{3,2},{4,5},{5,4},{6,7},{7,6},{8,9},{9,8},{10,11... | collective-permute-start | bytes 3932168 | tf_op jit(solution)/shard_map/ppermute | solution.py:54
  3.3 0.0 copy-done.2
  3.3 0.1 collective-permute-start.4
  3.4 1.8 %shard_map.83 = (bf16[32,5,16,512]{3,2,1,0:T(8,128)(2,1)S(1)}, bf16[512,512]{1,0:T(8,128)(2,1)S(1)}) custom-call(s32[1]{0:T(128)S(6)} %select_n.7.core_ref, bf16[16,16384]{1,0:T(8,128)(2,1)} %signal_ref.3, bf16[2,2,16,16384]{3,2,1,0:T(8,128)(2,1)} %filter_ref.3, bf16[2,512,512]{2,1,0:T(8,128)(2,1)} %constant.34.clone.refs_0_), custom_call_target="tpu_custom_call" | custom-call | bytes 8388608 | tf_op jit(solution)/shard_map/pallas_call | solution.py:129
  5.2 0.7 collective-permute-done.3.piece_ref
  6.0 0.1 shard_map.84
  6.1 0.0 collective-permute-done.4.near_taps
  6.1 41.6 %all_to_all.10.got_ref = bf16[32,5,16,512]{3,2,1,0:T(8,128)(2,1)S(1)} all-to-all(bf16[32,5,16,512]{3,2,1,0:T(8,128)(2,1)S(1)} %shard_map.84), channel_id=1, replica_groups=mesh['seq'=32,'ch'=4] {'seq'}, dimensions={0} | all-to-all | bytes 5242880 | tf_op jit(solution)/shard_map/all_to_all | solution.py:537
  47.7 2.3 %collective-permute-start.5 = (bf16[32,16,512]{2,1,0:T(8,128)(2,1)S(1)}, bf16[32,16,512]{2,1,0:T(8,128)(2,1)S(1)}, u32[]{:S(2)}, u32[]{:S(2)}) collective-permute-start(bf16[32,16,512]{2,1,0:T(8,128)(2,1)S(1)} %shard_map.85.own), channel_id=1, source_target_pairs={{0,1},{1,0},{2,3},{3,2},{4,5},{5,4},{6,7},{7,6},{8,9},{9,8},{10,11... | collective-permute-start | bytes 1572872 | tf_op jit(solution)/shard_map/ppermute | solution.py:54
  50.0 1.4 %shard_map.87 = (bf16[2,272,512]{2,1,0:T(8,128)(2,1)S(1)}, bf16[2,272,512]{2,1,0:T(8,128)(2,1)S(1)}, bf16[512,1024]{1,0:T(8,128)(2,1)S(1)}, bf16[2,272,512]{2,1,0:T(8,128)(2,1)S(1)}) custom-call(s32[1]{0:T(128)S(6)} %select_n.7.core_ref, bf16[32,5,16,512]{3,2,1,0:T(8,128)(2,1)S(1)} %all_to_all.10.got_ref, bf16[512,1024]{1,0:T(8,128)(2,1)} %constant.35.clone.refs_0_.wave_hbm, ...), custom_call_target="tpu_custom_call" | custom-call | tf_op jit(solution)/shard_map/pallas_call | solution.py:209
  51.4 0.1 collective-permute-done.5.other
  51.5 2.6 %shard_map.88.mine = bf16[2,32,16,512]{3,2,1,0:T(8,128)(2,1)S(1)} custom-call(s32[1]{0:T(128)S(6)} %select_n.7.core_ref, bf16[32,16,512]{2,1,0:T(8,128)(2,1)S(1)} %shard_map.85.own, bf16[32,16,512]{2,1,0:T(8,128)(2,1)S(1)} %collective-permute-done.5.other, bf16[2,272,512]{2,1,0:T(8,128)(2,1)S(1)} %get-tuple-element.29.gain, ...), custom_call_target="tpu_custom_call" | custom-call | tf_op jit(solution)/shard_map/pallas_call | solution.py:321
  54.1 0.5 collective-permute-start.6
  54.6 2.1 %shard_map.86 = (bf16[32,16,512]{2,1,0:T(8,128)(2,1)S(1)}, bf16[32,16,512]{2,1,0:T(8,128)(2,1)S(1)}, bf16[32,16,512]{2,1,0:T(8,128)(2,1)S(1)}, bf16[512,1024]{1,0:T(8,128)(2,1)S(1)}, bf16[2,272,512]{2,1,0:T(8,128)(2,1)S(1)}) custom-call(s32[1]{0:T(128)S(6)} %select_n.7.core_ref, s32[1]{0:T(128)} %bitcast.1.seat_ref, f32[2,3,16]{2,1,0:T(4,128)S(1)} %copy.12.own_taps, ...), custom_call_target="tpu_custom_call" | custom-call | tf_op jit(solution)/shard_map/pallas_call | solution.py:380
  56.7 0.3 collective-permute-done.6.theirs_any
  57.0 3.7 %shard_map.89 = (bf16[32,16,512]{2,1,0:T(8,128)(2,1)S(1)}, bf16[512,512]{1,0:T(8,128)(2,1)S(1)}) custom-call(s32[1]{0:T(128)S(6)} %select_n.7.core_ref, bf16[32,16,512]{2,1,0:T(8,128)(2,1)S(1)} %get-tuple-element.27.gate_own, bf16[32,16,512]{2,1,0:T(8,128)(2,1)S(1)} %get-tuple-element.28.gate_other, bf16[2,32,16,512]{3,2,1,0:T(8,128)(2,1)S(1)} %shard_map.88.mine, ...), custom_call_target="tpu_custom_call" | custom-call | tf_op jit(solution)/shard_map/pallas_call | solution.py:403
  60.7 0.5 collective-permute-start.7
  61.2 0.3 shard_map.90.keep_ref
  61.5 1.2 %collective-permute-done.7.theirs_ref = bf16[32,16,512]{2,1,0:T(8,128)(2,1)S(1)} collective-permute-done((bf16[32,16,512]{2,1,0:T(8,128)(2,1)S(1)}, bf16[32,16,512]{2,1,0:T(8,128)(2,1)S(1)}, u32[]{:S(2)}, u32[]{:S(2)}) %collective-permute-start.7) | collective-permute-done | bytes 524320 | tf_op jit(solution)/shard_map/ppermute | solution.py:54
  62.7 0.0 copy-start.1
  62.7 1.0 %shard_map.91 = bf16[2,32,16,512]{3,2,1,0:T(8,128)(2,1)} custom-call(bf16[32,16,512]{2,1,0:T(8,128)(2,1)S(1)} %get-tuple-element.25.gate_ref, bf16[32,16,512]{2,1,0:T(8,128)(2,1)S(1)} %shard_map.90.keep_ref, bf16[32,16,512]{2,1,0:T(8,128)(2,1)S(1)} %collective-permute-done.7.theirs_ref), custom_call_target="tpu_custom_call" | custom-call | tf_op jit(solution)/shard_map/pallas_call | solution.py:445
  63.8 0.0 copy-start
  63.8 6.6 %all-to-all-start.1 = ((bf16[64,16,512]{2,1,0:T(8,128)(2,1)}), bf16[64,16,512]{2,1,0:T(8,128)(2,1)S(1)}, u32[]{:S(2)}, u32[]{:S(2)}) async-start(bf16[64,16,512]{2,1,0:T(8,128)(2,1)} %bitcast.2), calls=%async_computation.1 | async-start | bytes 2097152 | tf_op jit(solution)/shard_map/all_to_all | solution.py:550
  70.4 0.0 copy-done.1
  70.4 0.7 collective-permute-start
  71.1 2.9 %collective-permute-start.1 = (bf16[16,64]{1,0:T(8,128)(2,1)S(1)}, bf16[16,64]{1,0:T(8,128)(2,1)S(1)}, u32[]{:S(2)}, u32[]{:S(2)}) collective-permute-start(bf16[16,64]{1,0:T(8,128)(2,1)S(1)} %copy-done.1), channel_id=1, source_target_pairs={{0,2},{1,3},{2,0},{3,1},{4,6},{5,7},{6,4},{7,5},{8,10},{9,11},{10,... | collective-permute-start | bytes 6152 | tf_op jit(solution)/shard_map/ppermute | solution.py:555
  74.0 0.3 collective-permute-start.2
  74.3 0.0 collective-permute-done.near
  74.3 9.9 %collective-permute-done.1.far = bf16[16,64]{1,0:T(8,128)(2,1)S(1)} collective-permute-done((bf16[16,64]{1,0:T(8,128)(2,1)S(1)}, bf16[16,64]{1,0:T(8,128)(2,1)S(1)}, u32[]{:S(2)}, u32[]{:S(2)}) %collective-permute-start.1) | collective-permute-done | bytes 2080 | tf_op jit(solution)/shard_map/ppermute | solution.py:555
  84.3 1.2 %collective-permute-done.2.across = bf16[16,64]{1,0:T(8,128)(2,1)S(1)} collective-permute-done((bf16[16,64]{1,0:T(8,128)(2,1)S(1)}, bf16[16,64]{1,0:T(8,128)(2,1)S(1)}, u32[]{:S(2)}, u32[]{:S(2)}) %collective-permute-start.2) | collective-permute-done | bytes 2080 | tf_op jit(solution)/shard_map/ppermute | solution.py:555
  85.5 2.7 %all-to-all-done.1.values_ref = bf16[64,16,512]{2,1,0:T(8,128)(2,1)S(1)} async-done(((bf16[64,16,512]{2,1,0:T(8,128)(2,1)}), bf16[64,16,512]{2,1,0:T(8,128)(2,1)S(1)}, u32[]{:S(2)}, u32[]{:S(2)}) %all-to-all-start.1) | async-done | bytes 1048608 | tf_op jit(solution)/shard_map/all_to_all | solution.py:550
  88.2 0.9 shard_map.92
  89.0 2.1 %collective-permute-start.8 = (bf16[16,8192]{1,0:T(8,128)(2,1)S(1)}, bf16[16,8192]{1,0:T(8,128)(2,1)S(1)}, u32[]{:S(2)}, u32[]{:S(2)}) collective-permute-start(bf16[16,8192]{1,0:T(8,128)(2,1)S(1)} %get-tuple-element.37), channel_id=1, source_target_pairs={{0,1},{1,0},{2,3},{3,2},{4,5},{5,4},{6,7},{7,6},{8,9},{9,8},{10,11... | collective-permute-start | bytes 786440 | tf_op jit(solution)/shard_map/ppermute | solution.py:54
  91.2 0.0 copy-done
  91.2 0.8 shard_map.93.refs_0_
  92.0 0.3 collective-permute-done.8.update_ref
  92.3 0.8 shard_map.94
  (2 shorter events, 0.0 us)
Async XLA Ops:
  0.0 3.3 %copy-start.2 = (f32[2,3,16]{2,0,1:T(2,128)S(1)}, f32[2,3,16]{2,0,1:T(2,128)}, u32[]{:S(2)}) copy-start(f32[2,3,16]{2,0,1:T(2,128)} %param.11) | copy-start | bytes 1156
  1.8 4.2 %collective-permute-start.3 = (bf16[16,5,16,512]{3,2,1,0:T(8,128)(2,1)S(1)}, bf16[16,5,16,512]{3,2,1,0:T(8,128)(2,1)S(1)}, u32[]{:S(2)}, u32[]{:S(2)}) collective-permute-start(bf16[16,5,16,512]{3,2,1,0:T(8,128)(2,1)S(1)} %shard_map.82), channel_id=1, source_target_pairs={{0,1},{1,0},{2,3},{3,2},{4,5},{5,4},{6,7},{7,6},{8,9},{9,8},{10,11... | collective-permute-start | bytes 3932168 | tf_op jit(solution)/shard_map/ppermute | solution.py:54
  3.3 2.8 %collective-permute-start.4 = (f32[2,3,16]{2,1,0:T(4,128)S(1)}, f32[2,3,16]{2,1,0:T(4,128)S(1)}, u32[]{:S(2)}, u32[]{:S(2)}) collective-permute-start(f32[2,3,16]{2,1,0:T(4,128)S(1)} %copy.12.own_taps), channel_id=1, source_target_pairs={{0,1},{1,0},{2,3},{3,2},{4,5},{5,4},{6,7},{7,6},{8,9},{9,8},{10,11... | collective-permute-start | bytes 1160 | tf_op jit(solution)/shard_map/ppermute | solution.py:54
  47.7 3.8 %collective-permute-start.5 = (bf16[32,16,512]{2,1,0:T(8,128)(2,1)S(1)}, bf16[32,16,512]{2,1,0:T(8,128)(2,1)S(1)}, u32[]{:S(2)}, u32[]{:S(2)}) collective-permute-start(bf16[32,16,512]{2,1,0:T(8,128)(2,1)S(1)} %shard_map.85.own), channel_id=1, source_target_pairs={{0,1},{1,0},{2,3},{3,2},{4,5},{5,4},{6,7},{7,6},{8,9},{9,8},{10,11... | collective-permute-start | bytes 1572872 | tf_op jit(solution)/shard_map/ppermute | solution.py:54
  54.1 2.9 %collective-permute-start.6 = (bf16[2,32,16,512]{3,2,1,0:T(8,128)(2,1)S(1)}, bf16[2,32,16,512]{3,2,1,0:T(8,128)(2,1)}, u32[]{:S(2)}, u32[]{:S(2)}) collective-permute-start(bf16[2,32,16,512]{3,2,1,0:T(8,128)(2,1)S(1)} %shard_map.88.mine), channel_id=1, source_target_pairs={{0,1},{1,0},{2,3},{3,2},{4,5},{5,4},{6,7},{7,6},{8,9},{9,8},{10,11... | collective-permute-start | bytes 3145736 | tf_op jit(solution)/shard_map/ppermute | solution.py:54
  60.7 2.0 %collective-permute-start.7 = (bf16[32,16,512]{2,1,0:T(8,128)(2,1)S(1)}, bf16[32,16,512]{2,1,0:T(8,128)(2,1)S(1)}, u32[]{:S(2)}, u32[]{:S(2)}) collective-permute-start(bf16[32,16,512]{2,1,0:T(8,128)(2,1)S(1)} %get-tuple-element.36), channel_id=1, source_target_pairs={{0,1},{1,0},{2,3},{3,2},{4,5},{5,4},{6,7},{7,6},{8,9},{9,8},{10,11... | collective-permute-start | bytes 1572872 | tf_op jit(solution)/shard_map/ppermute | solution.py:54
  62.7 7.6 %copy-start.1 = (bf16[16,64]{1,0:T(8,128)(2,1)S(1)}, bf16[16,64]{1,0:T(8,128)(2,1)}, u32[]{:S(2)}) copy-start(bf16[16,64]{1,0:T(8,128)(2,1)} %own.1) | copy-start | bytes 6148
  63.8 27.4 %copy-start = (bf16[16,16384]{1,0:T(8,128)(2,1)S(1)}, bf16[16,16384]{1,0:T(8,128)(2,1)}, u32[]{:S(2)}) copy-start(bf16[16,16384]{1,0:T(8,128)(2,1)} %second_ref.3) | copy-start | bytes 1572868
  63.8 24.4 %all-to-all-start.1 = ((bf16[64,16,512]{2,1,0:T(8,128)(2,1)}), bf16[64,16,512]{2,1,0:T(8,128)(2,1)S(1)}, u32[]{:S(2)}, u32[]{:S(2)}) async-start(bf16[64,16,512]{2,1,0:T(8,128)(2,1)} %bitcast.2), calls=%async_computation.1 | async-start | bytes 2097152 | tf_op jit(solution)/shard_map/all_to_all | solution.py:550
  70.4 4.0 %collective-permute-start = (bf16[16,64]{1,0:T(8,128)(2,1)S(1)}, bf16[16,64]{1,0:T(8,128)(2,1)S(1)}, u32[]{:S(2)}, u32[]{:S(2)}) collective-permute-start(bf16[16,64]{1,0:T(8,128)(2,1)S(1)} %copy-done.1), channel_id=1, source_target_pairs={{0,1},{1,0},{2,3},{3,2},{4,5},{5,4},{6,7},{7,6},{8,9},{9,8},{10,11... | collective-permute-start | bytes 6152 | tf_op jit(solution)/shard_map/ppermute | solution.py:555
  71.1 13.2 %collective-permute-start.1 = (bf16[16,64]{1,0:T(8,128)(2,1)S(1)}, bf16[16,64]{1,0:T(8,128)(2,1)S(1)}, u32[]{:S(2)}, u32[]{:S(2)}) collective-permute-start(bf16[16,64]{1,0:T(8,128)(2,1)S(1)} %copy-done.1), channel_id=1, source_target_pairs={{0,2},{1,3},{2,0},{3,1},{4,6},{5,7},{6,4},{7,5},{8,10},{9,11},{10,... | collective-permute-start | bytes 6152 | tf_op jit(solution)/shard_map/ppermute | solution.py:555
  74.0 11.5 %collective-permute-start.2 = (bf16[16,64]{1,0:T(8,128)(2,1)S(1)}, bf16[16,64]{1,0:T(8,128)(2,1)S(1)}, u32[]{:S(2)}, u32[]{:S(2)}) collective-permute-start(bf16[16,64]{1,0:T(8,128)(2,1)S(1)} %copy-done.1), channel_id=1, source_target_pairs={{0,3},{1,2},{2,1},{3,0},{4,7},{5,6},{6,5},{7,4},{8,11},{9,10},{10,... | collective-permute-start | bytes 6152 | tf_op jit(solution)/shard_map/ppermute | solution.py:555
  89.0 3.3 %collective-permute-start.8 = (bf16[16,8192]{1,0:T(8,128)(2,1)S(1)}, bf16[16,8192]{1,0:T(8,128)(2,1)S(1)}, u32[]{:S(2)}, u32[]{:S(2)}) collective-permute-start(bf16[16,8192]{1,0:T(8,128)(2,1)S(1)} %get-tuple-element.37), channel_id=1, source_target_pairs={{0,1},{1,0},{2,3},{3,2},{4,5},{5,4},{6,7},{7,6},{8,9},{9,8},{10,11... | collective-permute-start | bytes 786440 | tf_op jit(solution)/shard_map/ppermute | solution.py:54

commit v6 on v4

--- a/solution.py
+++ b/solution.py
@@ -418,7 +418,9 @@
         blocks = slice(part * BLOCKS // parts, (part + 1) * BLOCKS // parts)
         last[blocks] = gate_ref[blocks] * (keep_ref[blocks] + theirs_ref[blocks])
         for high in range(2):
-            copies.append(fetch(last.at[blocks], out_ref.at[high, blocks], sems, 2 * part + high))
+            copies.append(
+                fetch(last.at[blocks, :, high * HALF:(high + 1) * HALF], out_ref.at[high, blocks], sems, 2 * part + high)
+            )
     for copy in copies:
         copy.wait()
 
@@ -428,14 +430,14 @@
         last_kernel,
         in_specs=[VMEM] * 3,
         out_specs=ANY,
-        out_shape=jax.ShapeDtypeStruct((2, BLOCKS, TILE, N2), BF),
+        out_shape=jax.ShapeDtypeStruct((2, BLOCKS, TILE, HALF), BF),
         scratch_shapes=[pltpu.VMEM((BLOCKS, TILE, N2), BF), pltpu.SemaphoreType.DMA((8,))],
         compiler_params=params(2),
         cost_estimate=cost(0, 0),
     )(gate, keep, theirs)
 
 
-def mix_kernel(group_ref, own, near, far, across, values_ref, keep_ref, send_ref, wide_ref):
+def mix_kernel(group_ref, own, near, far, across, values_ref, keep_ref, near_ref, far_ref, across_ref, wide_ref):
     channels = 2 * BLOCKS
     group = group_ref[0]
     places = [own[...], near[...], far[...], across[...]]
@@ -447,62 +449,58 @@
             chosen = jnp.where(apart == index, places[index], chosen)
         rows.append(chosen)
     whole = jnp.concatenate(rows, axis=0)
-    wanted = lax.broadcasted_iota(jnp.int32, (2 * TILE, 4 * TILE), 0)
-    wanted = jnp.where(wanted < TILE, wanted + group * TILE, wanted - TILE + (group ^ 1) * TILE)
-    picks = (lax.broadcasted_iota(jnp.int32, (2 * TILE, 4 * TILE), 1) == wanted).astype(F32).astype(BF)
+    row = lax.broadcasted_iota(jnp.int32, (channels, channels), 0)
+    wanted = ((row // TILE) ^ group) * TILE + row % TILE
+    picks = (lax.broadcasted_iota(jnp.int32, (channels, channels), 1) == wanted).astype(F32).astype(BF)
     weights = lax.dot_general(
         picks, whole, (((1,), (1,)), ((), ())), preferred_element_type=F32
     ).astype(BF)
-    for part in range(N2 // LANES):
+    for part in range(HALF // LANES):
         here = slice(part * LANES, (part + 1) * LANES)
         for start in range(0, channels, TILE):
             piece = values_ref[start:start + TILE, :, here].astype(F32)
             wide_ref[:, start:start + TILE, here] = jnp.swapaxes(piece, 0, 1).astype(BF)
     for row in range(TILE):
-        piece = wide_ref[row]
-        mixed = jnp.dot(weights, piece, preferred_element_type=F32)
-        keep_ref[:, row * N2:(row + 1) * N2] = mixed[:TILE]
-        send_ref[:, row * N2:(row + 1) * N2] = mixed[TILE:].astype(BF)
+        mixed = jnp.dot(weights, wide_ref[row], preferred_element_type=F32)
+        here = slice(row * HALF, (row + 1) * HALF)
+        keep_ref[:, here] = mixed[:TILE]
+        for index, out_ref in enumerate((near_ref, far_ref, across_ref)):
+            out_ref[:, here] = mixed[(index + 1) * TILE:(index + 2) * TILE].astype(BF)
 
 
 def mix(group, mixings, values):
-    width = TILE * N2
+    shape = (TILE, TILE * HALF)
     return pl.pallas_call(
         mix_kernel,
         in_specs=[SMEM] + [VMEM] * 5,
-        out_specs=(VMEM, VMEM),
-        out_shape=(jax.ShapeDtypeStruct((TILE, width), F32), jax.ShapeDtypeStruct((TILE, width), BF)),
-        scratch_shapes=[pltpu.VMEM((TILE, 2 * BLOCKS, N2), BF)],
-        compiler_params=params(5),
+        out_specs=(VMEM,) * 4,
+        out_shape=(jax.ShapeDtypeStruct(shape, F32),) + (jax.ShapeDtypeStruct(shape, BF),) * 3,
+        scratch_shapes=[pltpu.VMEM((TILE, 2 * BLOCKS, HALF), BF)],
+        compiler_params=params(8),
         cost_estimate=cost(0, 0),
     )(group, *mixings, values)
 
 
-def finish_kernel(other, core_ref, second_ref, update_ref, *refs):
-    out_ref, result, sems = refs[-3:]
-    parts, width = 4, TILE * N2
-    base = (1 - core_ref[0] if other else core_ref[0]) * width
-    copies = []
-    for part in range(parts):
-        here = slice(part * width // parts, (part + 1) * width // parts)
-        there = pl.ds(pl.multiple_of(base + part * width // parts, width // parts), width // parts)
-        result[:, here] = second_ref[:, there].astype(F32) - update_ref[:, here].astype(F32)
-        copies.append(fetch(result.at[:, here], out_ref.at[:, there], sems, part))
-    for copy in copies:
-        copy.wait()
-
-
-def finish(other, core, second, update, *out):
-    return pl.pallas_call(
-        functools.partial(finish_kernel, other),
-        in_specs=[SMEM, VMEM, VMEM] + [ANY] * len(out),
-        out_specs=ANY,
+def finish_kernel(group_ref, second_ref, *refs):
+    updates, out_ref = refs[:4], refs[4]
+    for apart, update_ref in enumerate(updates):
+        source = group_ref[0] ^ apart
+        base = (source % 2) * (TILE * N2) + (source // 2) * HALF
+        for row in range(TILE):
+            there = pl.ds(pl.multiple_of(base + row * N2, HALF), HALF)
+            update = update_ref[:, row * HALF:(row + 1) * HALF].astype(F32)
+            out_ref[:, there] = second_ref[:, there].astype(F32) - update
+
+
+def finish(group, second, updates):
+    return pl.pallas_call(
+        finish_kernel,
+        in_specs=[SMEM] + [VMEM] * 5,
+        out_specs=VMEM,
         out_shape=jax.ShapeDtypeStruct(second.shape, F32),
-        scratch_shapes=[pltpu.VMEM((TILE, TILE * N2), F32), pltpu.SemaphoreType.DMA((4,))],
-        input_output_aliases={3: 0} if other else {},
-        compiler_params=params(4),
-        cost_estimate=cost(0, 0),
-    )(core, second, update, *out)
+        compiler_params=params(6),
+        cost_estimate=cost(0, 0),
+    )(group, second, *updates)
 
 
 def on_device(coupled_first, coupled_second, spectra, short_taps, mixing):
@@ -530,16 +528,17 @@
     spread = last_gate(gate_own, keep, theirs)
     members = [[4 * j + 2 * high + side for high in range(2) for j in range(BLOCKS)] for side in range(2)]
     values = lax.all_to_all(
-        spread.reshape(2 * BLOCKS, TILE, N2), ("seq", "ch"), split_axis=0, concat_axis=0, tiled=True,
+        spread.reshape(2 * BLOCKS, TILE, HALF), ("seq", "ch"), split_axis=0, concat_axis=0, tiled=True,
         axis_index_groups=members,
     )
     near, far, across = (
         lax.ppermute(mixing, "ch", [(i, i ^ apart) for i in range(4)]) for apart in (1, 2, 3)
     )
-    keep, send = mix(group, (mixing, near, far, across), values)
-    theirs = swap(send)
-    out = finish(False, core, coupled_second, keep)
-    return finish(True, core, coupled_second, theirs, out)
+    keep, *sends = mix(group, (mixing, near, far, across), values)
+    theirs = [
+        lax.ppermute(value, "ch", [(i, i ^ (apart + 1)) for i in range(4)]) for apart, value in enumerate(sends)
+    ]
+    return finish(group, coupled_second, (keep, *theirs))
 
 
 def solution(mesh):

time: 93.7 us -> 96.1 us (1.026)
  starting transfers between devices: 17.4 us -> 20.2 us
  Pallas kernels: 18.6 us -> 17.5 us
    ppermute x0 -> x3, waiting for transfers between devices: none -> 6.32 us  [on_device(): lax.ppermute(value, 'ch', [(i, i ^ apart + 1) for i in range(4)])]
    ppermute x3, waiting for transfers between devices: 11.2 us -> 5.57 us  [on_device(): lax.ppermute(mixing, 'ch', [(i, i ^ apart) for i in range(4)])]
    ppermute x0 -> x3, starting transfers between devices: none -> 5.11 us  [on_device(): lax.ppermute(value, 'ch', [(i, i ^ apart + 1) for i in range(4)])]
    ppermute x6 -> x5, starting transfers between devices: 6.88 us -> 4.77 us  [swap(): lax.ppermute(value, 'ch', [(i, i ^ 1) for i in range(lax.axis_size('ch'))])]
  transfers between devices with their start and end apart: 10 -> 12, of which waited for: 8 -> 9; matrix products, arithmetic and copies ran while one was open for 0% -> 0% of each run, Pallas kernels for 8% -> 7%
where the time goes in v6:
time: 96.1 us; the launch traced here: 95.8 us
  blocking collectives  41.6 us (43%)
  starting transfers between devices  20.2 us (21%)
  Pallas kernels  17.5 us (18%)
  waiting for transfers between devices  16.3 us (17%)
    all_to_all x1, blocking collectives, on_device(): got = lax.all_to_all(buffer, 'seq', split_axis=0, concat_axis=0, tiled=True)  41.6 us
    all_to_all x1, starting transfers between devices, on_device(): lax.all_to_all(spread.reshape(2 * BLOCKS, TILE, HALF), ('seq', 'ch'), spl...  6.44 us
    ppermute x3, waiting for transfers between devices, on_device(): lax.ppermute(value, 'ch', [(i, i ^ apart + 1) for i in range(4)])  6.32 us
    ppermute x3, waiting for transfers between devices, on_device(): lax.ppermute(mixing, 'ch', [(i, i ^ apart) for i in range(4)])  5.57 us
    ppermute x3, starting transfers between devices, on_device(): lax.ppermute(value, 'ch', [(i, i ^ apart + 1) for i in range(4)])  5.11 us
    ppermute x5, starting transfers between devices, swap(): lax.ppermute(value, 'ch', [(i, i ^ 1) for i in range(lax.axis_size('ch'))])  4.77 us
    ppermute x3, starting transfers between devices, on_device(): lax.ppermute(mixing, 'ch', [(i, i ^ apart) for i in range(4)])  3.91 us
    pallas_call x1, Pallas kernels, second_conv(): pl.pallas_call(second_conv_kernel, in_specs=[SMEM] + [VMEM] * 7 + [ANY],...  3.85 us
  transfers between devices with their start and end apart: 12, of which 9 were waited for; matrix products, arithmetic and copies ran while one was open for 0% of the time, Pallas kernels for 7%

profile of v6, /device:TPU:1, one launch (start us, length us, event | category | flops | bytes accessed | tf_op | source)
XLA Modules:
  0.0 95.8 jit_solution(3101347653455190487)
XLA Ops:
  0.0 0.0 copy-start.2
  0.0 1.8 %shard_map.82 = bf16[16,5,16,512]{3,2,1,0:T(8,128)(2,1)S(1)} custom-call(s32[1]{0:T(128)S(6)} %select_n.7.core_ref, bf16[16,16384]{1,0:T(8,128)(2,1)} %signal_ref.3, bf16[2,2,16,16384]{3,2,1,0:T(8,128)(2,1)} %filter_ref.3), custom_call_target="tpu_custom_call" | custom-call | bytes 8388608 | tf_op jit(solution)/shard_map/pallas_call | solution.py:129
  1.8 1.5 %collective-permute-start.3 = (bf16[16,5,16,512]{3,2,1,0:T(8,128)(2,1)S(1)}, bf16[16,5,16,512]{3,2,1,0:T(8,128)(2,1)S(1)}, u32[]{:S(2)}, u32[]{:S(2)}) collective-permute-start(bf16[16,5,16,512]{3,2,1,0:T(8,128)(2,1)S(1)} %shard_map.82), channel_id=1, source_target_pairs={{0,1},{1,0},{2,3},{3,2},{4,5},{5,4},{6,7},{7,6},{8,9},{9,8},{10,11... | collective-permute-start | bytes 3932168 | tf_op jit(solution)/shard_map/ppermute | solution.py:54
  3.3 0.0 copy-done.2
  3.3 0.1 collective-permute-start.4
  3.4 1.8 %shard_map.83 = (bf16[32,5,16,512]{3,2,1,0:T(8,128)(2,1)S(1)}, bf16[512,512]{1,0:T(8,128)(2,1)S(1)}) custom-call(s32[1]{0:T(128)S(6)} %select_n.7.core_ref, bf16[16,16384]{1,0:T(8,128)(2,1)} %signal_ref.3, bf16[2,2,16,16384]{3,2,1,0:T(8,128)(2,1)} %filter_ref.3, bf16[2,512,512]{2,1,0:T(8,128)(2,1)} %constant.34.clone.refs_0_), custom_call_target="tpu_custom_call" | custom-call | bytes 8388608 | tf_op jit(solution)/shard_map/pallas_call | solution.py:129
  5.2 0.7 collective-permute-done.3.piece_ref
  6.0 0.1 shard_map.84
  6.1 0.0 collective-permute-done.4.near_taps
  6.1 41.6 %all_to_all.10.got_ref = bf16[32,5,16,512]{3,2,1,0:T(8,128)(2,1)S(1)} all-to-all(bf16[32,5,16,512]{3,2,1,0:T(8,128)(2,1)S(1)} %shard_map.84), channel_id=1, replica_groups=mesh['seq'=32,'ch'=4] {'seq'}, dimensions={0} | all-to-all | bytes 5242880 | tf_op jit(solution)/shard_map/all_to_all | solution.py:517
  47.7 2.3 %collective-permute-start.5 = (bf16[32,16,512]{2,1,0:T(8,128)(2,1)S(1)}, bf16[32,16,512]{2,1,0:T(8,128)(2,1)S(1)}, u32[]{:S(2)}, u32[]{:S(2)}) collective-permute-start(bf16[32,16,512]{2,1,0:T(8,128)(2,1)S(1)} %shard_map.85.own), channel_id=1, source_target_pairs={{0,1},{1,0},{2,3},{3,2},{4,5},{5,4},{6,7},{7,6},{8,9},{9,8},{10,11... | collective-permute-start | bytes 1572872 | tf_op jit(solution)/shard_map/ppermute | solution.py:54
  50.0 1.4 %shard_map.88 = (bf16[2,272,512]{2,1,0:T(8,128)(2,1)S(1)}, bf16[2,272,512]{2,1,0:T(8,128)(2,1)S(1)}, bf16[512,1024]{1,0:T(8,128)(2,1)S(1)}, bf16[2,272,512]{2,1,0:T(8,128)(2,1)S(1)}) custom-call(s32[1]{0:T(128)S(6)} %select_n.7.core_ref, bf16[32,5,16,512]{3,2,1,0:T(8,128)(2,1)S(1)} %all_to_all.10.got_ref, bf16[512,1024]{1,0:T(8,128)(2,1)} %constant.35.clone.refs_0_.wave_hbm, ...), custom_call_target="tpu_custom_call" | custom-call | tf_op jit(solution)/shard_map/pallas_call | solution.py:209
  51.4 0.1 collective-permute-done.5.other
  51.5 2.6 %shard_map.89.mine = bf16[2,32,16,512]{3,2,1,0:T(8,128)(2,1)S(1)} custom-call(s32[1]{0:T(128)S(6)} %select_n.7.core_ref, bf16[32,16,512]{2,1,0:T(8,128)(2,1)S(1)} %shard_map.85.own, bf16[32,16,512]{2,1,0:T(8,128)(2,1)S(1)} %collective-permute-done.5.other, bf16[2,272,512]{2,1,0:T(8,128)(2,1)S(1)} %get-tuple-element.28.gain, ...), custom_call_target="tpu_custom_call" | custom-call | tf_op jit(solution)/shard_map/pallas_call | solution.py:322
  54.1 0.5 collective-permute-start.6
  54.6 2.1 %shard_map.87 = (bf16[32,16,512]{2,1,0:T(8,128)(2,1)S(1)}, bf16[32,16,512]{2,1,0:T(8,128)(2,1)S(1)}, bf16[512,1024]{1,0:T(8,128)(2,1)S(1)}, bf16[2,272,512]{2,1,0:T(8,128)(2,1)S(1)}) custom-call(s32[1]{0:T(128)S(6)} %select_n.7.core_ref, s32[1]{0:T(128)} %bitcast.1.seat_ref, f32[2,3,16]{2,1,0:T(4,128)S(1)} %copy.11.own_taps, ...), custom_call_target="tpu_custom_call" | custom-call | tf_op jit(solution)/shard_map/pallas_call | solution.py:381
  56.7 0.3 collective-permute-done.6.theirs_any
  57.0 3.9 %shard_map.90 = (bf16[32,16,512]{2,1,0:T(8,128)(2,1)S(1)}, bf16[32,16,512]{2,1,0:T(8,128)(2,1)S(1)}) custom-call(s32[1]{0:T(128)S(6)} %select_n.7.core_ref, bf16[32,16,512]{2,1,0:T(8,128)(2,1)S(1)} %get-tuple-element.26.gate_own, bf16[32,16,512]{2,1,0:T(8,128)(2,1)S(1)} %get-tuple-element.27.gate_other, bf16[2,32,16,512]{3,2,1,0:T(8,128)(2,1)S(1)} %shard_map.89.mine, ...), custom_call_target="tpu_custom_call" | custom-call | tf_op jit(solution)/shard_map/pallas_call | solution.py:404
  60.9 0.0 copy-start.1
  60.9 0.5 collective-permute-start.7
  61.3 1.3 %shard_map.86.gate_ref = bf16[32,16,512]{2,1,0:T(8,128)(2,1)S(1)} custom-call(s32[1]{0:T(128)S(6)} %select_n.7.core_ref, s32[1]{0:T(128)} %bitcast.1.seat_ref, f32[2,3,16]{2,1,0:T(4,128)S(1)} %copy.11.own_taps, f32[2,3,16]{2,1,0:T(4,128)S(1)} %collective-permute-done.4.near_taps, bf16[32,16,512]{2,1,0:T(8,128)(2,1)S(1)} %shard_map.85.own, ...), custom_call_target="tpu_custom_call" | custom-call | tf_op jit(solution)/shard_map/pallas_call | solution.py:381
  62.7 0.0 copy-start
  62.7 0.2 collective-permute-done.7.theirs_ref
  62.9 0.9 shard_map.91
  63.7 6.4 %all-to-all-start.1 = ((bf16[64,16,256]{2,1,0:T(8,128)(2,1)}), bf16[64,16,256]{2,1,0:T(8,128)(2,1)S(1)}, u32[]{:S(2)}, u32[]{:S(2)}) async-start(bf16[64,16,256]{2,1,0:T(8,128)(2,1)} %bitcast.2), calls=%async_computation.1 | async-start | bytes 1048576 | tf_op jit(solution)/shard_map/all_to_all | solution.py:530
  70.2 0.0 copy-done.1
  70.2 2.7 %collective-permute-start.1 = (bf16[16,64]{1,0:T(8,128)(2,1)S(1)}, bf16[16,64]{1,0:T(8,128)(2,1)S(1)}, u32[]{:S(2)}, u32[]{:S(2)}) collective-permute-start(bf16[16,64]{1,0:T(8,128)(2,1)S(1)} %copy-done.1), channel_id=1, source_target_pairs={{0,2},{1,3},{2,0},{3,1},{4,6},{5,7},{6,4},{7,5},{8,10},{9,11},{10,... | collective-permute-start | bytes 6152 | tf_op jit(solution)/shard_map/ppermute | solution.py:535
  72.9 1.2 %collective-permute-start = (bf16[16,64]{1,0:T(8,128)(2,1)S(1)}, bf16[16,64]{1,0:T(8,128)(2,1)S(1)}, u32[]{:S(2)}, u32[]{:S(2)}) collective-permute-start(bf16[16,64]{1,0:T(8,128)(2,1)S(1)} %copy-done.1), channel_id=1, source_target_pairs={{0,1},{1,0},{2,3},{3,2},{4,5},{5,4},{6,7},{7,6},{8,9},{9,8},{10,11... | collective-permute-start | bytes 6152 | tf_op jit(solution)/shard_map/ppermute | solution.py:535
  74.1 0.0 collective-permute-start.2
  74.1 4.4 %collective-permute-done.1.far = bf16[16,64]{1,0:T(8,128)(2,1)S(1)} collective-permute-done((bf16[16,64]{1,0:T(8,128)(2,1)S(1)}, bf16[16,64]{1,0:T(8,128)(2,1)S(1)}, u32[]{:S(2)}, u32[]{:S(2)}) %collective-permute-start.1) | collective-permute-done | bytes 2080 | tf_op jit(solution)/shard_map/ppermute | solution.py:535
  78.5 0.0 collective-permute-done.near
  78.5 1.2 %collective-permute-done.2.across = bf16[16,64]{1,0:T(8,128)(2,1)S(1)} collective-permute-done((bf16[16,64]{1,0:T(8,128)(2,1)S(1)}, bf16[16,64]{1,0:T(8,128)(2,1)S(1)}, u32[]{:S(2)}, u32[]{:S(2)}) %collective-permute-start.2) | collective-permute-done | bytes 2080 | tf_op jit(solution)/shard_map/ppermute | solution.py:535
  79.7 3.0 %all-to-all-done.1.values_ref = bf16[64,16,256]{2,1,0:T(8,128)(2,1)S(1)} async-done(((bf16[64,16,256]{2,1,0:T(8,128)(2,1)}), bf16[64,16,256]{2,1,0:T(8,128)(2,1)S(1)}, u32[]{:S(2)}, u32[]{:S(2)}) %all-to-all-start.1) | async-done | bytes 524320 | tf_op jit(solution)/shard_map/all_to_all | solution.py:530
  82.7 0.5 shard_map.92
  83.2 1.9 %collective-permute-start.8 = (bf16[16,4096]{1,0:T(8,128)(2,1)S(1)}, bf16[16,4096]{1,0:T(8,128)(2,1)S(1)}, u32[]{:S(2)}, u32[]{:S(2)}) collective-permute-start(bf16[16,4096]{1,0:T(8,128)(2,1)S(1)} %get-tuple-element.38), channel_id=1, source_target_pairs={{0,1},{1,0},{2,3},{3,2},{4,5},{5,4},{6,7},{7,6},{8,9},{9,8},{10,11... | collective-permute-start | bytes 393224 | tf_op jit(solution)/shard_map/ppermute | solution.py:539
  85.1 0.7 collective-permute-start.9
  85.8 2.5 %collective-permute-start.10 = (bf16[16,4096]{1,0:T(8,128)(2,1)S(1)}, bf16[16,4096]{1,0:T(8,128)(2,1)S(1)}, u32[]{:S(2)}, u32[]{:S(2)}) collective-permute-start(bf16[16,4096]{1,0:T(8,128)(2,1)S(1)} %get-tuple-element.40), channel_id=1, source_target_pairs={{0,3},{1,2},{2,1},{3,0},{4,7},{5,6},{6,5},{7,4},{8,11},{9,10},{10,... | collective-permute-start | bytes 393224 | tf_op jit(solution)/shard_map/ppermute | solution.py:539
  88.3 0.0 collective-permute-done.8.refs_1_
  88.4 3.3 %collective-permute-done.9.refs_2_ = bf16[16,4096]{1,0:T(8,128)(2,1)S(1)} collective-permute-done((bf16[16,4096]{1,0:T(8,128)(2,1)S(1)}, bf16[16,4096]{1,0:T(8,128)(2,1)S(1)}, u32[]{:S(2)}, u32[]{:S(2)}) %collective-permute-start.9) | collective-permute-done | bytes 131104 | tf_op jit(solution)/shard_map/ppermute | solution.py:539
  91.7 3.0 %collective-permute-done.10.refs_3_ = bf16[16,4096]{1,0:T(8,128)(2,1)S(1)} collective-permute-done((bf16[16,4096]{1,0:T(8,128)(2,1)S(1)}, bf16[16,4096]{1,0:T(8,128)(2,1)S(1)}, u32[]{:S(2)}, u32[]{:S(2)}) %collective-permute-start.10) | collective-permute-done | bytes 131104 | tf_op jit(solution)/shard_map/ppermute | solution.py:539
  94.7 0.0 copy-done
  94.7 1.1 %shard_map.93 = f32[16,16384]{1,0:T(8,128)} custom-call(s32[1]{0:T(128)} %bitcast.group_ref, bf16[16,16384]{1,0:T(8,128)(2,1)S(1)} %copy-done, f32[16,4096]{1,0:T(8,128)S(1)} %get-tuple-element.37.refs_0_, bf16[16,4096]{1,0:T(8,128)(2,1)S(1)} %collective-permute-done.8.refs_1_, bf16[16,4096]{1,0:T(8,128)(2,1)S(1)} %collective-permute-done.9.refs_2_, ...), custom_call_target="tpu_custom_call" | custom-call | tf_op jit(solution)/shard_map/pallas_call | solution.py:496
  (2 shorter events, 0.0 us)
Async XLA Ops:
  0.0 3.3 %copy-start.2 = (f32[2,3,16]{2,0,1:T(2,128)S(1)}, f32[2,3,16]{2,0,1:T(2,128)}, u32[]{:S(2)}) copy-start(f32[2,3,16]{2,0,1:T(2,128)} %param.11) | copy-start | bytes 1156
  1.8 4.2 %collective-permute-start.3 = (bf16[16,5,16,512]{3,2,1,0:T(8,128)(2,1)S(1)}, bf16[16,5,16,512]{3,2,1,0:T(8,128)(2,1)S(1)}, u32[]{:S(2)}, u32[]{:S(2)}) collective-permute-start(bf16[16,5,16,512]{3,2,1,0:T(8,128)(2,1)S(1)} %shard_map.82), channel_id=1, source_target_pairs={{0,1},{1,0},{2,3},{3,2},{4,5},{5,4},{6,7},{7,6},{8,9},{9,8},{10,11... | collective-permute-start | bytes 3932168 | tf_op jit(solution)/shard_map/ppermute | solution.py:54
  3.3 2.8 %collective-permute-start.4 = (f32[2,3,16]{2,1,0:T(4,128)S(1)}, f32[2,3,16]{2,1,0:T(4,128)S(1)}, u32[]{:S(2)}, u32[]{:S(2)}) collective-permute-start(f32[2,3,16]{2,1,0:T(4,128)S(1)} %copy.11.own_taps), channel_id=1, source_target_pairs={{0,1},{1,0},{2,3},{3,2},{4,5},{5,4},{6,7},{7,6},{8,9},{9,8},{10,11... | collective-permute-start | bytes 1160 | tf_op jit(solution)/shard_map/ppermute | solution.py:54
  47.7 3.8 %collective-permute-start.5 = (bf16[32,16,512]{2,1,0:T(8,128)(2,1)S(1)}, bf16[32,16,512]{2,1,0:T(8,128)(2,1)S(1)}, u32[]{:S(2)}, u32[]{:S(2)}) collective-permute-start(bf16[32,16,512]{2,1,0:T(8,128)(2,1)S(1)} %shard_map.85.own), channel_id=1, source_target_pairs={{0,1},{1,0},{2,3},{3,2},{4,5},{5,4},{6,7},{7,6},{8,9},{9,8},{10,11... | collective-permute-start | bytes 1572872 | tf_op jit(solution)/shard_map/ppermute | solution.py:54
  54.1 2.9 %collective-permute-start.6 = (bf16[2,32,16,512]{3,2,1,0:T(8,128)(2,1)S(1)}, bf16[2,32,16,512]{3,2,1,0:T(8,128)(2,1)}, u32[]{:S(2)}, u32[]{:S(2)}) collective-permute-start(bf16[2,32,16,512]{3,2,1,0:T(8,128)(2,1)S(1)} %shard_map.89.mine), channel_id=1, source_target_pairs={{0,1},{1,0},{2,3},{3,2},{4,5},{5,4},{6,7},{7,6},{8,9},{9,8},{10,11... | collective-permute-start | bytes 3145736 | tf_op jit(solution)/shard_map/ppermute | solution.py:54
  60.9 9.3 %copy-start.1 = (bf16[16,64]{1,0:T(8,128)(2,1)S(1)}, bf16[16,64]{1,0:T(8,128)(2,1)}, u32[]{:S(2)}) copy-start(bf16[16,64]{1,0:T(8,128)(2,1)} %own.1) | copy-start | bytes 6148
  60.9 2.0 %collective-permute-start.7 = (bf16[32,16,512]{2,1,0:T(8,128)(2,1)S(1)}, bf16[32,16,512]{2,1,0:T(8,128)(2,1)S(1)}, u32[]{:S(2)}, u32[]{:S(2)}) collective-permute-start(bf16[32,16,512]{2,1,0:T(8,128)(2,1)S(1)} %get-tuple-element.36), channel_id=1, source_target_pairs={{0,1},{1,0},{2,3},{3,2},{4,5},{5,4},{6,7},{7,6},{8,9},{9,8},{10,11... | collective-permute-start | bytes 1572872 | tf_op jit(solution)/shard_map/ppermute | solution.py:54
  62.7 32.0 %copy-start = (bf16[16,16384]{1,0:T(8,128)(2,1)S(1)}, bf16[16,16384]{1,0:T(8,128)(2,1)}, u32[]{:S(2)}) copy-start(bf16[16,16384]{1,0:T(8,128)(2,1)} %second_ref.1) | copy-start | bytes 1572868
  63.7 19.0 %all-to-all-start.1 = ((bf16[64,16,256]{2,1,0:T(8,128)(2,1)}), bf16[64,16,256]{2,1,0:T(8,128)(2,1)S(1)}, u32[]{:S(2)}, u32[]{:S(2)}) async-start(bf16[64,16,256]{2,1,0:T(8,128)(2,1)} %bitcast.2), calls=%async_computation.1 | async-start | bytes 1048576 | tf_op jit(solution)/shard_map/all_to_all | solution.py:530
  70.2 8.3 %collective-permute-start.1 = (bf16[16,64]{1,0:T(8,128)(2,1)S(1)}, bf16[16,64]{1,0:T(8,128)(2,1)S(1)}, u32[]{:S(2)}, u32[]{:S(2)}) collective-permute-start(bf16[16,64]{1,0:T(8,128)(2,1)S(1)} %copy-done.1), channel_id=1, source_target_pairs={{0,2},{1,3},{2,0},{3,1},{4,6},{5,7},{6,4},{7,5},{8,10},{9,11},{10,... | collective-permute-start | bytes 6152 | tf_op jit(solution)/shard_map/ppermute | solution.py:535
  72.9 5.6 %collective-permute-start = (bf16[16,64]{1,0:T(8,128)(2,1)S(1)}, bf16[16,64]{1,0:T(8,128)(2,1)S(1)}, u32[]{:S(2)}, u32[]{:S(2)}) collective-permute-start(bf16[16,64]{1,0:T(8,128)(2,1)S(1)} %copy-done.1), channel_id=1, source_target_pairs={{0,1},{1,0},{2,3},{3,2},{4,5},{5,4},{6,7},{7,6},{8,9},{9,8},{10,11... | collective-permute-start | bytes 6152 | tf_op jit(solution)/shard_map/ppermute | solution.py:535
  74.1 5.6 %collective-permute-start.2 = (bf16[16,64]{1,0:T(8,128)(2,1)S(1)}, bf16[16,64]{1,0:T(8,128)(2,1)S(1)}, u32[]{:S(2)}, u32[]{:S(2)}) collective-permute-start(bf16[16,64]{1,0:T(8,128)(2,1)S(1)} %copy-done.1), channel_id=1, source_target_pairs={{0,3},{1,2},{2,1},{3,0},{4,7},{5,6},{6,5},{7,4},{8,11},{9,10},{10,... | collective-permute-start | bytes 6152 | tf_op jit(solution)/shard_map/ppermute | solution.py:535
  83.2 5.1 %collective-permute-start.8 = (bf16[16,4096]{1,0:T(8,128)(2,1)S(1)}, bf16[16,4096]{1,0:T(8,128)(2,1)S(1)}, u32[]{:S(2)}, u32[]{:S(2)}) collective-permute-start(bf16[16,4096]{1,0:T(8,128)(2,1)S(1)} %get-tuple-element.38), channel_id=1, source_target_pairs={{0,1},{1,0},{2,3},{3,2},{4,5},{5,4},{6,7},{7,6},{8,9},{9,8},{10,11... | collective-permute-start | bytes 393224 | tf_op jit(solution)/shard_map/ppermute | solution.py:539
  85.1 6.6 %collective-permute-start.9 = (bf16[16,4096]{1,0:T(8,128)(2,1)S(1)}, bf16[16,4096]{1,0:T(8,128)(2,1)S(1)}, u32[]{:S(2)}, u32[]{:S(2)}) collective-permute-start(bf16[16,4096]{1,0:T(8,128)(2,1)S(1)} %get-tuple-element.39), channel_id=1, source_target_pairs={{0,2},{1,3},{2,0},{3,1},{4,6},{5,7},{6,4},{7,5},{8,10},{9,11},{10,... | collective-permute-start | bytes 393224 | tf_op jit(solution)/shard_map/ppermute | solution.py:539
  85.8 8.8 %collective-permute-start.10 = (bf16[16,4096]{1,0:T(8,128)(2,1)S(1)}, bf16[16,4096]{1,0:T(8,128)(2,1)S(1)}, u32[]{:S(2)}, u32[]{:S(2)}) collective-permute-start(bf16[16,4096]{1,0:T(8,128)(2,1)S(1)} %get-tuple-element.40), channel_id=1, source_target_pairs={{0,3},{1,2},{2,1},{3,0},{4,7},{5,6},{6,5},{7,4},{8,11},{9,10},{10,... | collective-permute-start | bytes 393224 | tf_op jit(solution)/shard_map/ppermute | solution.py:539

commit v7 on v4

--- a/solution.py
+++ b/solution.py
@@ -352,37 +352,37 @@
     return (taps[0] * tiles[0] + taps[1] * tiles[1] + taps[2] * tiles[2]).astype(BF)
 
 
-def gates_kernel(index, core_ref, seat_ref, own_taps, near_taps, own, other, *refs):
+def gates_kernel(core_ref, seat_ref, own_taps, near_taps, own, other, *refs):
     core = core_ref[0]
-    taps = taps_of(index, core, seat_ref, own_taps, near_taps)
-    if index == 0:
-        wave_hbm, twist_hbm, *outs, wave, twist, sems = refs
+    taps = [taps_of(index, core, seat_ref, own_taps, near_taps) for index in range(2)]
+    first_own, first_other, second_own = refs[2:5] if len(refs) > 3 else refs
+    loads = []
+    if len(refs) > 3:
+        wave_hbm, twist_hbm, *_, wave, twist, sems = refs
         loads = [fetch(twist_hbm.at[core], twist, sems, 0), fetch(wave_hbm, wave, sems, 1)]
-    else:
-        outs, loads = refs, []
 
     @pl.loop(0, BLOCKS, unroll=8)
     def _(block):
         last = (block + BLOCKS - 1) % BLOCKS
         ahead = other[jnp.where(core == 0, last, block), :, N2 - LANES:].astype(F32)
-        outs[0][block] = gate(taps, lagged(own[block].astype(F32), ahead))
-        if len(outs) > 1:
-            ahead = own[jnp.where(core == 0, block, last), :, N2 - LANES:].astype(F32)
-            outs[1][block] = gate(taps, lagged(other[block].astype(F32), ahead))
+        tiles = lagged(own[block].astype(F32), ahead)
+        first_own[block] = gate(taps[0], tiles)
+        second_own[block] = gate(taps[1], tiles)
+        ahead = own[jnp.where(core == 0, block, last), :, N2 - LANES:].astype(F32)
+        first_other[block] = gate(taps[0], lagged(other[block].astype(F32), ahead))
 
     for load in loads:
         load.wait()
 
 
-def gates(index, core, seat, taps, near_taps, own, other, *tables):
-    count = 2 if index == 0 else 1
+def gates(core, seat, taps, near_taps, own, other, *tables):
     field = jax.ShapeDtypeStruct((BLOCKS, TILE, N2), BF)
     brought = [jax.ShapeDtypeStruct((N2, 2 * N2), BF), jax.ShapeDtypeStruct((2, ROWS, N2), BF)] if tables else []
     return pl.pallas_call(
-        functools.partial(gates_kernel, index),
+        gates_kernel,
         in_specs=[SMEM] * 4 + [VMEM, VMEM] + [ANY] * len(tables),
-        out_specs=(VMEM,) * (count + len(tables)),
-        out_shape=[field] * count + brought,
+        out_specs=(VMEM,) * (3 + len(tables)),
+        out_shape=[field] * 3 + brought,
         scratch_shapes=[pltpu.SemaphoreType.DMA((2,))] if tables else [],
         compiler_params=params(4),
         cost_estimate=cost(0, 0),
@@ -523,10 +523,9 @@
     gain, second_gain, wave_now, twist_now = fold(core, got, wave, twist)
     mine = first_conv(core, own, other, gain, forward, wave_now, twist_now)
     theirs = swap(mine)
-    *gate_all, wave, twist = gates(0, core, seat, short_taps, near_taps, own, other, wave, twist)
+    *gate_all, gate_own, wave, twist = gates(core, seat, short_taps, near_taps, own, other, wave, twist)
     keep, send = second_conv(core, gate_all, mine, theirs, second_gain, forward, wave, twist)
     theirs = swap(send)
-    gate_own, = gates(1, core, seat, short_taps, near_taps, own, other)
     spread = last_gate(gate_own, keep, theirs)
     members = [[4 * j + 2 * high + side for high in range(2) for j in range(BLOCKS)] for side in range(2)]
     values = lax.all_to_all(

time: 93.7 us -> 93.7 us (level)
  Pallas kernels: 18.6 us -> 17.3 us
  waiting for transfers between devices: 15.6 us -> 16.8 us
    ppermute x6, waiting for transfers between devices: 1.68 us -> 3.02 us  [swap(): lax.ppermute(value, 'ch', [(i, i ^ 1) for i in range(lax.axis_size('ch'))])]
    pallas_call x2 -> x1, Pallas kernels: 3.42 us -> 2.09 us  [gates(): pl.pallas_call(gates_kernel, in_specs=[SMEM] * 4 + [VMEM, VMEM] + [ANY] *...]
  transfers between devices with their start and end apart: 10 -> 10, of which waited for: 8 -> 8; matrix products, arithmetic and copies ran while one was open for 0% -> 0% of each run, Pallas kernels for 8% -> 7%
where the time goes in v7:
time: 93.7 us; the launch traced here: 93.3 us
  blocking collectives  41.6 us (44%)
  starting transfers between devices  17.4 us (19%)
  Pallas kernels  17.3 us (18%)
  waiting for transfers between devices  16.8 us (18%)
    all_to_all x1, blocking collectives, on_device(): got = lax.all_to_all(buffer, 'seq', split_axis=0, concat_axis=0, tiled=True)  41.6 us
    ppermute x3, waiting for transfers between devices, on_device(): lax.ppermute(mixing, 'ch', [(i, i ^ apart) for i in range(4)])  11.1 us
    ppermute x6, starting transfers between devices, swap(): lax.ppermute(value, 'ch', [(i, i ^ 1) for i in range(lax.axis_size('ch'))])  6.88 us
    all_to_all x1, starting transfers between devices, on_device(): lax.all_to_all(spread.reshape(2 * BLOCKS, TILE, N2), ('seq', 'ch'), split...  6.58 us
    ppermute x3, starting transfers between devices, on_device(): lax.ppermute(mixing, 'ch', [(i, i ^ apart) for i in range(4)])  3.96 us
    pallas_call x1, Pallas kernels, second_conv(): pl.pallas_call(second_conv_kernel, in_specs=[SMEM] + [VMEM] * 7 + [ANY],...  3.85 us
    pallas_call x2, Pallas kernels, split(): pl.pallas_call(functools.partial(split_kernel, keep), in_specs=[SMEM, ANY...  3.6 us
    ppermute x6, waiting for transfers between devices, swap(): lax.ppermute(value, 'ch', [(i, i ^ 1) for i in range(lax.axis_size('ch'))])  3.02 us
  transfers between devices with their start and end apart: 10, of which 8 were waited for; matrix products, arithmetic and copies ran while one was open for 0% of the time, Pallas kernels for 7%

profile of v7, /device:TPU:1, one launch (start us, length us, event | category | flops | bytes accessed | tf_op | source)
XLA Modules:
  0.0 93.3 jit_solution(14453200583146263158)
XLA Ops:
  0.0 0.0 copy-start.2
  0.0 1.8 %shard_map.82 = bf16[16,5,16,512]{3,2,1,0:T(8,128)(2,1)S(1)} custom-call(s32[1]{0:T(128)S(6)} %select_n.7.core_ref, bf16[16,16384]{1,0:T(8,128)(2,1)} %signal_ref.3, bf16[2,2,16,16384]{3,2,1,0:T(8,128)(2,1)} %filter_ref.3), custom_call_target="tpu_custom_call" | custom-call | bytes 8388608 | tf_op jit(solution)/shard_map/pallas_call | solution.py:129
  1.8 1.5 %collective-permute-start.3 = (bf16[16,5,16,512]{3,2,1,0:T(8,128)(2,1)S(1)}, bf16[16,5,16,512]{3,2,1,0:T(8,128)(2,1)S(1)}, u32[]{:S(2)}, u32[]{:S(2)}) collective-permute-start(bf16[16,5,16,512]{3,2,1,0:T(8,128)(2,1)S(1)} %shard_map.82), channel_id=1, source_target_pairs={{0,1},{1,0},{2,3},{3,2},{4,5},{5,4},{6,7},{7,6},{8,9},{9,8},{10,11... | collective-permute-start | bytes 3932168 | tf_op jit(solution)/shard_map/ppermute | solution.py:54
  3.3 0.0 copy-done.2
  3.3 0.1 collective-permute-start.4
  3.4 1.8 %shard_map.83 = (bf16[32,5,16,512]{3,2,1,0:T(8,128)(2,1)S(1)}, bf16[512,512]{1,0:T(8,128)(2,1)S(1)}) custom-call(s32[1]{0:T(128)S(6)} %select_n.7.core_ref, bf16[16,16384]{1,0:T(8,128)(2,1)} %signal_ref.3, bf16[2,2,16,16384]{3,2,1,0:T(8,128)(2,1)} %filter_ref.3, bf16[2,512,512]{2,1,0:T(8,128)(2,1)} %constant.34.clone.refs_0_), custom_call_target="tpu_custom_call" | custom-call | bytes 8388608 | tf_op jit(solution)/shard_map/pallas_call | solution.py:129
  5.2 0.7 collective-permute-done.3.piece_ref
  6.0 0.1 shard_map.84
  6.1 0.0 collective-permute-done.4.near_taps
  6.1 41.6 %all_to_all.10.got_ref = bf16[32,5,16,512]{3,2,1,0:T(8,128)(2,1)S(1)} all-to-all(bf16[32,5,16,512]{3,2,1,0:T(8,128)(2,1)S(1)} %shard_map.84), channel_id=1, replica_groups=mesh['seq'=32,'ch'=4] {'seq'}, dimensions={0} | all-to-all | bytes 5242880 | tf_op jit(solution)/shard_map/all_to_all | solution.py:519
  47.7 2.3 %collective-permute-start.5 = (bf16[32,16,512]{2,1,0:T(8,128)(2,1)S(1)}, bf16[32,16,512]{2,1,0:T(8,128)(2,1)S(1)}, u32[]{:S(2)}, u32[]{:S(2)}) collective-permute-start(bf16[32,16,512]{2,1,0:T(8,128)(2,1)S(1)} %shard_map.85.own), channel_id=1, source_target_pairs={{0,1},{1,0},{2,3},{3,2},{4,5},{5,4},{6,7},{7,6},{8,9},{9,8},{10,11... | collective-permute-start | bytes 1572872 | tf_op jit(solution)/shard_map/ppermute | solution.py:54
  50.0 1.4 %shard_map.87 = (bf16[2,272,512]{2,1,0:T(8,128)(2,1)S(1)}, bf16[2,272,512]{2,1,0:T(8,128)(2,1)S(1)}, bf16[512,1024]{1,0:T(8,128)(2,1)S(1)}, bf16[2,272,512]{2,1,0:T(8,128)(2,1)S(1)}) custom-call(s32[1]{0:T(128)S(6)} %select_n.7.core_ref, bf16[32,5,16,512]{3,2,1,0:T(8,128)(2,1)S(1)} %all_to_all.10.got_ref, bf16[512,1024]{1,0:T(8,128)(2,1)} %constant.35.clone.refs_0_.wave_hbm, ...), custom_call_target="tpu_custom_call" | custom-call | tf_op jit(solution)/shard_map/pallas_call | solution.py:209
  51.4 0.1 collective-permute-done.5.other
  51.5 2.6 %shard_map.88.mine = bf16[2,32,16,512]{3,2,1,0:T(8,128)(2,1)S(1)} custom-call(s32[1]{0:T(128)S(6)} %select_n.7.core_ref, bf16[32,16,512]{2,1,0:T(8,128)(2,1)S(1)} %shard_map.85.own, bf16[32,16,512]{2,1,0:T(8,128)(2,1)S(1)} %collective-permute-done.5.other, bf16[2,272,512]{2,1,0:T(8,128)(2,1)S(1)} %get-tuple-element.28.gain, ...), custom_call_target="tpu_custom_call" | custom-call | tf_op jit(solution)/shard_map/pallas_call | solution.py:322
  54.1 0.5 collective-permute-start.6
  54.6 2.1 %shard_map.86 = (bf16[32,16,512]{2,1,0:T(8,128)(2,1)S(1)}, bf16[32,16,512]{2,1,0:T(8,128)(2,1)S(1)}, bf16[32,16,512]{2,1,0:T(8,128)(2,1)S(1)}, bf16[512,1024]{1,0:T(8,128)(2,1)S(1)}, bf16[2,272,512]{2,1,0:T(8,128)(2,1)S(1)}) custom-call(s32[1]{0:T(128)S(6)} %select_n.7.core_ref, s32[1]{0:T(128)} %bitcast.1.seat_ref, f32[2,3,16]{2,1,0:T(4,128)S(1)} %copy.12.own_taps, ...), custom_call_target="tpu_custom_call" | custom-call | tf_op jit(solution)/shard_map/pallas_call | solution.py:381
  56.7 0.3 collective-permute-done.6.theirs_any
  57.0 3.9 %shard_map.89 = (bf16[32,16,512]{2,1,0:T(8,128)(2,1)S(1)}, bf16[32,16,512]{2,1,0:T(8,128)(2,1)S(1)}) custom-call(s32[1]{0:T(128)S(6)} %select_n.7.core_ref, bf16[32,16,512]{2,1,0:T(8,128)(2,1)S(1)} %get-tuple-element.26.gate_own, bf16[32,16,512]{2,1,0:T(8,128)(2,1)S(1)} %get-tuple-element.27.gate_other, bf16[2,32,16,512]{3,2,1,0:T(8,128)(2,1)S(1)} %shard_map.88.mine, ...), custom_call_target="tpu_custom_call" | custom-call | tf_op jit(solution)/shard_map/pallas_call | solution.py:404
  60.9 0.5 collective-permute-start.7
  61.3 1.5 %collective-permute-done.7.theirs_ref = bf16[32,16,512]{2,1,0:T(8,128)(2,1)S(1)} collective-permute-done((bf16[32,16,512]{2,1,0:T(8,128)(2,1)S(1)}, bf16[32,16,512]{2,1,0:T(8,128)(2,1)S(1)}, u32[]{:S(2)}, u32[]{:S(2)}) %collective-permute-start.7) | collective-permute-done | bytes 524320 | tf_op jit(solution)/shard_map/ppermute | solution.py:54
  62.9 0.0 copy-start.1
  62.9 1.0 %shard_map.90 = bf16[2,32,16,512]{3,2,1,0:T(8,128)(2,1)} custom-call(bf16[32,16,512]{2,1,0:T(8,128)(2,1)S(1)} %get-tuple-element.25.gate_ref, bf16[32,16,512]{2,1,0:T(8,128)(2,1)S(1)} %get-tuple-element.35.keep_ref, bf16[32,16,512]{2,1,0:T(8,128)(2,1)S(1)} %collective-permute-done.7.theirs_ref), custom_call_target="tpu_custom_call" | custom-call | tf_op jit(solution)/shard_map/pallas_call | solution.py:427
  63.9 0.0 copy-start
  63.9 6.6 %all-to-all-start.1 = ((bf16[64,16,512]{2,1,0:T(8,128)(2,1)}), bf16[64,16,512]{2,1,0:T(8,128)(2,1)S(1)}, u32[]{:S(2)}, u32[]{:S(2)}) async-start(bf16[64,16,512]{2,1,0:T(8,128)(2,1)} %bitcast.2), calls=%async_computation.1 | async-start | bytes 2097152 | tf_op jit(solution)/shard_map/all_to_all | solution.py:531
  70.5 0.0 copy-done.1
  70.5 0.7 collective-permute-start
  71.2 2.9 %collective-permute-start.1 = (bf16[16,64]{1,0:T(8,128)(2,1)S(1)}, bf16[16,64]{1,0:T(8,128)(2,1)S(1)}, u32[]{:S(2)}, u32[]{:S(2)}) collective-permute-start(bf16[16,64]{1,0:T(8,128)(2,1)S(1)} %copy-done.1), channel_id=1, source_target_pairs={{0,2},{1,3},{2,0},{3,1},{4,6},{5,7},{6,4},{7,5},{8,10},{9,11},{10,... | collective-permute-start | bytes 6152 | tf_op jit(solution)/shard_map/ppermute | solution.py:536
  74.2 0.3 collective-permute-start.2
  74.5 0.0 collective-permute-done.near
  74.5 9.9 %collective-permute-done.1.far = bf16[16,64]{1,0:T(8,128)(2,1)S(1)} collective-permute-done((bf16[16,64]{1,0:T(8,128)(2,1)S(1)}, bf16[16,64]{1,0:T(8,128)(2,1)S(1)}, u32[]{:S(2)}, u32[]{:S(2)}) %collective-permute-start.1) | collective-permute-done | bytes 2080 | tf_op jit(solution)/shard_map/ppermute | solution.py:536
  84.4 1.2 %collective-permute-done.2.across = bf16[16,64]{1,0:T(8,128)(2,1)S(1)} collective-permute-done((bf16[16,64]{1,0:T(8,128)(2,1)S(1)}, bf16[16,64]{1,0:T(8,128)(2,1)S(1)}, u32[]{:S(2)}, u32[]{:S(2)}) %collective-permute-start.2) | collective-permute-done | bytes 2080 | tf_op jit(solution)/shard_map/ppermute | solution.py:536
  85.6 2.7 %all-to-all-done.1.values_ref = bf16[64,16,512]{2,1,0:T(8,128)(2,1)S(1)} async-done(((bf16[64,16,512]{2,1,0:T(8,128)(2,1)}), bf16[64,16,512]{2,1,0:T(8,128)(2,1)S(1)}, u32[]{:S(2)}, u32[]{:S(2)}) %all-to-all-start.1) | async-done | bytes 1048608 | tf_op jit(solution)/shard_map/all_to_all | solution.py:531
  88.3 0.9 shard_map.91
  89.2 2.1 %collective-permute-start.8 = (bf16[16,8192]{1,0:T(8,128)(2,1)S(1)}, bf16[16,8192]{1,0:T(8,128)(2,1)S(1)}, u32[]{:S(2)}, u32[]{:S(2)}) collective-permute-start(bf16[16,8192]{1,0:T(8,128)(2,1)S(1)} %get-tuple-element.37), channel_id=1, source_target_pairs={{0,1},{1,0},{2,3},{3,2},{4,5},{5,4},{6,7},{7,6},{8,9},{9,8},{10,11... | collective-permute-start | bytes 786440 | tf_op jit(solution)/shard_map/ppermute | solution.py:54
  91.3 0.0 copy-done
  91.3 0.8 shard_map.92.refs_0_
  92.1 0.3 collective-permute-done.8.update_ref
  92.4 0.8 shard_map.93
  (2 shorter events, 0.0 us)
Async XLA Ops:
  0.0 3.3 %copy-start.2 = (f32[2,3,16]{2,0,1:T(2,128)S(1)}, f32[2,3,16]{2,0,1:T(2,128)}, u32[]{:S(2)}) copy-start(f32[2,3,16]{2,0,1:T(2,128)} %param.11) | copy-start | bytes 1156
  1.8 4.2 %collective-permute-start.3 = (bf16[16,5,16,512]{3,2,1,0:T(8,128)(2,1)S(1)}, bf16[16,5,16,512]{3,2,1,0:T(8,128)(2,1)S(1)}, u32[]{:S(2)}, u32[]{:S(2)}) collective-permute-start(bf16[16,5,16,512]{3,2,1,0:T(8,128)(2,1)S(1)} %shard_map.82), channel_id=1, source_target_pairs={{0,1},{1,0},{2,3},{3,2},{4,5},{5,4},{6,7},{7,6},{8,9},{9,8},{10,11... | collective-permute-start | bytes 3932168 | tf_op jit(solution)/shard_map/ppermute | solution.py:54
  3.3 2.8 %collective-permute-start.4 = (f32[2,3,16]{2,1,0:T(4,128)S(1)}, f32[2,3,16]{2,1,0:T(4,128)S(1)}, u32[]{:S(2)}, u32[]{:S(2)}) collective-permute-start(f32[2,3,16]{2,1,0:T(4,128)S(1)} %copy.12.own_taps), channel_id=1, source_target_pairs={{0,1},{1,0},{2,3},{3,2},{4,5},{5,4},{6,7},{7,6},{8,9},{9,8},{10,11... | collective-permute-start | bytes 1160 | tf_op jit(solution)/shard_map/ppermute | solution.py:54
  47.7 3.8 %collective-permute-start.5 = (bf16[32,16,512]{2,1,0:T(8,128)(2,1)S(1)}, bf16[32,16,512]{2,1,0:T(8,128)(2,1)S(1)}, u32[]{:S(2)}, u32[]{:S(2)}) collective-permute-start(bf16[32,16,512]{2,1,0:T(8,128)(2,1)S(1)} %shard_map.85.own), channel_id=1, source_target_pairs={{0,1},{1,0},{2,3},{3,2},{4,5},{5,4},{6,7},{7,6},{8,9},{9,8},{10,11... | collective-permute-start | bytes 1572872 | tf_op jit(solution)/shard_map/ppermute | solution.py:54
  54.1 2.9 %collective-permute-start.6 = (bf16[2,32,16,512]{3,2,1,0:T(8,128)(2,1)S(1)}, bf16[2,32,16,512]{3,2,1,0:T(8,128)(2,1)}, u32[]{:S(2)}, u32[]{:S(2)}) collective-permute-start(bf16[2,32,16,512]{3,2,1,0:T(8,128)(2,1)S(1)} %shard_map.88.mine), channel_id=1, source_target_pairs={{0,1},{1,0},{2,3},{3,2},{4,5},{5,4},{6,7},{7,6},{8,9},{9,8},{10,11... | collective-permute-start | bytes 3145736 | tf_op jit(solution)/shard_map/ppermute | solution.py:54
  60.9 2.0 %collective-permute-start.7 = (bf16[32,16,512]{2,1,0:T(8,128)(2,1)S(1)}, bf16[32,16,512]{2,1,0:T(8,128)(2,1)S(1)}, u32[]{:S(2)}, u32[]{:S(2)}) collective-permute-start(bf16[32,16,512]{2,1,0:T(8,128)(2,1)S(1)} %get-tuple-element.36), channel_id=1, source_target_pairs={{0,1},{1,0},{2,3},{3,2},{4,5},{5,4},{6,7},{7,6},{8,9},{9,8},{10,11... | collective-permute-start | bytes 1572872 | tf_op jit(solution)/shard_map/ppermute | solution.py:54
  62.9 7.7 %copy-start.1 = (bf16[16,64]{1,0:T(8,128)(2,1)S(1)}, bf16[16,64]{1,0:T(8,128)(2,1)}, u32[]{:S(2)}) copy-start(bf16[16,64]{1,0:T(8,128)(2,1)} %own.1) | copy-start | bytes 6148
  63.9 27.4 %copy-start = (bf16[16,16384]{1,0:T(8,128)(2,1)S(1)}, bf16[16,16384]{1,0:T(8,128)(2,1)}, u32[]{:S(2)}) copy-start(bf16[16,16384]{1,0:T(8,128)(2,1)} %second_ref.3) | copy-start | bytes 1572868
  63.9 24.4 %all-to-all-start.1 = ((bf16[64,16,512]{2,1,0:T(8,128)(2,1)}), bf16[64,16,512]{2,1,0:T(8,128)(2,1)S(1)}, u32[]{:S(2)}, u32[]{:S(2)}) async-start(bf16[64,16,512]{2,1,0:T(8,128)(2,1)} %bitcast.2), calls=%async_computation.1 | async-start | bytes 2097152 | tf_op jit(solution)/shard_map/all_to_all | solution.py:531
  70.5 4.0 %collective-permute-start = (bf16[16,64]{1,0:T(8,128)(2,1)S(1)}, bf16[16,64]{1,0:T(8,128)(2,1)S(1)}, u32[]{:S(2)}, u32[]{:S(2)}) collective-permute-start(bf16[16,64]{1,0:T(8,128)(2,1)S(1)} %copy-done.1), channel_id=1, source_target_pairs={{0,1},{1,0},{2,3},{3,2},{4,5},{5,4},{6,7},{7,6},{8,9},{9,8},{10,11... | collective-permute-start | bytes 6152 | tf_op jit(solution)/shard_map/ppermute | solution.py:536
  71.2 13.2 %collective-permute-start.1 = (bf16[16,64]{1,0:T(8,128)(2,1)S(1)}, bf16[16,64]{1,0:T(8,128)(2,1)S(1)}, u32[]{:S(2)}, u32[]{:S(2)}) collective-permute-start(bf16[16,64]{1,0:T(8,128)(2,1)S(1)} %copy-done.1), channel_id=1, source_target_pairs={{0,2},{1,3},{2,0},{3,1},{4,6},{5,7},{6,4},{7,5},{8,10},{9,11},{10,... | collective-permute-start | bytes 6152 | tf_op jit(solution)/shard_map/ppermute | solution.py:536
  74.2 11.5 %collective-permute-start.2 = (bf16[16,64]{1,0:T(8,128)(2,1)S(1)}, bf16[16,64]{1,0:T(8,128)(2,1)S(1)}, u32[]{:S(2)}, u32[]{:S(2)}) collective-permute-start(bf16[16,64]{1,0:T(8,128)(2,1)S(1)} %copy-done.1), channel_id=1, source_target_pairs={{0,3},{1,2},{2,1},{3,0},{4,7},{5,6},{6,5},{7,4},{8,11},{9,10},{10,... | collective-permute-start | bytes 6152 | tf_op jit(solution)/shard_map/ppermute | solution.py:536
  89.2 3.3 %collective-permute-start.8 = (bf16[16,8192]{1,0:T(8,128)(2,1)S(1)}, bf16[16,8192]{1,0:T(8,128)(2,1)S(1)}, u32[]{:S(2)}, u32[]{:S(2)}) collective-permute-start(bf16[16,8192]{1,0:T(8,128)(2,1)S(1)} %get-tuple-element.37), channel_id=1, source_target_pairs={{0,1},{1,0},{2,3},{3,2},{4,5},{5,4},{6,7},{7,6},{8,9},{9,8},{10,11... | collective-permute-start | bytes 786440 | tf_op jit(solution)/shard_map/ppermute | solution.py:54
